TPU v7x, 256 devices: a whole 4x4x8 slice. The times are simulated.
256 devices in a mesh: gx: 8 (over x, core), gy: 32 (over z, y).
Axes of the slice: x: 4, y: 4, z: 8, core: 2. Of those that a mesh axis runs over, the one named last changes fastest.
Arguments:
- fields: float32 [8, 1024, 8192], P(None, 'gx', 'gy'), may hold values from -6 to 6
- velocity: float32 [2, 1024, 8192], P(None, 'gx', 'gy'), may hold values from -1 to 1
- mode_gain: float32 [256, 256, 2, 128], P('gx', 'gy'), may hold values from -5 to 5
- lift_weight: float32 [8, 128], replicated, may hold values from -2 to 2
- project_weight: float32 [128, 8], replicated, may hold values from -0.5 to 0.5
- obs_height: float32 [256, 256, 128], P(('gx', 'gy')), may hold values from -6 to 6
- obs_weight: float32 [256, 256, 128], P(('gx', 'gy')), may hold values from 0.25 to 4
- cell_rows: int32 [256, 256, 128], P(('gx', 'gy')), may hold values from 0 to 127
- cell_cols: int32 [256, 256, 128], P(('gx', 'gy')), may hold values from 0 to 255
- counts: int32 [256, 256], P(('gx', 'gy')), may hold values from 0 to 128, as said below
Outputs:
- corrected: float32 [8, 1024, 8192], P(None, 'gx', 'gy')
- surface_gradient: float32 [1024, 8192], P('gx', 'gy')
Inputs may be any that keep to these rules, and one draw needn't show every extreme that they name: The first counts[o, s] points of a block are live, the rest are padding; some owning tile has every block full.
All inputs are finite; a program needn't handle non-finite values.
Results may differ from a plain program's by a relative error of at most 0.000076.
Values sent between devices are 32-bit elements; how exact they have to be, the bound alone decides.
No kernel may reach another device: no remote copies, remote signals or barrier semaphores. Data moves between devices by JAX's collectives and lax.ppermute only.
A program may use at most 128 MiB of HBM per device.

v0:
```python
import math

import jax
import jax.numpy as jnp
from jax import lax
from jax.sharding import PartitionSpec as P

MX = 256
MY = 256


time_step = 0.2
diffusion = 0.25
highest = lax.Precision.HIGHEST


def padded_2(array, sides, width):
    for axis, dim in sides:
        count, length = (lax.axis_size(axis), array.shape[dim])
        up = [(i, (i + 1) % count) for i in range(count - 1)]
        down = [(j, i) for i, j in up]
        last = lax.slice_in_dim(array, length - width, length, axis=dim)
        leading = lax.slice_in_dim(array, 0, width, axis=dim)
        before = lax.ppermute(last, axis, up)
        after = lax.ppermute(leading, axis, down)
        array = jnp.concatenate([before, array, after], axis=dim)
    return array


def twiddle(position, frequency, length):
    phase = position[:, None] * frequency[None, :] % length
    angle = phase.astype(jnp.float32) * (2.0 * math.pi / length)
    return (jnp.cos(angle), jnp.sin(angle))


def wave_numbers(amount):
    mode_index = jnp.arange(amount, dtype=jnp.int32)
    return jnp.where(mode_index < MX // 2, mode_index, mode_index - MX)


def blocked_table(position, length, blocks):
    cosine, sine = twiddle(position, jnp.arange(MY, dtype=jnp.int32), length)
    paired = jnp.stack((cosine, -sine), axis=1)
    paired = paired.reshape(position.shape[0], 2, blocks, MY // blocks)
    return paired.transpose(0, 2, 1, 3).reshape(position.shape[0], 2 * MY)


def body(
    fields,
    velocity,
    mode_gain,
    lift_weight,
    project_weight,
    obs_height,
    obs_weight,
    cell_rows,
    cell_cols,
    counts,
):
    nfield, tile_rows, tile_cols = fields.shape
    row_groups = lax.axis_size("gx")
    col_groups = lax.axis_size("gy")
    total_rows = tile_rows * row_groups
    total_cols = tile_cols * col_groups
    row_start = lax.axis_index("gx") * tile_rows
    col_start = lax.axis_index("gy") * tile_cols
    mode_cols = MY // col_groups
    mode_rows = MX // row_groups
    along_first = (((1,), (1,)), ((), ()))
    along_lead = (((0,), (0,)), ((), ()))
    joined = jnp.concatenate((fields, velocity), axis=0)
    padded = padded_2(joined, (("gx", 1), ("gy", 2)), 1)
    west_side = padded[:nfield, :-1, 1:-1]
    east_side = padded[:nfield, 1:, 1:-1]
    speed_x = padded[nfield, 1:, 1:-1]
    faces_x = row_start + jnp.arange(tile_rows + 1, dtype=jnp.int32)
    open_x = ((faces_x >= 1) & (faces_x <= total_rows - 1)).astype(jnp.float32)[:, None]
    flux_x = (
        jnp.maximum(speed_x, 0.0) * west_side
        + jnp.minimum(speed_x, 0.0) * east_side
        - diffusion * (east_side - west_side)
    ) * open_x
    south_side = padded[:nfield, 1:-1, :-1]
    north_side = padded[:nfield, 1:-1, 1:]
    speed_y = padded[nfield + 1, 1:-1, 1:]
    faces_y = col_start + jnp.arange(tile_cols + 1, dtype=jnp.int32)
    open_y = ((faces_y >= 1) & (faces_y <= total_cols - 1)).astype(jnp.float32)[None, :]
    flux_y = (
        jnp.maximum(speed_y, 0.0) * south_side
        + jnp.minimum(speed_y, 0.0) * north_side
        - diffusion * (north_side - south_side)
    ) * open_y
    stepped = fields - time_step * (
        flux_x[:, 1:] - flux_x[:, :-1] + flux_y[:, :, 1:] - flux_y[:, :, :-1]
    )
    row_index = row_start + jnp.arange(tile_rows, dtype=jnp.int32)
    col_index = col_start + jnp.arange(tile_cols, dtype=jnp.int32)
    scale_in = 1.0 / math.sqrt(total_rows * total_cols)
    local_table = blocked_table(col_index, total_cols, col_groups)
    flattened = stepped.reshape(nfield * tile_rows, tile_cols)
    by_mode = lax.psum_scatter(
        lax.dot_general(local_table, flattened, (((0,), (1,)), ((), ())), precision=highest),
        "gy",
        scatter_dimension=0,
        tiled=True,
    )
    by_mode = by_mode.reshape(2 * mode_cols, nfield, tile_rows)
    real_rows = by_mode[:mode_cols].reshape(mode_cols * nfield, tile_rows)
    imag_rows = by_mode[mode_cols:].reshape(mode_cols * nfield, tile_rows)
    cosine, sine = twiddle(wave_numbers(mode_rows * lax.axis_size("gx")), row_index, total_rows)
    real_term = lax.dot_general(
        cosine, real_rows, along_first, precision=highest
    ) + lax.dot_general(sine, imag_rows, along_first, precision=highest)
    imag_term = lax.dot_general(
        cosine, imag_rows, along_first, precision=highest
    ) - lax.dot_general(sine, real_rows, along_first, precision=highest)
    coeffs = (
        lax.psum_scatter(
            jnp.stack((real_term, imag_term), axis=1), "gx", scatter_dimension=0, tiled=True
        )
        * scale_in
    )
    coeffs = coeffs.reshape(mode_rows, 2, mode_cols, nfield)
    lifted = jnp.einsum("mpnf,fc->mnpc", coeffs, lift_weight, precision=highest)
    gain_real = mode_gain[:, :, 0]
    gain_imag = mode_gain[:, :, 1]
    mixed = jnp.stack(
        (
            gain_real * lifted[:, :, 0] - gain_imag * lifted[:, :, 1],
            gain_real * lifted[:, :, 1] + gain_imag * lifted[:, :, 0],
        ),
        axis=2,
    )
    outgoing = jnp.einsum("mnpc,cf->mpnf", mixed, project_weight, precision=highest)
    ky_index = lax.axis_index("gy") * mode_cols + jnp.arange(mode_cols, dtype=jnp.int32)
    ky_weight = jnp.where(ky_index == 0, 1.0, 2.0).astype(jnp.float32) / math.sqrt(MX * MY)
    outgoing = outgoing * ky_weight[None, None, :, None]
    out_flat = outgoing.reshape(mode_rows, 2, mode_cols * nfield)
    block_in = lax.all_gather(out_flat, "gx", axis=0, tiled=True)
    cosine, sine = twiddle(wave_numbers(block_in.shape[0]), row_index, total_rows)
    real_in = block_in[:, 0]
    imag_in = block_in[:, 1]
    real_out = lax.dot_general(real_in, cosine, along_lead, precision=highest) - lax.dot_general(
        imag_in, sine, along_lead, precision=highest
    )
    imag_out = lax.dot_general(real_in, sine, along_lead, precision=highest) + lax.dot_general(
        imag_in, cosine, along_lead, precision=highest
    )
    spatial = jnp.stack((real_out, imag_out))
    spatial = spatial.reshape(2, mode_cols, nfield, tile_rows).transpose(1, 0, 2, 3)
    block_in = lax.all_gather(spatial, "gy", axis=0, tiled=True)
    amount = block_in.shape[0]
    cosine, sine = twiddle(jnp.arange(amount, dtype=jnp.int32), col_index, total_cols)
    inverse_piece = jnp.stack((cosine, -sine), axis=1).reshape(2 * amount, tile_cols)
    correction = lax.dot_general(
        block_in.reshape(2 * amount, -1), inverse_piece, along_lead, precision=highest
    )
    correction = correction.reshape(nfield, tile_rows, tile_cols)
    corrected = stepped + correction
    paired = jnp.stack((obs_height[0], obs_weight[0])).reshape(2, row_groups, col_groups, -1)
    arrived = lax.all_to_all(
        lax.all_to_all(paired, "gx", split_axis=1, concat_axis=1, tiled=True),
        "gy",
        split_axis=2,
        concat_axis=2,
        tiled=True,
    )
    arrived = arrived.reshape(2, row_groups * col_groups, -1)
    points = arrived.shape[2]
    flat_index = cell_rows[0] * tile_cols + cell_cols[0]
    surface = corrected[0].reshape(-1)
    is_live = (jnp.arange(points, dtype=jnp.int32)[None, :] < counts[0][:, None]).astype(
        jnp.float32
    )
    misfit = arrived[1] * (surface[flat_index] - arrived[0]) * is_live
    gradient = (
        jnp.zeros((tile_rows * tile_cols,), jnp.float32)
        .at[flat_index.reshape(-1)]
        .add(misfit.reshape(-1))
    )
    return (corrected, gradient.reshape(tile_rows, tile_cols))


def solution(mesh):
    return jax.shard_map(
        body,
        mesh=mesh,
        in_specs=(
            P(None, "gx", "gy"),
            P(None, "gx", "gy"),
            P("gx", "gy", None, None),
            P(),
            P(),
            P(("gx", "gy"), None, None),
            P(("gx", "gy"), None, None),
            P(("gx", "gy"), None, None),
            P(("gx", "gy"), None, None),
            P(("gx", "gy"), None),
        ),
        out_specs=(P(None, "gx", "gy"), P("gx", "gy")),
        check_vma=False,
    )
```

profile of v0, /device:TPU:1, one launch (start us, length us, event | category | flops | bytes accessed | tf_op | source)
XLA Modules:
  0.0 785.0 jit_solution(8494573461176585706)
XLA Ops:
  7.2 1.4 constant_dynamic-update-slice_fusion.1
  8.7 5.1 collective-permute-start
  13.8 1.9 collective-permute-start.1
  15.8 1.1 fusion.25
  18.6 1.3 collective-permute-start.2
  20.3 4.0 collective-permute-start.3
  25.7 1.2 copy.74
  26.9 1.8 subtract_multiply_fusion
  29.8 3.2 fusion.89
  33.0 0.9 copy-done.6
  34.7 4.4 all-to-all-start
  40.7 209.4 %reduce-scatter.2.cloned.1.call-done = f32[16,1024]{1,0:T(8,128)} async-done(((f32[512,1024]{1,0:T(8,128)}), f32[16,1024]{1,0:T(8,128)}) %reduce-scatter.2.cloned.1.call-update) | async-done | bytes 65552 | tf_op jit(solution)/shard_map/reduce_scatter | solution.py:101
  256.0 6.3 all-to-all-start.1
  262.3 59.0 %all-reduce.3.cloned.1.call-done = f32[256,2,64]{2,1,0:T(2,128)} async-done(((f32[256,2,64]{2,1,0:T(2,128)}), f32[256,2,64]{2,1,0:T(2,128)}) %all-reduce.3.cloned.1.call-update) | async-done | bytes 131088
  323.4 15.6 %all_gather.6 = f32[256,2,64]{2,1,0:T(2,128)S(1)} all-gather(f32[32,2,64]{2,1,0:T(2,128)S(1)} %copy.81), channel_id=1, replica_groups=mesh['gx'=8,'gy'=32] {'gx'}, dimensions={0}, use_global_device_ids=true | all-gather | bytes 147456 | tf_op jit(solution)/shard_map/all_gather | solution.py:139
  343.8 1.0 fusion.24
  345.3 1.2 reshape.379
  346.6 69.9 %all-gather.2.cloned.1.call-done = f32[256,2,8,128]{3,2,1,0:T(8,128)} async-done(((f32[8,2,8,128]{3,2,1,0:T(8,128)}), f32[256,2,8,128]{3,2,1,0:T(8,128)}) %all-gather.2.cloned.1.call-update) | async-done | bytes 2097168 | tf_op jit(solution)/shard_map/all_gather | solution.py:151
  416.5 3.4 copy.99
  419.9 1.9 copy.84
  421.8 2.9 convolution_add_fusion
  424.7 1.0 copy-done.3
  425.8 180.5 %gather_fusion = f32[32768]{0:T(1024)S(1)} fusion(f32[32768]{0:T(1024)S(1)} %bitcast.89, s32[32768]{0:T(1024)S(1)} %get-tuple-element.2), kind=kCustom, calls=%fused_computation | custom fusion | bytes 393216 | tf_op jit(solution)/shard_map/gather | solution.py:175
  606.4 171.3 %scatter_custom_fusion = f32[32768]{0:T(1024)S(1)} fusion(s32[32768]{0:T(1024)} %bitcast.102, f32[32768]{0:T(1024)S(1)} %multiply_select_fusion.2, f32[]{:T(128)} %constant.32.clone.1), kind=kCustom, calls=%fused_computation.85 | custom fusion | flops 32768 | bytes 131584 | tf_op jit(solution)/shard_map/scatter-add | solution.py:179
  (97 shorter events, 20.4 us)
Async XLA Ops:
  7.2 315.2 %copy-start = (f32[8,128]{1,0:T(8,128)S(1)}, f32[8,128]{1,0:T(8,128)}, u32[]{:S(2)}) copy-start(f32[8,128]{1,0:T(8,128)} %param.13) | copy-start | bytes 12292
  7.2 1.4 copy-start.4
  7.2 242.9 %reduce-scatter.2.cloned.1.call-start = ((), (), s32[]{:S(2)}) async-start(), calls=%async_computation.3 | async-start | bytes 2162688 | tf_op jit(solution)/shard_map/reduce_scatter | solution.py:101
  8.7 9.1 %collective-permute-start = (f32[10,1,256]{2,1,0:T(1,128)S(1)}, f32[10,1,256]{2,1,0:T(1,128)S(1)}, u32[]{:S(2)}, u32[]{:S(2)}) collective-permute-start(f32[10,1,256]{2,1,0:T(1,128)S(1)} %get-tuple-element.11), channel_id=1, source_target_pairs={{32,0},{64,32},{96,64},{128,96},{160,128},{192,160},{224,192},{33,... | collective-permute-start | bytes 30728 | tf_op jit(solution)/shard_map/ppermute | solution.py:25
  13.8 3.9 collective-permute-start.1
  18.6 6.1 collective-permute-start.2
  20.3 5.4 collective-permute-start.3
  26.9 1.9 copy-start.1
  28.7 1.0 copy-start.2
  33.0 0.9 copy-start.6
  33.0 1.0 copy-start.7
  33.0 6.1 copy-start.12
  33.0 7.4 copy-start.5
  34.0 6.6 copy-start.8
  34.0 6.6 copy-start.9
  34.7 220.4 %all-to-all-start = ((f32[2,8,32,128]{3,2,0,1:T(8,128)}), f32[2,8,32,128]{3,2,0,1:T(8,128)S(1)}, u32[]{:S(2)}, u32[]{:S(2)}) async-start(f32[2,8,32,128]{3,2,0,1:T(8,128)} %copy.86), calls=%async_computation.1 | async-start | bytes 524288 | tf_op jit(solution)/shard_map/all_to_all | solution.py:162
  39.1 282.2 %all-reduce.3.cloned.1.call-start = ((), (), s32[]{:S(2)}) async-start(), calls=%async_computation.5 | async-start | bytes 524288
  255.1 67.7 %copy-start.10 = (f32[128,8]{0,1:T(8,128)S(1)}, f32[128,8]{0,1:T(8,128)}, u32[]{:S(2)}) copy-start(f32[128,8]{0,1:T(8,128)} %param.14) | copy-start | bytes 12292
  256.0 90.5 %all-to-all-start.1 = ((f32[2,8,32,128]{3,1,0,2:T(8,128)}), f32[2,8,32,128]{3,1,0,2:T(8,128)S(1)}, u32[]{:S(2)}, u32[]{:S(2)}) async-start(f32[2,8,32,128]{3,1,0,2:T(8,128)} %copy.87), calls=%async_computation.2 | async-start | bytes 524288 | tf_op jit(solution)/shard_map/all_to_all | solution.py:161
  262.3 154.3 %all-gather.2.cloned.1.call-start = ((), (), s32[]{:S(2)}) async-start(), calls=%async_computation.4 | async-start | bytes 2162688 | tf_op jit(solution)/shard_map/all_gather | solution.py:151
  424.7 1.0 copy-start.3
  425.8 180.6 %copy-start.11 = (s32[1,256]{1,0:T(1,128)S(1)}, s32[1,256]{1,0:T(1,128)}, u32[]{:S(2)}) copy-start(s32[1,256]{1,0:T(1,128)} %param.19) | copy-start | bytes 3076
Sparse Core Ops, SparseCore 0:
  33.2 216.8 reduce-scatter.1
  255.2 66.1 all-reduce.2
  343.2 73.3 all-gather.1
where the time goes:
time: 789 us; the launch traced here: 785 us
  waiting for transfers between devices  338 us (43%)
  local copies, waits for them, and re-layouts  200 us (25%)
  other arithmetic  180 us (23%)
  starting transfers between devices  23.1 us (3%)
  blocking collectives  15.6 us (2%)
  between operations  14.9 us (2%)
  matrix products  13.3 us (2%)
    reduce_scatter x1, waiting for transfers between devices, body(): lax.psum_scatter(lax.dot_general(local_table, flattened, (((0,), (1,)), (...  209 us
    gather x1, local copies, waits for them, and re-layouts, body(): misfit = arrived[1] * (surface[flat_index] - arrived[0]) * is_live  181 us
    scatter-add x1, other arithmetic, body(): gradient = jnp.zeros((tile_rows * tile_cols,), jnp.float32).at[flat_index...  171 us
    all_gather x1, waiting for transfers between devices, body(): block_in = lax.all_gather(spatial, 'gy', axis=0, tiled=True)  69.9 us
    unnamed x4, waiting for transfers between devices  59.1 us
  transfers between devices with their start and end apart: 9, of which 3 were waited for; matrix products, arithmetic and copies ran while one was open for 3% of the time, Pallas kernels for 0%

commit v1 on v0

v1 whole, which is shorter than its diff:
```python
import math

import jax
import jax.numpy as jnp
import numpy as np
from jax import lax
from jax.experimental import pallas as pl
from jax.experimental.pallas import tpu as pltpu
from jax.sharding import PartitionSpec as P

MX = 256
MY = 256
NX = 1024
NY = 8192
F = 8
CX = 128
CY = 256
GX = 8
GY = 32
DEV = GX * GY
HALF = MY // 2

time_step = 0.2
diffusion = 0.25
highest = lax.Precision.HIGHEST


def tables():
    x = np.arange(NX)
    rows = np.zeros((DEV + 8, NX))
    for gx in range(GX):
        for gy in range(GY):
            q = GY * (gx // 2) + gy
            ang = 2.0 * np.pi * ((q * x) % NX) / NX
            rows[gx * GY + gy] = np.cos(ang) if gx % 2 == 0 else -np.sin(ang)
    ang = 2.0 * np.pi * ((MX // 2 * x) % NX) / NX
    rows[GY] = np.cos(ang)
    rows[DEV] = -np.sin(ang)
    n = np.arange(MY)
    j = np.arange(CY)
    ang = 2.0 * np.pi * ((j[:, None] * n[None, :]) % NY) / NY
    local = np.concatenate((np.cos(ang), -np.sin(ang)), axis=1)
    g = np.arange(GY)
    ang = 2.0 * np.pi * ((g[:, None] * n[None, :]) % GY) / GY
    turn = np.concatenate((np.cos(ang), np.sin(ang)), axis=1)
    return rows.astype(np.float32), local.astype(np.float32), turn.astype(np.float32)


ROWS, LOCAL, TURN = tables()


def gain_moves():
    first, second = [], []
    for gx in range(GX):
        for gy in range(GY):
            source = gx * GY + gy
            m = 32 * gx + gy
            if gx < GX // 2:
                first.append((source, 2 * gx * GY + gy))
                second.append((source, (2 * gx + 1) * GY + gy))
            else:
                q = 0 if m == MX // 2 else MX - m
                x, y = q // GY, q % GY
                first.append((source, (2 * x + 1) * GY + y))
                second.append((source, 2 * x * GY + y))
    return first, second


def all_to_all(array, axis):
    return lax.all_to_all(array, axis, split_axis=0, concat_axis=0, tiled=True)


def advance(fields, velocity):
    gx = lax.axis_index("gx")
    gy = lax.axis_index("gy")
    up_x = [(i, i + 1) for i in range(GX - 1)]
    down_x = [(i + 1, i) for i in range(GX - 1)]
    up_y = [(i, i + 1) for i in range(GY - 1)]
    down_y = [(i + 1, i) for i in range(GY - 1)]
    west = lax.ppermute(fields[:, -1, :], "gx", up_x)
    east = lax.ppermute(
        jnp.concatenate((fields[:, 0, :], velocity[:1, 0, :]), axis=0), "gx", down_x
    )
    south = lax.ppermute(fields[:, :, -1], "gy", up_y)
    north = lax.ppermute(
        jnp.concatenate((fields[:, :, 0], velocity[1:, :, 0]), axis=0), "gy", down_y
    )
    wide = jnp.concatenate((west[:, None, :], fields, east[:F, None, :]), axis=1)
    speed = jnp.concatenate((velocity[0], east[F:]), axis=0)
    face = gx * CX + jnp.arange(CX + 1, dtype=jnp.int32)
    open_x = ((face >= 1) & (face <= NX - 1)).astype(jnp.float32)[:, None]
    low, high = wide[:, :-1], wide[:, 1:]
    flux_x = (
        jnp.maximum(speed, 0.0) * low + jnp.minimum(speed, 0.0) * high - diffusion * (high - low)
    ) * open_x
    wide = jnp.concatenate((south[:, :, None], fields, north[:F, :, None]), axis=2)
    speed = jnp.concatenate((velocity[1], north[F:].T), axis=1)
    face = gy * CY + jnp.arange(CY + 1, dtype=jnp.int32)
    open_y = ((face >= 1) & (face <= NY - 1)).astype(jnp.float32)[None, :]
    low, high = wide[:, :, :-1], wide[:, :, 1:]
    flux_y = (
        jnp.maximum(speed, 0.0) * low + jnp.minimum(speed, 0.0) * high - diffusion * (high - low)
    ) * open_y
    return fields - time_step * (
        flux_x[:, 1:] - flux_x[:, :-1] + flux_y[:, :, 1:] - flux_y[:, :, :-1]
    )


CHUNK = 16
CPTS = CHUNK * 128


def scatter_kernel(rows_ref, cols_ref, weight_ref, height_ref, sum_w_ref, sum_wh_ref, a_ref, b_ref, acc_ref):
    step = pl.program_id(0)
    weight = weight_ref[...]
    product = weight * height_ref[...]
    pieces = []
    for value in (weight, product):
        for _ in range(3):
            piece = value.astype(jnp.bfloat16)
            pieces.append(piece)
            value = value - piece.astype(jnp.float32)
    rows = rows_ref[...].astype(jnp.float32).astype(jnp.bfloat16)
    cols = cols_ref[...].astype(jnp.float32).astype(jnp.bfloat16)
    spot_r = lax.broadcasted_iota(jnp.int32, (CX, 128), 0).astype(jnp.float32).astype(jnp.bfloat16)
    spot_c = lax.broadcasted_iota(jnp.int32, (CY, 128), 0).astype(jnp.float32).astype(jnp.bfloat16)
    zero = jnp.zeros((CX, 128), jnp.bfloat16)
    one_c = jnp.ones((CY, 128), jnp.bfloat16)
    zero_c = jnp.zeros((CY, 128), jnp.bfloat16)
    for s in range(CHUNK):
        lanes = pl.ds(s * 128, 128)
        hit = spot_r == jnp.broadcast_to(rows[s : s + 1], (CX, 128))
        for k, piece in enumerate(pieces):
            a_ref[pl.ds(k * CX, CX), lanes] = jnp.where(
                hit, jnp.broadcast_to(piece[s : s + 1], (CX, 128)), zero
            )
        hit = spot_c == jnp.broadcast_to(cols[s : s + 1], (CY, 128))
        b_ref[:, lanes] = jnp.where(hit, one_c, zero_c)
    part = lax.dot_general(
        a_ref[...], b_ref[...], (((1,), (1,)), ((), ())), preferred_element_type=jnp.float32
    )

    @pl.when(step == 0)
    def _():
        acc_ref[...] = part

    @pl.when(step > 0)
    def _():
        acc_ref[...] += part

    @pl.when(step == pl.num_programs(0) - 1)
    def _():
        sum_w_ref[...] = acc_ref[0:CX] + acc_ref[CX : 2 * CX] + acc_ref[2 * CX : 3 * CX]
        sum_wh_ref[...] = (
            acc_ref[3 * CX : 4 * CX] + acc_ref[4 * CX : 5 * CX] + acc_ref[5 * CX : 6 * CX]
        )


def scatter(rows, cols, weight, height):
    steps = rows.shape[0] // CHUNK
    block = pl.BlockSpec((CHUNK, 128), lambda i: (i, 0))
    whole = pl.BlockSpec((CX, CY), lambda i: (0, 0))
    return pl.pallas_call(
        scatter_kernel,
        grid=(steps,),
        in_specs=[block] * 4,
        out_specs=[whole, whole],
        out_shape=[jax.ShapeDtypeStruct((CX, CY), jnp.float32)] * 2,
        scratch_shapes=[
            pltpu.VMEM((6 * CX, CPTS), jnp.bfloat16),
            pltpu.VMEM((CY, CPTS), jnp.bfloat16),
            pltpu.VMEM((6 * CX, CY), jnp.float32),
        ],
        compiler_params=pltpu.CompilerParams(vmem_limit_bytes=24 * 1024 * 1024),
        cost_estimate=pl.CostEstimate(
            flops=2 * 6 * CX * CY * 128 * rows.shape[0],
            bytes_accessed=4 * 128 * 4 * rows.shape[0],
            transcendentals=0,
        ),
    )(rows, cols, weight, height)


def body(
    fields,
    velocity,
    mode_gain,
    lift_weight,
    project_weight,
    obs_height,
    obs_weight,
    cell_rows,
    cell_cols,
    counts,
):
    gx = lax.axis_index("gx")
    gy = lax.axis_index("gy")
    core = gx % 2
    special = ((gx < 2) & (gy == 0)).astype(jnp.float32)
    swap = [(i, i ^ 1) for i in range(GX)]

    gains = lax.all_to_all(mode_gain, "gy", split_axis=0, concat_axis=1, tiled=True)[0]
    low_gain, high_gain = gains[:HALF], gains[HALF:]
    first, second = gain_moves()
    positive = gx < GX // 2
    gain_a = lax.ppermute(jnp.where(positive, low_gain, high_gain), ("gx", "gy"), first)
    gain_b = lax.ppermute(jnp.where(positive, high_gain, low_gain), ("gx", "gy"), second)

    stepped = advance(fields, velocity)

    columns = all_to_all(stepped, "gx").reshape(NX, CY)
    rows = jnp.asarray(ROWS)
    parts = jnp.dot(rows, columns, precision=highest)
    extra = parts[DEV]
    extra = jnp.where(
        (jnp.arange(DEV)[:, None] // GY) % 2 == 0, extra[None, :HALF], extra[None, HALF:]
    )
    sent = jnp.concatenate((parts[:DEV], extra, obs_height[0], obs_weight[0]), axis=1)
    got = all_to_all(sent, ("gx", "gy"))

    live = jnp.arange(128, dtype=jnp.int32)[None, :] < counts[0][:, None]
    weight = jnp.where(live, got[:, 512:640], 0.0)
    sum_w, sum_wh = scatter(cell_rows[0], cell_cols[0], weight, got[:, 384:512])

    scale = 1.0 / math.sqrt(NX * NY)
    local = jnp.asarray(LOCAL)
    turn_r, turn_i = jnp.asarray(TURN[:, :MY]), jnp.asarray(TURN[:, MY:])
    local_half = jnp.where(core == 0, local[:HALF], local[HALF:])

    def along_y(block, table):
        modes = jnp.dot(block, table, precision=highest).reshape(F, GY, 2 * MY)
        real, imag = modes[:, :, :MY], modes[:, :, MY:]
        out_r = jnp.sum(real * turn_r + imag * turn_i, axis=1)
        out_i = jnp.sum(imag * turn_r - real * turn_i, axis=1)
        return jnp.stack((out_r, out_i)) * scale

    mine = jnp.stack((along_y(got[:, :256], local), along_y(got[:, 256:384], local_half)))
    keep = jnp.where(core == 0, mine[..., :HALF], mine[..., HALF:])
    give = jnp.where(core == 0, mine[..., HALF:], mine[..., :HALF])
    other = lax.ppermute(give, "gx", swap)
    real_part = jnp.where(core == 0, keep[0], other[0])
    imag_part = jnp.where(core == 0, other[0], keep[0])
    extra_part = keep[1] + other[1]

    plain = 1.0 - special
    plus = jnp.stack(
        (real_part[0] - plain * imag_part[1], real_part[1] + plain * imag_part[0])
    )
    base = plain * real_part + special * imag_part
    turned = plain * imag_part + special * extra_part
    minus = jnp.stack((base[0] + turned[1], base[1] - turned[0]))

    def mix(coeffs, gain):
        lifted = jnp.einsum("pfn,fc->pnc", coeffs, lift_weight, precision=highest)
        gain_r, gain_i = gain[:, 0], gain[:, 1]
        mixed = jnp.stack(
            (
                gain_r * lifted[0] - gain_i * lifted[1],
                gain_r * lifted[1] + gain_i * lifted[0],
            )
        )
        return jnp.einsum("pnc,cf->pfn", mixed, project_weight, precision=highest)

    out_a = mix(jnp.where(core == 0, plus, minus), gain_a)
    out_b = mix(jnp.where(core == 0, minus, plus), gain_b)
    n_index = core * HALF + jnp.arange(HALF, dtype=jnp.int32)
    n_weight = jnp.where(n_index == 0, 1.0, 2.0).astype(jnp.float32) / math.sqrt(MX * MY)
    plus = jnp.where(core == 0, out_a, out_b) * n_weight
    minus = jnp.where(core == 0, out_b, out_a) * n_weight

    even = plus + plain * minus
    gap = plus - minus
    odd = plain * jnp.stack((gap[1], -gap[0])) + special * minus
    spare = jnp.stack((-minus[1], minus[0]))
    keep = jnp.stack((jnp.where(core == 0, even, odd), spare))
    give = jnp.stack((jnp.where(core == 0, odd, even), spare))
    other = lax.ppermute(give, "gx", swap)
    lower = jnp.where(core == 0, keep, other)
    upper = jnp.where(core == 0, other, keep)
    modes = jnp.concatenate((lower, upper), axis=-1)

    def back_y(coeffs, table):
        real, imag = coeffs[0][:, None, :], coeffs[1][:, None, :]
        turned = jnp.concatenate(
            (real * turn_r - imag * turn_i, real * turn_i + imag * turn_r), axis=-1
        ).reshape(DEV, 2 * MY)
        return lax.dot_general(turned, table, (((1,), (1,)), ((), ())), precision=highest)

    sent = jnp.concatenate((back_y(modes[0], local), back_y(modes[1], local_half)), axis=1)
    got = all_to_all(sent, ("gx", "gy"))

    spare_row = jnp.concatenate((got[0, 256:384], got[GY, 256:384]))
    block = jnp.concatenate(
        (got[:, :256], spare_row[None], jnp.zeros((7, 256), jnp.float32)), axis=0
    )
    correction = lax.dot_general(rows, block, (((0,), (0,)), ((), ())), precision=highest)
    correction = all_to_all(correction.reshape(GX, CX, CY), "gx")
    corrected = stepped + correction
    gradient = corrected[0] * sum_w - sum_wh
    return (corrected, gradient)


def solution(mesh):
    return jax.shard_map(
        body,
        mesh=mesh,
        in_specs=(
            P(None, "gx", "gy"),
            P(None, "gx", "gy"),
            P("gx", "gy", None, None),
            P(),
            P(),
            P(("gx", "gy"), None, None),
            P(("gx", "gy"), None, None),
            P(("gx", "gy"), None, None),
            P(("gx", "gy"), None, None),
            P(("gx", "gy"), None),
        ),
        out_specs=(P(None, "gx", "gy"), P("gx", "gy")),
        check_vma=False,
    )
```

time: 789 us -> 179 us (0.23)
  waiting for transfers between devices: 338 us -> 68.1 us
  local copies, waits for them, and re-layouts: 200 us -> 11.7 us
  other arithmetic: 180 us -> 7.72 us
  starting transfers between devices: 23.1 us -> 63.5 us
  Pallas kernels: 0 us -> 19.4 us
  blocking collectives: 15.6 us -> 0 us
  between operations: 14.9 us -> 1.43 us
    reduce_scatter x1 -> x0, waiting for transfers between devices: 209 us -> none  [body(): lax.psum_scatter(lax.dot_general(local_table, flattened, (((0,), (1,)), (...]
    gather x1 -> x0, local copies, waits for them, and re-layouts: 181 us -> none  [body(): misfit = arrived[1] * (surface[flat_index] - arrived[0]) * is_live]
    scatter-add x1 -> x0, other arithmetic: 171 us -> none  [body(): gradient = jnp.zeros((tile_rows * tile_cols,), jnp.float32).at[flat_index...]
    all_gather x1 -> x0, waiting for transfers between devices: 69.9 us -> none  [body(): block_in = lax.all_gather(spatial, 'gy', axis=0, tiled=True)]
    all_to_all x2 -> x5, waiting for transfers between devices: 0.01 us -> 62.3 us  [the longest x4 55.1 us: all_to_all(): return lax.all_to_all(array, axis, split_axis=0, concat_axis=0, tiled=True)]
    unnamed x4 -> x0, waiting for transfers between devices: 59.1 us -> none
    all_to_all x2 -> x5, starting transfers between devices: 10.7 us -> 42.9 us  [the longest x4 38.9 us: all_to_all(): return lax.all_to_all(array, axis, split_axis=0, concat_axis=0, tiled=True)]
    pallas_call x0 -> x1, Pallas kernels: none -> 19.4 us  [scatter(): pl.pallas_call(scatter_kernel, grid=(steps,), in_specs=[block] * 4, out_s...]
  transfers between devices with their start and end apart: 9 -> 13, of which waited for: 3 -> 6; matrix products, arithmetic and copies ran while one was open for 3% -> 4% of each run, Pallas kernels for 0% -> 11%
where the time goes in v1:
time: 179 us; the launch traced here: 178 us
  waiting for transfers between devices  68.1 us (38%)
  starting transfers between devices  63.5 us (35%)
  Pallas kernels  19.4 us (11%)
  local copies, waits for them, and re-layouts  11.7 us (7%)
  other arithmetic  7.72 us (4%)
  matrix products  5.94 us (3%)
    all_to_all x4, waiting for transfers between devices, all_to_all(): return lax.all_to_all(array, axis, split_axis=0, concat_axis=0, tiled=True)  55.1 us
    all_to_all x4, starting transfers between devices, all_to_all(): return lax.all_to_all(array, axis, split_axis=0, concat_axis=0, tiled=True)  38.9 us
    pallas_call x1, Pallas kernels, scatter(): pl.pallas_call(scatter_kernel, grid=(steps,), in_specs=[block] * 4, out_s...  19.4 us
    all_to_all x1, waiting for transfers between devices, body(): lax.all_to_all(mode_gain, 'gy', split_axis=0, concat_axis=1, tiled=True)[0]  7.16 us
    ppermute x1, starting transfers between devices, advance(): lax.ppermute(jnp.concatenate((fields[:, 0, :], velocity[:1, 0, :]), axis=...  5.04 us
    ppermute x1, starting transfers between devices, body(): lax.ppermute(jnp.where(positive, low_gain, high_gain), ('gx', 'gy'), first)  4.82 us
    ppermute x1, starting transfers between devices, advance(): south = lax.ppermute(fields[:, :, -1], 'gy', up_y)  4.66 us
    ppermute x1, waiting for transfers between devices, body(): lax.ppermute(jnp.where(positive, low_gain, high_gain), ('gx', 'gy'), first)  4.63 us
  transfers between devices with their start and end apart: 13, of which 6 were waited for; matrix products, arithmetic and copies ran while one was open for 4% of the time, Pallas kernels for 11%

profile of v1, /device:TPU:1, one launch (start us, length us, event | category | flops | bytes accessed | tf_op | source)
XLA Modules:
  0.0 177.8 jit_solution(11267651533617016220)
XLA Ops:
  1.6 1.5 fusion.68
  4.8 4.7 %collective-permute-start.3 = (f32[8,128]{1,0:T(8,128)S(1)}, f32[8,128]{1,0:T(8,128)S(1)}, u32[]{:S(2)}, u32[]{:S(2)}) collective-permute-start(f32[8,128]{1,0:T(8,128)S(1)} %bitcast.170), channel_id=1, source_target_pairs={{0,1},{1,2},{2,3},{3,4},{4,5},{5,6},{6,7},{7,8},{8,9},{9,10},{10,1... | collective-permute-start | bytes 12296 | tf_op jit(solution)/shard_map/ppermute | solution.py:84
  9.5 5.0 %collective-permute-start = (f32[9,256]{1,0:T(8,128)S(1)}, f32[9,256]{1,0:T(8,128)S(1)}, u32[]{:S(2)}, u32[]{:S(2)}) collective-permute-start(f32[9,256]{1,0:T(8,128)S(1)} %pad_maximum_fusion.8), channel_id=1, source_target_pairs={{32,0},{64,32},{96,64},{128,96},{160,128},{192,160},{224,192},{33,... | collective-permute-start | bytes 27656 | tf_op jit(solution)/shard_map/ppermute | solution.py:81
  14.6 1.9 %collective-permute-start.1 = (f32[8,256]{1,0:T(8,128)S(1)}, f32[8,256]{1,0:T(8,128)S(1)}, u32[]{:S(2)}, u32[]{:S(2)}) collective-permute-start(f32[8,256]{1,0:T(8,128)S(1)} %bitcast.169), channel_id=1, source_target_pairs={{0,32},{32,64},{64,96},{96,128},{128,160},{160,192},{192,224},{1,3... | collective-permute-start | bytes 24584 | tf_op jit(solution)/shard_map/ppermute | solution.py:80
  19.1 1.6 subtract_multiply_fusion
  20.9 1.5 dynamic-update-slice.1
  22.4 1.6 subtract_multiply_fusion.1
  24.0 1.4 fusion.2
  25.4 4.1 %all-to-all-start.1 = ((f32[8,128,256]{2,1,0:T(8,128)}), f32[8,128,256]{2,1,0:T(8,128)S(1)}, u32[]{:S(2)}, u32[]{:S(2)}) async-start(f32[8,128,256]{2,1,0:T(8,128)} %fusion.2), calls=%async_computation.1 | async-start | bytes 2097152 | tf_op jit(solution)/shard_map/all_to_all | solution.py:70
  29.5 15.1 %all-to-all-done.1 = f32[8,128,256]{2,1,0:T(8,128)S(1)} async-done(((f32[8,128,256]{2,1,0:T(8,128)}), f32[8,128,256]{2,1,0:T(8,128)S(1)}, u32[]{:S(2)}, u32[]{:S(2)}) %all-to-all-start.1) | async-done | bytes 1048608 | tf_op jit(solution)/shard_map/all_to_all | solution.py:70
  45.9 1.5 copy.42
  47.4 14.6 %all-to-all-start.2 = ((f32[256,1,640]{2,1,0:T(1,128)}), f32[256,1,640]{2,1,0:T(1,128)S(1)}, u32[]{:S(2)}, u32[]{:S(2)}) async-start(f32[256,1,640]{2,1,0:T(1,128)} %copy.42), calls=%async_computation.2 | async-start | bytes 1310720 | tf_op jit(solution)/shard_map/all_to_all | solution.py:70
  62.1 22.9 %all-to-all-done.2 = f32[256,1,640]{2,1,0:T(1,128)S(1)} async-done(((f32[256,1,640]{2,1,0:T(1,128)}), f32[256,1,640]{2,1,0:T(1,128)S(1)}, u32[]{:S(2)}, u32[]{:S(2)}) %all-to-all-start.2) | async-done | bytes 655392 | tf_op jit(solution)/shard_map/all_to_all | solution.py:70
  85.0 4.0 %all-to-all-start = ((f32[32,8,2,128]{3,2,1,0:T(2,128)}), f32[32,8,2,128]{3,2,1,0:T(2,128)S(1)}, u32[]{:S(2)}, u32[]{:S(2)}) async-start(f32[32,8,2,128]{3,2,1,0:T(2,128)} %param.16), calls=%async_computation | async-start | bytes 524288 | tf_op jit(solution)/shard_map/all_to_all | solution.py:201
  90.9 1.4 collective-permute-start.5
  92.3 7.2 %all-to-all-done = f32[32,8,2,128]{3,2,1,0:T(2,128)S(1)} async-done(((f32[32,8,2,128]{3,2,1,0:T(2,128)}), f32[32,8,2,128]{3,2,1,0:T(2,128)S(1)}, u32[]{:S(2)}, u32[]{:S(2)}) %all-to-all-start) | async-done | bytes 262176 | tf_op jit(solution)/shard_map/all_to_all | solution.py:201
  100.8 4.8 %collective-permute-start.4 = (f32[128,2,128]{2,0,1:T(8,128)S(1)}, f32[128,2,128]{2,0,1:T(8,128)S(1)}, u32[]{:S(2)}, u32[]{:S(2)}) collective-permute-start(f32[128,2,128]{2,0,1:T(8,128)S(1)} %bitcast.161), channel_id=1, source_target_pairs={{0,0},{1,1},{2,2},{3,3},{4,4},{5,5},{6,6},{7,7},{8,8},{9,9},{10,10... | collective-permute-start | bytes 393224 | tf_op jit(solution)/shard_map/ppermute | solution.py:205
  106.8 4.6 %collective-permute-done.4 = f32[128,2,128]{2,0,1:T(8,128)S(1)} collective-permute-done((f32[128,2,128]{2,0,1:T(8,128)S(1)}, f32[128,2,128]{2,0,1:T(8,128)S(1)}, u32[]{:S(2)}, u32[]{:S(2)}) %collective-permute-start.4) | collective-permute-done | bytes 131104 | tf_op jit(solution)/shard_map/ppermute | solution.py:205
  116.0 15.2 %all-to-all-start.3 = ((f32[256,1,384]{2,1,0:T(1,128)}), f32[256,1,384]{2,1,0:T(1,128)S(1)}, u32[]{:S(2)}, u32[]{:S(2)}) async-start(f32[256,1,384]{2,1,0:T(1,128)} %copy.44), calls=%async_computation.3 | async-start | bytes 786432 | tf_op jit(solution)/shard_map/all_to_all | solution.py:70
  131.3 17.1 %all-to-all-done.3 = f32[256,1,384]{2,1,0:T(1,128)S(1)} async-done(((f32[256,1,384]{2,1,0:T(1,128)}), f32[256,1,384]{2,1,0:T(1,128)S(1)}, u32[]{:S(2)}, u32[]{:S(2)}) %all-to-all-start.3) | async-done | bytes 393248 | tf_op jit(solution)/shard_map/all_to_all | solution.py:70
  149.6 1.3 copy.45
  150.9 5.0 %all-to-all-start.4 = ((f32[8,128,256]{2,1,0:T(8,128)}), f32[8,128,256]{2,1,0:T(8,128)S(1)}, u32[]{:S(2)}, u32[]{:S(2)}) async-start(f32[8,128,256]{2,1,0:T(8,128)} %bitcast.51), calls=%async_computation.4 | async-start | bytes 2097152 | tf_op jit(solution)/shard_map/all_to_all | solution.py:70
  155.9 19.4 %shard_map.149 = (f32[128,256]{1,0:T(8,128)S(1)}, f32[128,256]{1,0:T(8,128)S(1)}) custom-call(s32[256,128]{1,0:T(8,128)S(1)} %bitcast.145, s32[256,128]{1,0:T(8,128)S(1)} %bitcast.146, f32[256,128]{1,0:T(8,128)S(1)} %get-tuple-element.23.weight_ref, f32[256,128]{1,0:T(8,128)S(1)} %get-tuple-element.22.height_ref), custom_call_target="tpu_custom_call" | custom-call | flops 12884901888 | bytes 524288 | tf_op jit(solution)/shard_map/pallas_call | solution.py:163
  175.4 1.4 add.151
  (120 shorter events, 17.4 us)
Async XLA Ops:
  0.6 105.1 %copy-start = (f32[8,128]{1,0:T(8,128)S(1)}, f32[8,128]{1,0:T(8,128)}, u32[]{:S(2)}) copy-start(f32[8,128]{1,0:T(8,128)} %param.17) | copy-start | bytes 12292
  1.6 7.9 %copy-start.10 = (f32[2,128,256]{2,1,0:T(8,128)S(1)}, f32[2,128,256]{2,1,0:T(8,128)}, u32[]{:S(2)}) copy-start(f32[2,128,256]{2,1,0:T(8,128)} %param.15) | copy-start | bytes 786436
  1.6 7.9 %copy-start.3 = (f32[8,128,256]{2,1,0:T(8,128)S(1)}, f32[8,128,256]{2,1,0:T(8,128)}, u32[]{:S(2)}) copy-start(f32[8,128,256]{2,1,0:T(8,128)} %param.14) | copy-start | bytes 3145732
  3.3 14.6 %collective-permute-start.2 = (f32[9,128]{1,0:T(8,128)S(1)}, f32[9,128]{1,0:T(8,128)S(1)}, u32[]{:S(2)}, u32[]{:S(2)}) collective-permute-start(f32[9,128]{1,0:T(8,128)S(1)} %pad_maximum_fusion.10), channel_id=1, source_target_pairs={{1,0},{2,1},{3,2},{4,3},{5,4},{6,5},{7,6},{8,7},{9,8},{10,9},{11,1... | collective-permute-start | bytes 13832 | tf_op jit(solution)/shard_map/ppermute | solution.py:85
  4.8 12.9 %collective-permute-start.3 = (f32[8,128]{1,0:T(8,128)S(1)}, f32[8,128]{1,0:T(8,128)S(1)}, u32[]{:S(2)}, u32[]{:S(2)}) collective-permute-start(f32[8,128]{1,0:T(8,128)S(1)} %bitcast.170), channel_id=1, source_target_pairs={{0,1},{1,2},{2,3},{3,4},{4,5},{5,6},{6,7},{7,8},{8,9},{9,10},{10,1... | collective-permute-start | bytes 12296 | tf_op jit(solution)/shard_map/ppermute | solution.py:84
  9.5 11.2 %collective-permute-start = (f32[9,256]{1,0:T(8,128)S(1)}, f32[9,256]{1,0:T(8,128)S(1)}, u32[]{:S(2)}, u32[]{:S(2)}) collective-permute-start(f32[9,256]{1,0:T(8,128)S(1)} %pad_maximum_fusion.8), channel_id=1, source_target_pairs={{32,0},{64,32},{96,64},{128,96},{160,128},{192,160},{224,192},{33,... | collective-permute-start | bytes 27656 | tf_op jit(solution)/shard_map/ppermute | solution.py:81
  14.6 6.2 %collective-permute-start.1 = (f32[8,256]{1,0:T(8,128)S(1)}, f32[8,256]{1,0:T(8,128)S(1)}, u32[]{:S(2)}, u32[]{:S(2)}) collective-permute-start(f32[8,256]{1,0:T(8,128)S(1)} %bitcast.169), channel_id=1, source_target_pairs={{0,32},{32,64},{64,96},{96,128},{128,160},{160,192},{192,224},{1,3... | collective-permute-start | bytes 24584 | tf_op jit(solution)/shard_map/ppermute | solution.py:80
  25.4 19.2 %copy-start.5 = (f32[264,1024]{1,0:T(8,128)S(1)}, f32[264,1024]{1,0:T(8,128)}, u32[]{:S(2)}) copy-start(f32[264,1024]{1,0:T(8,128)} %constant.88.clone) | copy-start | bytes 3244036
  25.4 19.2 %all-to-all-start.1 = ((f32[8,128,256]{2,1,0:T(8,128)}), f32[8,128,256]{2,1,0:T(8,128)S(1)}, u32[]{:S(2)}, u32[]{:S(2)}) async-start(f32[8,128,256]{2,1,0:T(8,128)} %fusion.2), calls=%async_computation.1 | async-start | bytes 2097152 | tf_op jit(solution)/shard_map/all_to_all | solution.py:70
  47.4 37.6 %all-to-all-start.2 = ((f32[256,1,640]{2,1,0:T(1,128)}), f32[256,1,640]{2,1,0:T(1,128)S(1)}, u32[]{:S(2)}, u32[]{:S(2)}) async-start(f32[256,1,640]{2,1,0:T(1,128)} %copy.42), calls=%async_computation.2 | async-start | bytes 1310720 | tf_op jit(solution)/shard_map/all_to_all | solution.py:70
  62.0 27.1 %copy-start.9 = (f32[256,512]{1,0:T(8,128)S(1)}, f32[256,512]{1,0:T(8,128)}, u32[]{:S(2)}) copy-start(f32[256,512]{1,0:T(8,128)} %constant.89.clone) | copy-start | bytes 1572868
  85.0 14.5 %all-to-all-start = ((f32[32,8,2,128]{3,2,1,0:T(2,128)}), f32[32,8,2,128]{3,2,1,0:T(2,128)S(1)}, u32[]{:S(2)}, u32[]{:S(2)}) async-start(f32[32,8,2,128]{3,2,1,0:T(2,128)} %param.16), calls=%async_computation | async-start | bytes 524288 | tf_op jit(solution)/shard_map/all_to_all | solution.py:201
  90.8 15.8 %copy-start.17 = (f32[128,8]{0,1:T(8,128)S(1)}, f32[128,8]{0,1:T(8,128)}, u32[]{:S(2)}) copy-start(f32[128,8]{0,1:T(8,128)} %param.18) | copy-start | bytes 12292
  90.9 14.8 %collective-permute-start.5 = (f32[2,2,8,128]{3,2,1,0:T(8,128)S(1)}, f32[2,2,8,128]{3,2,1,0:T(8,128)S(1)}, u32[]{:S(2)}, u32[]{:S(2)}) collective-permute-start(f32[2,2,8,128]{3,2,1,0:T(8,128)S(1)} %get-tuple-element.53), channel_id=1, source_target_pairs={{0,32},{32,0},{64,96},{96,64},{128,160},{160,128},{192,224},{224,1... | collective-permute-start | bytes 49160 | tf_op jit(solution)/shard_map/ppermute | solution.py:239
  99.5 7.0 %collective-permute-start.6 = (f32[128,2,128]{2,0,1:T(8,128)S(1)}, f32[128,2,128]{2,0,1:T(8,128)S(1)}, u32[]{:S(2)}, u32[]{:S(2)}) collective-permute-start(f32[128,2,128]{2,0,1:T(8,128)S(1)} %bitcast.162), channel_id=1, source_target_pairs={{0,32},{1,33},{2,34},{3,35},{4,36},{5,37},{6,38},{7,39},{8,40},{9,... | collective-permute-start | bytes 393224 | tf_op jit(solution)/shard_map/ppermute | solution.py:206
  100.8 10.6 %collective-permute-start.4 = (f32[128,2,128]{2,0,1:T(8,128)S(1)}, f32[128,2,128]{2,0,1:T(8,128)S(1)}, u32[]{:S(2)}, u32[]{:S(2)}) collective-permute-start(f32[128,2,128]{2,0,1:T(8,128)S(1)} %bitcast.161), channel_id=1, source_target_pairs={{0,0},{1,1},{2,2},{3,3},{4,4},{5,5},{6,6},{7,7},{8,8},{9,9},{10,10... | collective-permute-start | bytes 393224 | tf_op jit(solution)/shard_map/ppermute | solution.py:205
  111.7 1.5 collective-permute-start.7
  115.0 16.2 %copy-start.19 = (s32[1,256]{1,0:T(1,128)S(1)}, s32[1,256]{1,0:T(1,128)}, u32[]{:S(2)}) copy-start(s32[1,256]{1,0:T(1,128)} %param.23) | copy-start | bytes 3076
  116.0 32.4 %copy-start.6 = (f32[256,1024]{1,0:T(8,128)S(1)}, f32[256,1024]{1,0:T(8,128)}, u32[]{:S(2)}) copy-start(f32[256,1024]{1,0:T(8,128)} %constant.102) | copy-start | bytes 3145732
  116.0 32.5 %copy-start.18 = (f32[1024]{0:T(1024)S(1)}, f32[1024]{0:T(1024)}, u32[]{:S(2)}) copy-start(f32[1024]{0:T(1024)} %constant.104) | copy-start | bytes 12292
  116.0 32.4 %all-to-all-start.3 = ((f32[256,1,384]{2,1,0:T(1,128)}), f32[256,1,384]{2,1,0:T(1,128)S(1)}, u32[]{:S(2)}, u32[]{:S(2)}) async-start(f32[256,1,384]{2,1,0:T(1,128)} %copy.44), calls=%async_computation.3 | async-start | bytes 786432 | tf_op jit(solution)/shard_map/all_to_all | solution.py:70
  150.9 5.0 %copy-start.1 = (s32[1,256,128]{2,1,0:T(8,128)S(1)}, s32[1,256,128]{2,1,0:T(8,128)}, u32[]{:S(2)}) copy-start(s32[1,256,128]{2,1,0:T(8,128)} %param.21) | copy-start | bytes 393220
  150.9 5.0 %copy-start.2 = (s32[1,256,128]{2,1,0:T(8,128)S(1)}, s32[1,256,128]{2,1,0:T(8,128)}, u32[]{:S(2)}) copy-start(s32[1,256,128]{2,1,0:T(8,128)} %param.22) | copy-start | bytes 393220
  150.9 24.5 %all-to-all-start.4 = ((f32[8,128,256]{2,1,0:T(8,128)}), f32[8,128,256]{2,1,0:T(8,128)S(1)}, u32[]{:S(2)}, u32[]{:S(2)}) async-start(f32[8,128,256]{2,1,0:T(8,128)} %bitcast.51), calls=%async_computation.4 | async-start | bytes 2097152 | tf_op jit(solution)/shard_map/all_to_all | solution.py:70
  (9 other events, 10.7 us)

commit v2 on v1

v2 whole, which is shorter than its diff:
```python
import math

import jax
import jax.numpy as jnp
import numpy as np
from jax import lax
from jax.experimental import pallas as pl
from jax.experimental.pallas import tpu as pltpu
from jax.sharding import PartitionSpec as P

MX = 256
MY = 256
NX = 1024
NY = 8192
F = 8
CX = 128
CY = 256
GX = 8
GY = 32
DEV = GX * GY
HALF = MY // 2

time_step = 0.2
diffusion = 0.25
highest = lax.Precision.HIGHEST


ORDER = np.array(
    [GX * gy + 4 * high + low for high in range(2) for low in range(4) for gy in range(GY)]
)


def tables():
    x = np.arange(MX)
    q = np.arange(MX // 2)
    ang = 2.0 * np.pi * (q[:, None] * x[None, :]) / NX
    fore_x = np.concatenate((np.cos(ang), -np.sin(ang)))
    m = np.arange(MX)
    q = np.where(m < MX // 2, m, m - MX)
    ang = 2.0 * np.pi * (x[:, None] * q[None, :]) / NX
    back_x = np.concatenate((np.cos(ang), -np.sin(ang)), axis=1)
    ang = 2.0 * np.pi * np.arange(8) / 8.0
    period = np.stack([np.tile(row[:, None], (1, CY)) for row in (np.cos(ang), -np.sin(ang))])
    ang = 2.0 * np.pi * (ORDER[:, None] * np.arange(CY)[None, :]) / NY
    fore_y = np.concatenate((np.cos(ang), np.sin(ang)))
    back_y = np.concatenate((np.cos(ang.T), np.sin(ang.T)))
    turn = np.zeros((2, 4, 4, GY, 2, 2, 32))
    for quarter in range(4):
        for low in range(4):
            for high in range(2):
                n = 8 * quarter + 4 * high + low
                ang = 2.0 * np.pi * ((n * np.arange(GY)) % GY) / GY
                turn[0, quarter, low, :, :, high] = np.cos(ang)[:, None, None]
                turn[1, quarter, low, :, :, high] = np.sin(ang)[:, None, None]
    turn = turn.reshape(2, 4, 4, GY, 128)
    return tuple(
        array.astype(np.float32) for array in (fore_x, back_x, period, fore_y, back_y, turn)
    )


FORE_X, BACK_X, PERIOD, FORE_Y, BACK_Y, TURN = tables()
SCALE_IN = 1.0 / math.sqrt(NX * NY)
SCALE_OUT = 1.0 / math.sqrt(MX * MY)


def all_to_all(array, axis):
    return lax.all_to_all(array, axis, split_axis=0, concat_axis=0, tiled=True)


def dot(a, b, contract=((1,), (0,))):
    return lax.dot_general(
        a, b, (contract, ((), ())), precision=highest, preferred_element_type=jnp.float32
    )


def shape(*dims):
    return jax.ShapeDtypeStruct(dims, jnp.float32)


def local_kernel(kernel, out_shape, operands, scalars=(), flops=0, scratch=()):
    vmem = pl.BlockSpec(memory_space=pltpu.VMEM)
    smem = pl.BlockSpec(memory_space=pltpu.SMEM)
    size = sum(4 * math.prod(a.shape) for a in (*operands, *out_shape))
    return pl.pallas_call(
        kernel,
        in_specs=[smem] * len(scalars) + [vmem] * len(operands),
        out_specs=[vmem] * len(out_shape),
        out_shape=out_shape,
        scratch_shapes=scratch,
        compiler_params=pltpu.CompilerParams(vmem_limit_bytes=24 * 1024 * 1024),
        cost_estimate=pl.CostEstimate(flops=flops, bytes_accessed=size, transcendentals=0),
    )(*scalars, *operands)


def edge_kernel(fields_ref, velocity_ref, last_x_ref, first_x_ref, last_y_ref, first_y_ref):
    first_x_ref[...] = jnp.zeros((16, CY), jnp.float32)
    first_y_ref[...] = jnp.zeros((16, CX), jnp.float32)
    row = lax.broadcasted_iota(jnp.int32, (8, CY), 0)
    col = lax.broadcasted_iota(jnp.int32, (8, CY), 1)
    pick = jnp.where(
        ((row == 0) & (col == 0)) | ((row == 1) & (col == CY - 1)), 1.0, 0.0
    ).astype(jnp.float32)
    for f in range(F):
        block = fields_ref[f]
        last_x_ref[f : f + 1] = block[CX - 1 : CX]
        first_x_ref[f : f + 1] = block[0:1]
        ends = dot(pick, block, ((1,), (1,)))
        first_y_ref[f : f + 1] = ends[0:1]
        last_y_ref[f : f + 1] = ends[1:2]
    first_x_ref[F : F + 1] = velocity_ref[0, 0:1]
    first_y_ref[F : F + 1] = dot(pick, velocity_ref[1], ((1,), (1,)))[0:1]


def step_kernel(
    fields_ref, velocity_ref, west_ref, east_ref, south_ref, north_ref, out_ref, *block_refs
):
    row = lax.broadcasted_iota(jnp.int32, (CX, CY), 0)
    col = lax.broadcasted_iota(jnp.int32, (CX, CY), 1)
    first_row, last_row = row == 0, row == CX - 1
    first_col, last_col = col == 0, col == CY - 1
    gx, gy = lax.axis_index("gx"), lax.axis_index("gy")
    is_open = [
        jnp.where(test, 1.0, 0.0) for test in (gx > 0, gx < GX - 1, gy > 0, gy < GY - 1)
    ]
    before = jnp.transpose(south_ref[...])
    after = jnp.transpose(north_ref[...])
    speed = velocity_ref[0]
    shut = jnp.where(first_row, is_open[0], 1.0)
    low_w = time_step * shut * (jnp.maximum(speed, 0.0) + diffusion)
    high_w = time_step * shut * (jnp.minimum(speed, 0.0) - diffusion)
    edge = east_ref[F : F + 1]
    low_edge = time_step * is_open[1] * (jnp.maximum(edge, 0.0) + diffusion)
    high_edge = time_step * is_open[1] * (jnp.minimum(edge, 0.0) - diffusion)
    low_e = jnp.where(last_row, low_edge, pltpu.roll(low_w, CX - 1, 0))
    high_e = jnp.where(last_row, high_edge, pltpu.roll(high_w, CX - 1, 0))
    speed = velocity_ref[1]
    shut = jnp.where(first_col, is_open[2], 1.0)
    low_s = time_step * shut * (jnp.maximum(speed, 0.0) + diffusion)
    high_s = time_step * shut * (jnp.minimum(speed, 0.0) - diffusion)
    edge = after[:, F : F + 1]
    low_edge = time_step * is_open[3] * (jnp.maximum(edge, 0.0) + diffusion)
    high_edge = time_step * is_open[3] * (jnp.minimum(edge, 0.0) - diffusion)
    low_n = jnp.where(last_col, low_edge, pltpu.roll(low_s, CY - 1, 1))
    high_n = jnp.where(last_col, high_edge, pltpu.roll(high_s, CY - 1, 1))
    own = 1.0 - low_e + high_w - low_n + high_s
    for f in range(F):
        block = fields_ref[f]
        west = jnp.where(first_row, west_ref[f : f + 1], pltpu.roll(block, 1, 0))
        east = jnp.where(last_row, east_ref[f : f + 1], pltpu.roll(block, CX - 1, 0))
        south = jnp.where(first_col, before[:, f : f + 1], pltpu.roll(block, 1, 1))
        north = jnp.where(last_col, after[:, f : f + 1], pltpu.roll(block, CY - 1, 1))
        out_ref[f] = (
            own * block + low_w * west - high_e * east + low_s * south - high_n * north
        )
    for k, ref in enumerate(block_refs):
        ref[...] = out_ref[lax.rem(lax.axis_index("gx") + k, GX)]


def quarter_turn(index, t):
    place = lax.rem(index * t, 4)
    cosine = jnp.where(place == 0, 1.0, jnp.where(place == 2, -1.0, 0.0))
    sine = jnp.where(place == 1, 1.0, jnp.where(place == 3, -1.0, 0.0))
    return cosine.astype(jnp.float32), sine.astype(jnp.float32)


def forward_kernel(*refs):
    *block_refs, fore_x_ref, period_ref, fore_y_ref, height_ref, weight_ref = refs[:-3]
    out_ref, columns_ref, parts_ref = refs[-3:]
    for k, ref in enumerate(block_refs):
        source = lax.rem(lax.axis_index("gx") + (GX - k), GX)
        columns_ref[pl.ds(pl.multiple_of(source * CX, CX), CX), :] = ref[...]
    q = lax.broadcasted_iota(jnp.int32, (HALF, CY), 0)
    real = jnp.zeros((HALF, CY), jnp.float32)
    imag = jnp.zeros((HALF, CY), jnp.float32)
    for t in range(4):
        piece = dot(fore_x_ref[...], columns_ref[t * MX : (t + 1) * MX])
        piece_r, piece_i = piece[:HALF], piece[HALF:]
        if t == 0:
            real, imag = piece_r, piece_i
        else:
            cosine, sine = quarter_turn(q, t)
            real = real + piece_r * cosine + piece_i * sine
            imag = imag + piece_i * cosine - piece_r * sine
    folded = jnp.sum(columns_ref[...].reshape(NX // 8, 8, CY), axis=0)
    last_r = jnp.sum(folded * period_ref[0], axis=0, keepdims=True)
    last_i = jnp.sum(folded * period_ref[1], axis=0, keepdims=True)
    row = lax.broadcasted_iota(jnp.int32, (HALF, HALF), 0)
    col = lax.broadcasted_iota(jnp.int32, (HALF, HALF), 1)
    mirror = jnp.where(row + col == HALF, 1.0, 0.0).astype(jnp.float32)
    parts_ref[0:HALF] = real
    parts_ref[HALF:MX] = jnp.where(q == 0, last_r, dot(mirror, real))
    parts_ref[MX : MX + HALF] = imag
    parts_ref[MX + HALF :] = -jnp.where(q == 0, last_i, dot(mirror, imag))
    mixed = dot(fore_y_ref[...], parts_ref[...], ((1,), (1,)))
    modes = (mixed[:MY, :MX] + mixed[MY:, MX:], mixed[:MY, MX:] - mixed[MY:, :MX])
    group = lax.broadcasted_iota(jnp.int32, (GY, 128), 1) // 32
    for low in range(4):
        for half in range(2):
            tiles = [
                modes[part][high * 128 + low * 32 : high * 128 + low * 32 + 32, half * 128 : half * 128 + 128]
                for part in range(2)
                for high in range(2)
            ]
            for s in range(4):
                gx = 4 * half + s
                value = None
                for k, tile in enumerate(tiles):
                    shift = (32 * (k - s)) % 128
                    moved = pltpu.roll(tile, shift, 1) if shift else tile
                    value = moved if value is None else jnp.where(group == k, moved, value)
                out_ref[gx * GY : (gx + 1) * GY, 0, low * 128 : (low + 1) * 128] = value
    out_ref[:, 0, 512:640] = height_ref[...]
    out_ref[:, 0, 640:768] = weight_ref[...]


def mix_kernel(got_ref, turn_ref, gain_ref, lift_ref, project_ref, out_ref):
    gy = lax.axis_index("gy")
    quarter = lax.rem(gy, 4)
    lane = lax.broadcasted_iota(jnp.int32, (F, 128), 1)
    is_real = lane < 64
    high_zero = (lane // 32) % 2 == 0
    for low in range(4):
        cosine = turn_ref[0, quarter, low]
        sine = turn_ref[1, quarter, low]
        straight, crossed = [], []
        for f in range(F):
            block = got_ref[f * GY : (f + 1) * GY, low * 128 : (low + 1) * 128]
            straight.append(jnp.sum(block * cosine, axis=0, keepdims=True))
            crossed.append(jnp.sum(block * sine, axis=0, keepdims=True))
        crossed = pltpu.roll(jnp.concatenate(crossed, axis=0), 64, 1)
        coeffs = jnp.concatenate(straight, axis=0) + jnp.where(is_real, crossed, -crossed)
        lifted = dot(jnp.transpose(coeffs * SCALE_IN), lift_ref[...])
        mixed_r, mixed_i = [], []
        for high in range(2):
            lift_r = lifted[high * 32 : high * 32 + 32]
            lift_i = lifted[64 + high * 32 : 96 + high * 32]
            gain_r = gain_ref[0, 4 * high + low]
            gain_i = gain_ref[1, 4 * high + low]
            mixed_r.append(gain_r * lift_r - gain_i * lift_i)
            mixed_i.append(gain_r * lift_i + gain_i * lift_r)
        mixed = jnp.concatenate(mixed_r + mixed_i, axis=0)
        outgoing = dot(project_ref[...], mixed, ((1,), (1,)))
        first = high_zero & (gy == 0) if low == 0 else None
        scale = 2.0 * SCALE_OUT if first is None else jnp.where(first, SCALE_OUT, 2.0 * SCALE_OUT)
        outgoing = outgoing * scale
        swapped = pltpu.roll(outgoing, 64, 1)
        swapped = jnp.where(is_real, -swapped, swapped)
        for f in range(F):
            out_ref[f * GY : (f + 1) * GY, 0, low * 128 : (low + 1) * 128] = (
                outgoing[f : f + 1] * cosine + swapped[f : f + 1] * sine
            )


def backward_kernel(got_ref, back_y_ref, back_x_ref, *refs):
    *out_refs, modes_ref, field_ref = refs
    group = lax.broadcasted_iota(jnp.int32, (GY, 128), 1) // 32
    for low in range(4):
        for half in range(2):
            tiles = [
                got_ref[gx * GY : (gx + 1) * GY, low * 128 : (low + 1) * 128]
                for gx in range(4 * half, 4 * half + 4)
            ]
            for part in range(2):
                for high in range(2):
                    k = 2 * part + high
                    value = None
                    for s, tile in enumerate(tiles):
                        shift = (32 * (s - k)) % 128
                        moved = pltpu.roll(tile, shift, 1) if shift else tile
                        value = moved if value is None else jnp.where(group == s, moved, value)
                    lanes = part * MX + half * 128
                    start = high * 128 + low * 32
                    modes_ref[start : start + 32, lanes : lanes + 128] = value
    mixed = dot(back_y_ref[...], modes_ref[...])
    real = mixed[:CY, :MX] - mixed[CY:, MX:]
    imag = mixed[:CY, MX:] + mixed[CY:, :MX]
    index = lax.broadcasted_iota(jnp.int32, (CY, MX), 1)
    for t in range(4):
        if t == 0:
            turned = jnp.concatenate((real, imag), axis=1)
        else:
            cosine, sine = quarter_turn(index, t)
            turned = jnp.concatenate(
                (real * cosine - imag * sine, imag * cosine + real * sine), axis=1
            )
        field_ref[t * MX : (t + 1) * MX] = dot(back_x_ref[...], turned, ((1,), (1,)))
    for k, ref in enumerate(out_refs):
        owner = lax.rem(lax.axis_index("gx") + k, GX)
        ref[...] = field_ref[pl.ds(pl.multiple_of(owner * CX, CX), CX), :]


def finish_kernel(*refs):
    stepped_ref, *block_refs, w_0, w_1, wh_0, wh_1, out_ref, gradient_ref = refs
    for k, ref in enumerate(block_refs):
        f = lax.rem(lax.axis_index("gx") + (GX - k), GX)
        out_ref[f] = stepped_ref[f] + ref[...]
    gradient_ref[...] = out_ref[0] * (w_0[...] + w_1[...]) - (wh_0[...] + wh_1[...])


def exchange(blocks):
    moved = {0: blocks[0]}
    for k in (4, 3, 5, 2, 6, 7, 1):
        moved[k] = lax.ppermute(blocks[k], "gx", [(i, (i + k) % GX) for i in range(GX)])
    return [moved[k] for k in range(GX)]


def advance(fields, velocity):
    up_x = [(i, i + 1) for i in range(GX - 1)]
    down_x = [(i + 1, i) for i in range(GX - 1)]
    up_y = [(i, i + 1) for i in range(GY - 1)]
    down_y = [(i + 1, i) for i in range(GY - 1)]
    last_x, first_x, last_y, first_y = local_kernel(
        edge_kernel, [shape(F, CY), shape(16, CY), shape(F, CX), shape(16, CX)], (fields, velocity)
    )
    west = lax.ppermute(last_x, "gx", up_x)
    east = lax.ppermute(first_x, "gx", down_x)
    south = lax.ppermute(last_y, "gy", up_y)
    north = lax.ppermute(first_y, "gy", down_y)
    stepped, *blocks = local_kernel(
        step_kernel,
        [shape(F, CX, CY)] + [shape(CX, CY)] * GX,
        (fields, velocity, west, east, south, north),
    )
    return stepped, blocks


CHUNK = 16
CPTS = CHUNK * 128


def scatter_kernel(rows_ref, cols_ref, weight_ref, height_ref, sum_w_ref, sum_wh_ref, a_ref, b_ref, acc_ref):
    step = pl.program_id(0)
    weight = weight_ref[...]
    product = weight * height_ref[...]
    pieces = []
    for value in (weight, product):
        for _ in range(3):
            piece = value.astype(jnp.bfloat16)
            pieces.append(piece)
            value = value - piece.astype(jnp.float32)
    rows = rows_ref[...].astype(jnp.float32).astype(jnp.bfloat16)
    cols = cols_ref[...].astype(jnp.float32).astype(jnp.bfloat16)
    spot_r = lax.broadcasted_iota(jnp.int32, (CX, 128), 0).astype(jnp.float32).astype(jnp.bfloat16)
    spot_c = lax.broadcasted_iota(jnp.int32, (CY, 128), 0).astype(jnp.float32).astype(jnp.bfloat16)
    zero = jnp.zeros((CX, 128), jnp.bfloat16)
    one_c = jnp.ones((CY, 128), jnp.bfloat16)
    zero_c = jnp.zeros((CY, 128), jnp.bfloat16)
    for s in range(CHUNK):
        lanes = pl.ds(s * 128, 128)
        hit = spot_r == jnp.broadcast_to(rows[s : s + 1], (CX, 128))
        for k, piece in enumerate(pieces):
            a_ref[pl.ds(k * CX, CX), lanes] = jnp.where(
                hit, jnp.broadcast_to(piece[s : s + 1], (CX, 128)), zero
            )
        hit = spot_c == jnp.broadcast_to(cols[s : s + 1], (CY, 128))
        b_ref[:, lanes] = jnp.where(hit, one_c, zero_c)
    part = lax.dot_general(
        a_ref[...], b_ref[...], (((1,), (1,)), ((), ())), preferred_element_type=jnp.float32
    )

    @pl.when(step == 0)
    def _():
        acc_ref[...] = part

    @pl.when(step > 0)
    def _():
        acc_ref[...] += part

    @pl.when(step == pl.num_programs(0) - 1)
    def _():
        sum_w_ref[...] = acc_ref[0:CX] + acc_ref[CX : 2 * CX] + acc_ref[2 * CX : 3 * CX]
        sum_wh_ref[...] = (
            acc_ref[3 * CX : 4 * CX] + acc_ref[4 * CX : 5 * CX] + acc_ref[5 * CX : 6 * CX]
        )


def scatter(rows, cols, weight, height):
    steps = rows.shape[0] // CHUNK
    block = pl.BlockSpec((CHUNK, 128), lambda i: (i, 0))
    whole = pl.BlockSpec((CX, CY), lambda i: (0, 0))
    return pl.pallas_call(
        scatter_kernel,
        grid=(steps,),
        in_specs=[block] * 4,
        out_specs=[whole, whole],
        out_shape=[jax.ShapeDtypeStruct((CX, CY), jnp.float32)] * 2,
        scratch_shapes=[
            pltpu.VMEM((6 * CX, CPTS), jnp.bfloat16),
            pltpu.VMEM((CY, CPTS), jnp.bfloat16),
            pltpu.VMEM((6 * CX, CY), jnp.float32),
        ],
        compiler_params=pltpu.CompilerParams(vmem_limit_bytes=24 * 1024 * 1024),
        cost_estimate=pl.CostEstimate(
            flops=2 * 6 * CX * CY * 128 * rows.shape[0],
            bytes_accessed=4 * 128 * 4 * rows.shape[0],
            transcendentals=0,
        ),
    )(rows, cols, weight, height)


def body(
    fields,
    velocity,
    mode_gain,
    lift_weight,
    project_weight,
    obs_height,
    obs_weight,
    cell_rows,
    cell_cols,
    counts,
):
    stepped, blocks = advance(fields, velocity)
    sent = local_kernel(
        forward_kernel,
        [shape(DEV, 1, 768)],
        (*exchange(blocks), *map(jnp.asarray, (FORE_X, PERIOD, FORE_Y)), obs_height[0], obs_weight[0]),
        flops=6 * 2 * (256 * NX * CY + 512 * 256 * 512),
        scratch=[pltpu.VMEM((NX, CY), jnp.float32), pltpu.VMEM((2 * MX, CY), jnp.float32)],
    )[0]
    got = all_to_all(sent, ("gx", "gy")).reshape(DEV, 768)
    sent = local_kernel(
        mix_kernel,
        [shape(DEV, 1, 512)],
        (
            got,
            jnp.asarray(TURN),
            mode_gain.transpose(2, 1, 0, 3),
            lift_weight,
            project_weight.T,
        ),
        flops=6 * 2 * 512 * 128 * 16,
    )[0]

    live = jnp.arange(128, dtype=jnp.int32)[None, :] < counts[0][:, None]
    weight = jnp.where(live, got[:, 640:], 0.0)
    height = got[:, 512:640]
    cut = 112
    w_0, wh_0 = scatter(cell_rows[0, :cut], cell_cols[0, :cut], weight[:cut], height[:cut])

    back = all_to_all(sent, ("gx", "gy")).reshape(DEV, 512)
    back, w_0, wh_0 = lax.optimization_barrier((back, w_0, wh_0))
    blocks = local_kernel(
        backward_kernel,
        [shape(CX, CY)] * GX,
        (back, jnp.asarray(BACK_Y), jnp.asarray(BACK_X)),
        flops=6 * 2 * (512 * NX * CY + 512 * 256 * 512),
        scratch=[pltpu.VMEM((MY, 2 * MX), jnp.float32), pltpu.VMEM((NX, CY), jnp.float32)],
    )
    weight, w_0 = lax.optimization_barrier((weight, w_0))
    w_1, wh_1 = scatter(cell_rows[0, cut:], cell_cols[0, cut:], weight[cut:], height[cut:])
    return tuple(
        local_kernel(
            finish_kernel,
            [shape(F, CX, CY), shape(CX, CY)],
            (stepped, *exchange(blocks), w_0, w_1, wh_0, wh_1),
        )
    )


def solution(mesh):
    return jax.shard_map(
        body,
        mesh=mesh,
        in_specs=(
            P(None, "gx", "gy"),
            P(None, "gx", "gy"),
            P("gx", "gy", None, None),
            P(),
            P(),
            P(("gx", "gy"), None, None),
            P(("gx", "gy"), None, None),
            P(("gx", "gy"), None, None),
            P(("gx", "gy"), None, None),
            P(("gx", "gy"), None),
        ),
        out_specs=(P(None, "gx", "gy"), P("gx", "gy")),
        check_vma=False,
    )
```

time: 179 us -> 146 us (0.82)
  Pallas kernels: 19.4 us -> 34.1 us
  starting transfers between devices: 63.5 us -> 49.3 us
  waiting for transfers between devices: 68.1 us -> 55.7 us
  other arithmetic: 7.72 us -> 0.1 us
  local copies, waits for them, and re-layouts: 11.7 us -> 4.84 us
  matrix products: 5.94 us -> 0 us
    all_to_all x4 -> x2, waiting for transfers between devices: 55.1 us -> 35.2 us  [all_to_all(): return lax.all_to_all(array, axis, split_axis=0, concat_axis=0, tiled=True)]
    all_to_all x4 -> x2, starting transfers between devices: 38.9 us -> 20.9 us  [all_to_all(): return lax.all_to_all(array, axis, split_axis=0, concat_axis=0, tiled=True)]
    ppermute x8 -> x18, waiting for transfers between devices: 5.82 us -> 20.5 us  [the longest x14 19.8 us: exchange(): lax.ppermute(blocks[k], 'gx', [(i, (i + k) % GX) for i in range(GX)])]
    pallas_call x0 -> x6, Pallas kernels: none -> 14.7 us  [local_kernel(): pl.pallas_call(kernel, in_specs=[smem] * len(scalars) + [vmem] * len(oper...]
    ppermute x8 -> x18, starting transfers between devices: 20.7 us -> 28.3 us  [the longest x14 15.9 us: exchange(): lax.ppermute(blocks[k], 'gx', [(i, (i + k) % GX) for i in range(GX)])]
    all_to_all x1 -> x0, waiting for transfers between devices: 7.16 us -> none  [body(): lax.all_to_all(mode_gain, 'gy', split_axis=0, concat_axis=1, tiled=True)[0]]
    dot_general x11 -> x0, matrix products: 5.94 us -> none  [the longest x3 1.47 us: back_y(): lax.dot_general(turned, table, (((1,), (1,)), ((), ())), precision=highest)]
    all_to_all x1 -> x0, starting transfers between devices: 4.01 us -> none  [body(): lax.all_to_all(mode_gain, 'gy', split_axis=0, concat_axis=1, tiled=True)[0]]
  transfers between devices with their start and end apart: 13 -> 20, of which waited for: 6 -> 8; matrix products, arithmetic and copies ran while one was open for 4% -> 0% of each run, Pallas kernels for 11% -> 13%
where the time goes in v2:
time: 146 us; the launch traced here: 145 us
  waiting for transfers between devices  55.7 us (38%)
  starting transfers between devices  49.3 us (34%)
  Pallas kernels  34.1 us (23%)
  local copies, waits for them, and re-layouts  4.84 us (3%)
    all_to_all x2, waiting for transfers between devices, all_to_all(): return lax.all_to_all(array, axis, split_axis=0, concat_axis=0, tiled=True)  35.2 us
    all_to_all x2, starting transfers between devices, all_to_all(): return lax.all_to_all(array, axis, split_axis=0, concat_axis=0, tiled=True)  20.9 us
    ppermute x14, waiting for transfers between devices, exchange(): lax.ppermute(blocks[k], 'gx', [(i, (i + k) % GX) for i in range(GX)])  19.8 us
    pallas_call x2, Pallas kernels, scatter(): pl.pallas_call(scatter_kernel, grid=(steps,), in_specs=[block] * 4, out_s...  19.4 us
    ppermute x14, starting transfers between devices, exchange(): lax.ppermute(blocks[k], 'gx', [(i, (i + k) % GX) for i in range(GX)])  15.9 us
    pallas_call x6, Pallas kernels, local_kernel(): pl.pallas_call(kernel, in_specs=[smem] * len(scalars) + [vmem] * len(oper...  14.7 us
    ppermute x1, starting transfers between devices, advance(): east = lax.ppermute(first_x, 'gx', down_x)  5.15 us
    unnamed x35, local copies, waits for them, and re-layouts  4.79 us
  transfers between devices with their start and end apart: 20, of which 8 were waited for; matrix products, arithmetic and copies ran while one was open for 0% of the time, Pallas kernels for 13%

profile of v2, /device:TPU:1, one launch (start us, length us, event | category | flops | bytes accessed | tf_op | source)
XLA Modules:
  0.0 145.0 jit_solution(11830052551424500197)
XLA Ops:
  3.8 5.2 %collective-permute-start.1 = (f32[16,256]{1,0:T(8,128)S(1)}, f32[16,256]{1,0:T(8,128)S(1)}, u32[]{:S(2)}, u32[]{:S(2)}) collective-permute-start(f32[16,256]{1,0:T(8,128)S(1)} %get-tuple-element.33), channel_id=1, source_target_pairs={{32,0},{64,32},{96,64},{128,96},{160,128},{192,160},{224,192},{33,... | collective-permute-start | bytes 49160 | tf_op jit(solution)/shard_map/ppermute | solution.py:316
  9.0 1.9 %collective-permute-start = (f32[8,256]{1,0:T(8,128)S(1)}, f32[8,256]{1,0:T(8,128)S(1)}, u32[]{:S(2)}, u32[]{:S(2)}) collective-permute-start(f32[8,256]{1,0:T(8,128)S(1)} %get-tuple-element.32), channel_id=1, source_target_pairs={{0,32},{32,64},{64,96},{96,128},{128,160},{160,192},{192,224},{1,3... | collective-permute-start | bytes 24584 | tf_op jit(solution)/shard_map/ppermute | solution.py:315
  10.9 1.3 collective-permute-start.3
  12.3 4.1 %collective-permute-start.2 = (f32[8,128]{1,0:T(8,128)S(1)}, f32[8,128]{1,0:T(8,128)S(1)}, u32[]{:S(2)}, u32[]{:S(2)}) collective-permute-start(f32[8,128]{1,0:T(8,128)S(1)} %get-tuple-element.34), channel_id=1, source_target_pairs={{0,1},{1,2},{2,3},{3,4},{4,5},{5,6},{6,7},{7,8},{8,9},{9,10},{10,1... | collective-permute-start | bytes 12296 | tf_op jit(solution)/shard_map/ppermute | solution.py:317
  17.2 1.4 shard_map.168
  20.8 1.6 %collective-permute-start.6 = (f32[128,256]{1,0:T(8,128)S(1)}, f32[128,256]{1,0:T(8,128)S(1)}, u32[]{:S(2)}, u32[]{:S(2)}) collective-permute-start(f32[128,256]{1,0:T(8,128)S(1)} %get-tuple-element.40), channel_id=1, source_target_pairs={{0,96},{32,128},{64,160},{96,192},{128,224},{160,0},{192,32},{224,... | collective-permute-start | bytes 393224 | tf_op jit(solution)/shard_map/ppermute | solution.py:303
  22.4 1.6 %collective-permute-start.7 = (f32[128,256]{1,0:T(8,128)S(1)}, f32[128,256]{1,0:T(8,128)S(1)}, u32[]{:S(2)}, u32[]{:S(2)}) collective-permute-start(f32[128,256]{1,0:T(8,128)S(1)} %get-tuple-element.41), channel_id=1, source_target_pairs={{0,128},{32,160},{64,192},{96,224},{128,0},{160,32},{192,64},{224,... | collective-permute-start | bytes 393224 | tf_op jit(solution)/shard_map/ppermute | solution.py:303
  24.0 2.6 %collective-permute-start.8 = (f32[128,256]{1,0:T(8,128)S(1)}, f32[128,256]{1,0:T(8,128)S(1)}, u32[]{:S(2)}, u32[]{:S(2)}) collective-permute-start(f32[128,256]{1,0:T(8,128)S(1)} %get-tuple-element.42), channel_id=1, source_target_pairs={{0,160},{32,192},{64,224},{96,0},{128,32},{160,64},{192,96},{224,1... | collective-permute-start | bytes 393224 | tf_op jit(solution)/shard_map/ppermute | solution.py:303
  26.6 7.7 %collective-permute-done.5.refs_2_ = f32[128,256]{1,0:T(8,128)S(1)} collective-permute-done((f32[128,256]{1,0:T(8,128)S(1)}, f32[128,256]{1,0:T(8,128)S(1)}, u32[]{:S(2)}, u32[]{:S(2)}) %collective-permute-start.5) | collective-permute-done | bytes 131104 | tf_op jit(solution)/shard_map/ppermute | solution.py:303
  35.1 3.6 %collective-permute-done.10.refs_7_ = f32[128,256]{1,0:T(8,128)S(1)} collective-permute-done((f32[128,256]{1,0:T(8,128)S(1)}, f32[128,256]{1,0:T(8,128)S(1)}, u32[]{:S(2)}, u32[]{:S(2)}) %collective-permute-start.10) | collective-permute-done | bytes 131104 | tf_op jit(solution)/shard_map/ppermute | solution.py:303
  38.8 4.1 %shard_map.169 = f32[256,1,768]{2,1,0:T(1,128)} custom-call(f32[128,256]{1,0:T(8,128)S(1)} %get-tuple-element.37.refs_0_, f32[128,256]{1,0:T(8,128)S(1)} %collective-permute-done.4.refs_1_, f32[128,256]{1,0:T(8,128)S(1)} %collective-permute-done.5.refs_2_, f32[128,256]{1,0:T(8,128)S(1)} %collective-permute-done.6.refs_3_, ...), custom_call_target="tpu_custom_call" | custom-call | flops 1610612736 | bytes 2899968 | tf_op jit(solution)/shard_map/pallas_call | solution.py:84
  42.8 13.6 %all-to-all-start = ((f32[256,1,768]{2,1,0:T(1,128)}), f32[256,1,768]{2,1,0:T(1,128)S(1)}, u32[]{:S(2)}, u32[]{:S(2)}) async-start(f32[256,1,768]{2,1,0:T(1,128)} %shard_map.169), calls=%async_computation | async-start | bytes 1572864 | tf_op jit(solution)/shard_map/all_to_all | solution.py:67
  56.6 25.4 %all-to-all-done = f32[256,1,768]{2,1,0:T(1,128)S(1)} async-done(((f32[256,1,768]{2,1,0:T(1,128)}), f32[256,1,768]{2,1,0:T(1,128)S(1)}, u32[]{:S(2)}, u32[]{:S(2)}) %all-to-all-start) | async-done | bytes 786464 | tf_op jit(solution)/shard_map/all_to_all | solution.py:67
  82.7 2.3 %shard_map.170 = f32[256,1,512]{2,1,0:T(1,128)} custom-call(f32[256,768]{1,0:T(8,128)S(1)} %bitcast.21, f32[2,4,4,32,128]{4,3,2,1,0:T(8,128)S(1)} %copy-done.2, f32[2,8,32,128]{3,2,1,0:T(8,128)S(1)} %bitcast.25, f32[8,128]{1,0:T(8,128)S(1)} %copy-done.3, f32[8,128]{1,0:T(8,128)S(1)} %bitcast.27), custom_call_target="tpu_custom_call" | custom-call | flops 12582912 | bytes 2105344 | tf_op jit(solution)/shard_map/pallas_call | solution.py:84
  85.0 7.3 %all-to-all-start.1 = ((f32[256,1,512]{2,1,0:T(1,128)}), f32[256,1,512]{2,1,0:T(1,128)}, u32[]{:S(2)}, u32[]{:S(2)}) async-start(f32[256,1,512]{2,1,0:T(1,128)} %shard_map.170), calls=%async_computation.1 | async-start | bytes 1048576 | tf_op jit(solution)/shard_map/all_to_all | solution.py:67
  93.2 8.5 %shard_map.171 = (f32[128,256]{1,0:T(8,128)S(1)}, f32[128,256]{1,0:T(8,128)S(1)}) custom-call(s32[112,128]{1,0:T(8,128)S(1)} %get-tuple-element.63.rows_ref, s32[112,128]{1,0:T(8,128)S(1)} %get-tuple-element.62.cols_ref, f32[112,128]{1,0:T(8,128)S(1)} %slice.40.weight_ref, f32[112,128]{1,0:T(8,128)S(1)} %slice.41.height_ref), custom_call_target="tpu_custom_call" | custom-call | flops 5637144576 | bytes 229376 | tf_op jit(solution)/shard_map/pallas_call | solution.py:381
  101.8 9.8 %all-to-all-done.1 = f32[256,1,512]{2,1,0:T(1,128)} async-done(((f32[256,1,512]{2,1,0:T(1,128)}), f32[256,1,512]{2,1,0:T(1,128)}, u32[]{:S(2)}, u32[]{:S(2)}) %all-to-all-start.1) | async-done | bytes 524320 | tf_op jit(solution)/shard_map/all_to_all | solution.py:67
  112.7 4.7 %shard_map.172 = (f32[128,256]{1,0:T(8,128)S(1)}, f32[128,256]{1,0:T(8,128)S(1)}, f32[128,256]{1,0:T(8,128)S(1)}, f32[128,256]{1,0:T(8,128)S(1)}, f32[128,256]{1...) custom-call(f32[256,512]{1,0:T(8,128)S(1)} %bitcast.26, ...), custom_call_target="tpu_custom_call" | custom-call | flops 2415919104 | bytes 2621440 | tf_op jit(solution)/shard_map/pallas_call | solution.py:84
  117.4 1.2 collective-permute-start.11
  119.6 1.3 collective-permute-start.13
  120.9 1.9 %collective-permute-start.14 = (f32[128,256]{1,0:T(8,128)S(1)}, f32[128,256]{1,0:T(8,128)S(1)}, u32[]{:S(2)}, u32[]{:S(2)}) collective-permute-start(f32[128,256]{1,0:T(8,128)S(1)} %get-tuple-element.52), channel_id=1, source_target_pairs={{0,128},{32,160},{64,192},{96,224},{128,0},{160,32},{192,64},{224,... | collective-permute-start | bytes 393224 | tf_op jit(solution)/shard_map/ppermute | solution.py:303
  122.7 2.5 %collective-permute-start.15 = (f32[128,256]{1,0:T(8,128)S(1)}, f32[128,256]{1,0:T(8,128)S(1)}, u32[]{:S(2)}, u32[]{:S(2)}) collective-permute-start(f32[128,256]{1,0:T(8,128)S(1)} %get-tuple-element.53), channel_id=1, source_target_pairs={{0,160},{32,192},{64,224},{96,0},{128,32},{160,64},{192,96},{224,1... | collective-permute-start | bytes 393224 | tf_op jit(solution)/shard_map/ppermute | solution.py:303
  125.3 7.6 %collective-permute-done.12.refs_3_ = f32[128,256]{1,0:T(8,128)S(1)} collective-permute-done((f32[128,256]{1,0:T(8,128)S(1)}, f32[128,256]{1,0:T(8,128)S(1)}, u32[]{:S(2)}, u32[]{:S(2)}) %collective-permute-start.12) | collective-permute-done | bytes 131104 | tf_op jit(solution)/shard_map/ppermute | solution.py:303
  132.9 10.9 %shard_map.173 = (f32[128,256]{1,0:T(8,128)S(1)}, f32[128,256]{1,0:T(8,128)S(1)}) custom-call(s32[144,128]{1,0:T(8,128)S(1)} %get-tuple-element.65.rows_ref, s32[144,128]{1,0:T(8,128)S(1)} %get-tuple-element.64.cols_ref, f32[144,128]{1,0:T(8,128)S(1)} %slice.37.weight_ref, f32[144,128]{1,0:T(8,128)S(1)} %slice.42.height_ref), custom_call_target="tpu_custom_call" | custom-call | flops 7247757312 | bytes 294912 | tf_op jit(solution)/shard_map/pallas_call | solution.py:381
  (66 shorter events, 11.7 us)
Async XLA Ops:
  3.8 13.3 %collective-permute-start.1 = (f32[16,256]{1,0:T(8,128)S(1)}, f32[16,256]{1,0:T(8,128)S(1)}, u32[]{:S(2)}, u32[]{:S(2)}) collective-permute-start(f32[16,256]{1,0:T(8,128)S(1)} %get-tuple-element.33), channel_id=1, source_target_pairs={{32,0},{64,32},{96,64},{128,96},{160,128},{192,160},{224,192},{33,... | collective-permute-start | bytes 49160 | tf_op jit(solution)/shard_map/ppermute | solution.py:316
  9.0 8.1 %collective-permute-start = (f32[8,256]{1,0:T(8,128)S(1)}, f32[8,256]{1,0:T(8,128)S(1)}, u32[]{:S(2)}, u32[]{:S(2)}) collective-permute-start(f32[8,256]{1,0:T(8,128)S(1)} %get-tuple-element.32), channel_id=1, source_target_pairs={{0,32},{32,64},{64,96},{96,128},{128,160},{160,192},{192,224},{1,3... | collective-permute-start | bytes 24584 | tf_op jit(solution)/shard_map/ppermute | solution.py:315
  10.9 6.2 %collective-permute-start.3 = (f32[16,128]{1,0:T(8,128)S(1)}, f32[16,128]{1,0:T(8,128)S(1)}, u32[]{:S(2)}, u32[]{:S(2)}) collective-permute-start(f32[16,128]{1,0:T(8,128)S(1)} %get-tuple-element.35), channel_id=1, source_target_pairs={{1,0},{2,1},{3,2},{4,3},{5,4},{6,5},{7,6},{8,7},{9,8},{10,9},{11,1... | collective-permute-start | bytes 24584 | tf_op jit(solution)/shard_map/ppermute | solution.py:318
  12.2 26.5 %copy-start.5 = (f32[1,256,128]{2,1,0:T(8,128)S(1)}, f32[1,256,128]{2,1,0:T(8,128)}, u32[]{:S(2)}) copy-start(f32[1,256,128]{2,1,0:T(8,128)} %param.21) | copy-start | bytes 393220
  12.2 26.5 %copy-start.6 = (f32[1,256,128]{2,1,0:T(8,128)S(1)}, f32[1,256,128]{2,1,0:T(8,128)}, u32[]{:S(2)}) copy-start(f32[1,256,128]{2,1,0:T(8,128)} %param.22) | copy-start | bytes 393220
  12.3 26.5 %copy-start.9 = (f32[512,256]{1,0:T(8,128)S(1)}, f32[512,256]{1,0:T(8,128)}, u32[]{:S(2)}) copy-start(f32[512,256]{1,0:T(8,128)} %constant.16.clone.refs_10_) | copy-start | bytes 1572868
  12.3 26.5 %copy-start.10 = (f32[256,256]{1,0:T(8,128)S(1)}, f32[256,256]{1,0:T(8,128)}, u32[]{:S(2)}) copy-start(f32[256,256]{1,0:T(8,128)} %constant.14.clone.refs_8_) | copy-start | bytes 786436
  12.3 4.9 %collective-permute-start.2 = (f32[8,128]{1,0:T(8,128)S(1)}, f32[8,128]{1,0:T(8,128)S(1)}, u32[]{:S(2)}, u32[]{:S(2)}) collective-permute-start(f32[8,128]{1,0:T(8,128)S(1)} %get-tuple-element.34), channel_id=1, source_target_pairs={{0,1},{1,2},{2,3},{3,4},{4,5},{5,6},{6,7},{7,8},{8,9},{9,10},{10,1... | collective-permute-start | bytes 12296 | tf_op jit(solution)/shard_map/ppermute | solution.py:317
  18.6 8.0 %collective-permute-start.4 = (f32[128,256]{1,0:T(8,128)S(1)}, f32[128,256]{1,0:T(8,128)S(1)}, u32[]{:S(2)}, u32[]{:S(2)}) collective-permute-start(f32[128,256]{1,0:T(8,128)S(1)} %get-tuple-element.38), channel_id=1, source_target_pairs={{0,32},{32,64},{64,96},{96,128},{128,160},{160,192},{192,224},{224... | collective-permute-start | bytes 393224 | tf_op jit(solution)/shard_map/ppermute | solution.py:303
  19.6 14.8 %collective-permute-start.5 = (f32[128,256]{1,0:T(8,128)S(1)}, f32[128,256]{1,0:T(8,128)S(1)}, u32[]{:S(2)}, u32[]{:S(2)}) collective-permute-start(f32[128,256]{1,0:T(8,128)S(1)} %get-tuple-element.39), channel_id=1, source_target_pairs={{0,64},{32,96},{64,128},{96,160},{128,192},{160,224},{192,0},{224,... | collective-permute-start | bytes 393224 | tf_op jit(solution)/shard_map/ppermute | solution.py:303
  20.8 14.2 %collective-permute-start.6 = (f32[128,256]{1,0:T(8,128)S(1)}, f32[128,256]{1,0:T(8,128)S(1)}, u32[]{:S(2)}, u32[]{:S(2)}) collective-permute-start(f32[128,256]{1,0:T(8,128)S(1)} %get-tuple-element.40), channel_id=1, source_target_pairs={{0,96},{32,128},{64,160},{96,192},{128,224},{160,0},{192,32},{224,... | collective-permute-start | bytes 393224 | tf_op jit(solution)/shard_map/ppermute | solution.py:303
  22.4 12.6 %collective-permute-start.7 = (f32[128,256]{1,0:T(8,128)S(1)}, f32[128,256]{1,0:T(8,128)S(1)}, u32[]{:S(2)}, u32[]{:S(2)}) collective-permute-start(f32[128,256]{1,0:T(8,128)S(1)} %get-tuple-element.41), channel_id=1, source_target_pairs={{0,128},{32,160},{64,192},{96,224},{128,0},{160,32},{192,64},{224,... | collective-permute-start | bytes 393224 | tf_op jit(solution)/shard_map/ppermute | solution.py:303
  24.0 11.0 %collective-permute-start.8 = (f32[128,256]{1,0:T(8,128)S(1)}, f32[128,256]{1,0:T(8,128)S(1)}, u32[]{:S(2)}, u32[]{:S(2)}) collective-permute-start(f32[128,256]{1,0:T(8,128)S(1)} %get-tuple-element.42), channel_id=1, source_target_pairs={{0,160},{32,192},{64,224},{96,0},{128,32},{160,64},{192,96},{224,1... | collective-permute-start | bytes 393224 | tf_op jit(solution)/shard_map/ppermute | solution.py:303
  26.6 8.5 %collective-permute-start.9 = (f32[128,256]{1,0:T(8,128)S(1)}, f32[128,256]{1,0:T(8,128)S(1)}, u32[]{:S(2)}, u32[]{:S(2)}) collective-permute-start(f32[128,256]{1,0:T(8,128)S(1)} %get-tuple-element.43), channel_id=1, source_target_pairs={{0,192},{32,224},{64,0},{96,32},{128,64},{160,96},{192,128},{224,1... | collective-permute-start | bytes 393224 | tf_op jit(solution)/shard_map/ppermute | solution.py:303
  34.3 4.4 %collective-permute-start.10 = (f32[128,256]{1,0:T(8,128)S(1)}, f32[128,256]{1,0:T(8,128)S(1)}, u32[]{:S(2)}, u32[]{:S(2)}) collective-permute-start(f32[128,256]{1,0:T(8,128)S(1)} %get-tuple-element.44), channel_id=1, source_target_pairs={{0,224},{32,0},{64,32},{96,64},{128,96},{160,128},{192,160},{224,1... | collective-permute-start | bytes 393224 | tf_op jit(solution)/shard_map/ppermute | solution.py:303
  42.8 39.1 %all-to-all-start = ((f32[256,1,768]{2,1,0:T(1,128)}), f32[256,1,768]{2,1,0:T(1,128)S(1)}, u32[]{:S(2)}, u32[]{:S(2)}) async-start(f32[256,1,768]{2,1,0:T(1,128)} %shard_map.169), calls=%async_computation | async-start | bytes 1572864 | tf_op jit(solution)/shard_map/all_to_all | solution.py:67
  85.0 26.5 %all-to-all-start.1 = ((f32[256,1,512]{2,1,0:T(1,128)}), f32[256,1,512]{2,1,0:T(1,128)}, u32[]{:S(2)}, u32[]{:S(2)}) async-start(f32[256,1,512]{2,1,0:T(1,128)} %shard_map.170), calls=%async_computation.1 | async-start | bytes 1048576 | tf_op jit(solution)/shard_map/all_to_all | solution.py:67
  117.4 7.9 %collective-permute-start.11 = (f32[128,256]{1,0:T(8,128)S(1)}, f32[128,256]{1,0:T(8,128)S(1)}, u32[]{:S(2)}, u32[]{:S(2)}) collective-permute-start(f32[128,256]{1,0:T(8,128)S(1)} %get-tuple-element.49), channel_id=1, source_target_pairs={{0,32},{32,64},{64,96},{96,128},{128,160},{160,192},{192,224},{224... | collective-permute-start | bytes 393224 | tf_op jit(solution)/shard_map/ppermute | solution.py:303
  118.6 14.3 %collective-permute-start.12 = (f32[128,256]{1,0:T(8,128)S(1)}, f32[128,256]{1,0:T(8,128)S(1)}, u32[]{:S(2)}, u32[]{:S(2)}) collective-permute-start(f32[128,256]{1,0:T(8,128)S(1)} %get-tuple-element.50), channel_id=1, source_target_pairs={{0,64},{32,96},{64,128},{96,160},{128,192},{160,224},{192,0},{224,... | collective-permute-start | bytes 393224 | tf_op jit(solution)/shard_map/ppermute | solution.py:303
  119.6 24.3 %collective-permute-start.13 = (f32[128,256]{1,0:T(8,128)S(1)}, f32[128,256]{1,0:T(8,128)S(1)}, u32[]{:S(2)}, u32[]{:S(2)}) collective-permute-start(f32[128,256]{1,0:T(8,128)S(1)} %get-tuple-element.51), channel_id=1, source_target_pairs={{0,96},{32,128},{64,160},{96,192},{128,224},{160,0},{192,32},{224,... | collective-permute-start | bytes 393224 | tf_op jit(solution)/shard_map/ppermute | solution.py:303
  120.9 23.0 %collective-permute-start.14 = (f32[128,256]{1,0:T(8,128)S(1)}, f32[128,256]{1,0:T(8,128)S(1)}, u32[]{:S(2)}, u32[]{:S(2)}) collective-permute-start(f32[128,256]{1,0:T(8,128)S(1)} %get-tuple-element.52), channel_id=1, source_target_pairs={{0,128},{32,160},{64,192},{96,224},{128,0},{160,32},{192,64},{224,... | collective-permute-start | bytes 393224 | tf_op jit(solution)/shard_map/ppermute | solution.py:303
  122.7 21.1 %collective-permute-start.15 = (f32[128,256]{1,0:T(8,128)S(1)}, f32[128,256]{1,0:T(8,128)S(1)}, u32[]{:S(2)}, u32[]{:S(2)}) collective-permute-start(f32[128,256]{1,0:T(8,128)S(1)} %get-tuple-element.53), channel_id=1, source_target_pairs={{0,160},{32,192},{64,224},{96,0},{128,32},{160,64},{192,96},{224,1... | collective-permute-start | bytes 393224 | tf_op jit(solution)/shard_map/ppermute | solution.py:303
  125.3 18.6 %collective-permute-start.16 = (f32[128,256]{1,0:T(8,128)S(1)}, f32[128,256]{1,0:T(8,128)S(1)}, u32[]{:S(2)}, u32[]{:S(2)}) collective-permute-start(f32[128,256]{1,0:T(8,128)S(1)} %get-tuple-element.54), channel_id=1, source_target_pairs={{0,192},{32,224},{64,0},{96,32},{128,64},{160,96},{192,128},{224,1... | collective-permute-start | bytes 393224 | tf_op jit(solution)/shard_map/ppermute | solution.py:303
  132.9 11.0 %collective-permute-start.17 = (f32[128,256]{1,0:T(8,128)S(1)}, f32[128,256]{1,0:T(8,128)S(1)}, u32[]{:S(2)}, u32[]{:S(2)}) collective-permute-start(f32[128,256]{1,0:T(8,128)S(1)} %get-tuple-element.55), channel_id=1, source_target_pairs={{0,224},{32,0},{64,32},{96,64},{128,96},{160,128},{192,160},{224,1... | collective-permute-start | bytes 393224 | tf_op jit(solution)/shard_map/ppermute | solution.py:303
  (12 other events, 100.0 us)

commit v3 on v2

--- a/solution.py
+++ b/solution.py
@@ -53,12 +53,18 @@
                 turn[0, quarter, low, :, :, high] = np.cos(ang)[:, None, None]
                 turn[1, quarter, low, :, :, high] = np.sin(ang)[:, None, None]
     turn = turn.reshape(2, 4, 4, GY, 128)
-    return tuple(
-        array.astype(np.float32) for array in (fore_x, back_x, period, fore_y, back_y, turn)
-    )
-
-
-FORE_X, BACK_X, PERIOD, FORE_Y, BACK_Y, TURN = tables()
+    def pair(array):
+        high = array.astype(np.float32).astype(jnp.bfloat16)
+        return high, (array - high.astype(np.float64)).astype(np.float32).astype(jnp.bfloat16)
+
+    return (
+        *map(pair, (fore_x, back_x, fore_y, back_y)),
+        period.astype(np.float32),
+        turn.astype(np.float32),
+    )
+
+
+FORE_X, BACK_X, FORE_Y, BACK_Y, PERIOD, TURN = tables()
 SCALE_IN = 1.0 / math.sqrt(NX * NY)
 SCALE_OUT = 1.0 / math.sqrt(MX * MY)
 
@@ -73,87 +79,116 @@
     )
 
 
+def split_dot(table, b, contract=((1,), (0,))):
+    table_high, table_low = table
+    b_high = b.astype(jnp.bfloat16)
+    b_low = (b - b_high.astype(jnp.float32)).astype(jnp.bfloat16)
+
+    def one(left, right):
+        return lax.dot_general(
+            left, right, (contract, ((), ())), preferred_element_type=jnp.float32
+        )
+
+    return one(table_high, b_high) + (one(table_high, b_low) + one(table_low, b_high))
+
+
 def shape(*dims):
     return jax.ShapeDtypeStruct(dims, jnp.float32)
 
 
-def local_kernel(kernel, out_shape, operands, scalars=(), flops=0, scratch=()):
+def local_kernel(kernel, out_shape, operands, flops=0, scratch=(), in_place=False, limit=24):
     vmem = pl.BlockSpec(memory_space=pltpu.VMEM)
-    smem = pl.BlockSpec(memory_space=pltpu.SMEM)
+    place = pl.BlockSpec(memory_space=pl.ANY) if in_place else vmem
     size = sum(4 * math.prod(a.shape) for a in (*operands, *out_shape))
     return pl.pallas_call(
         kernel,
-        in_specs=[smem] * len(scalars) + [vmem] * len(operands),
+        in_specs=[place] * len(operands),
         out_specs=[vmem] * len(out_shape),
         out_shape=out_shape,
         scratch_shapes=scratch,
-        compiler_params=pltpu.CompilerParams(vmem_limit_bytes=24 * 1024 * 1024),
+        compiler_params=pltpu.CompilerParams(vmem_limit_bytes=limit * 1024 * 1024),
         cost_estimate=pl.CostEstimate(flops=flops, bytes_accessed=size, transcendentals=0),
-    )(*scalars, *operands)
-
-
-def edge_kernel(fields_ref, velocity_ref, last_x_ref, first_x_ref, last_y_ref, first_y_ref):
+    )(*operands)
+
+
+def face(speed):
+    return (
+        time_step * (jnp.maximum(speed, 0.0) + diffusion),
+        time_step * (jnp.minimum(speed, 0.0) - diffusion),
+    )
+
+
+def step_kernel(fields_hbm, velocity_hbm, *refs):
+    out_ref, last_x_ref, first_x_ref, last_y_ref, first_y_ref = refs[:5]
+    block_refs = refs[5:-3]
+    fields_ref, velocity_ref, sems = refs[-3:]
+    copies = [pltpu.make_async_copy(velocity_hbm, velocity_ref, sems.at[F])]
+    copies += [
+        pltpu.make_async_copy(fields_hbm.at[f], fields_ref.at[f], sems.at[f]) for f in range(F)
+    ]
+    for copy in copies:
+        copy.start()
+    row = lax.broadcasted_iota(jnp.int32, (CX, CY), 0)
+    col = lax.broadcasted_iota(jnp.int32, (CX, CY), 1)
+    pick_row = lax.broadcasted_iota(jnp.int32, (8, CY), 0)
+    pick_col = lax.broadcasted_iota(jnp.int32, (8, CY), 1)
+    pick = jnp.where(pick_col == pick_row * (CY - 1), 1.0, 0.0).astype(jnp.float32)
     first_x_ref[...] = jnp.zeros((16, CY), jnp.float32)
     first_y_ref[...] = jnp.zeros((16, CX), jnp.float32)
-    row = lax.broadcasted_iota(jnp.int32, (8, CY), 0)
-    col = lax.broadcasted_iota(jnp.int32, (8, CY), 1)
-    pick = jnp.where(
-        ((row == 0) & (col == 0)) | ((row == 1) & (col == CY - 1)), 1.0, 0.0
-    ).astype(jnp.float32)
+    copies[0].wait()
+    first_x_ref[F : F + 1] = velocity_ref[0, 0:1]
+    first_y_ref[F : F + 1] = dot(pick, velocity_ref[1], ((1,), (1,)))[0:1]
+    low_w, high_w = (jnp.where(row == 0, 0.0, value) for value in face(velocity_ref[0]))
+    low_e, high_e = (
+        jnp.where(row == CX - 1, 0.0, pltpu.roll(value, CX - 1, 0)) for value in (low_w, high_w)
+    )
+    low_s, high_s = (jnp.where(col == 0, 0.0, value) for value in face(velocity_ref[1]))
+    low_n, high_n = (
+        jnp.where(col == CY - 1, 0.0, pltpu.roll(value, CY - 1, 1)) for value in (low_s, high_s)
+    )
+    own = 1.0 - low_e + high_w - low_n + high_s
     for f in range(F):
+        copies[f + 1].wait()
         block = fields_ref[f]
-        last_x_ref[f : f + 1] = block[CX - 1 : CX]
-        first_x_ref[f : f + 1] = block[0:1]
         ends = dot(pick, block, ((1,), (1,)))
         first_y_ref[f : f + 1] = ends[0:1]
         last_y_ref[f : f + 1] = ends[1:2]
-    first_x_ref[F : F + 1] = velocity_ref[0, 0:1]
-    first_y_ref[F : F + 1] = dot(pick, velocity_ref[1], ((1,), (1,)))[0:1]
-
-
-def step_kernel(
-    fields_ref, velocity_ref, west_ref, east_ref, south_ref, north_ref, out_ref, *block_refs
-):
-    row = lax.broadcasted_iota(jnp.int32, (CX, CY), 0)
-    col = lax.broadcasted_iota(jnp.int32, (CX, CY), 1)
-    first_row, last_row = row == 0, row == CX - 1
-    first_col, last_col = col == 0, col == CY - 1
-    gx, gy = lax.axis_index("gx"), lax.axis_index("gy")
-    is_open = [
-        jnp.where(test, 1.0, 0.0) for test in (gx > 0, gx < GX - 1, gy > 0, gy < GY - 1)
-    ]
-    before = jnp.transpose(south_ref[...])
-    after = jnp.transpose(north_ref[...])
-    speed = velocity_ref[0]
-    shut = jnp.where(first_row, is_open[0], 1.0)
-    low_w = time_step * shut * (jnp.maximum(speed, 0.0) + diffusion)
-    high_w = time_step * shut * (jnp.minimum(speed, 0.0) - diffusion)
-    edge = east_ref[F : F + 1]
-    low_edge = time_step * is_open[1] * (jnp.maximum(edge, 0.0) + diffusion)
-    high_edge = time_step * is_open[1] * (jnp.minimum(edge, 0.0) - diffusion)
-    low_e = jnp.where(last_row, low_edge, pltpu.roll(low_w, CX - 1, 0))
-    high_e = jnp.where(last_row, high_edge, pltpu.roll(high_w, CX - 1, 0))
-    speed = velocity_ref[1]
-    shut = jnp.where(first_col, is_open[2], 1.0)
-    low_s = time_step * shut * (jnp.maximum(speed, 0.0) + diffusion)
-    high_s = time_step * shut * (jnp.minimum(speed, 0.0) - diffusion)
-    edge = after[:, F : F + 1]
-    low_edge = time_step * is_open[3] * (jnp.maximum(edge, 0.0) + diffusion)
-    high_edge = time_step * is_open[3] * (jnp.minimum(edge, 0.0) - diffusion)
-    low_n = jnp.where(last_col, low_edge, pltpu.roll(low_s, CY - 1, 1))
-    high_n = jnp.where(last_col, high_edge, pltpu.roll(high_s, CY - 1, 1))
-    own = 1.0 - low_e + high_w - low_n + high_s
-    for f in range(F):
-        block = fields_ref[f]
-        west = jnp.where(first_row, west_ref[f : f + 1], pltpu.roll(block, 1, 0))
-        east = jnp.where(last_row, east_ref[f : f + 1], pltpu.roll(block, CX - 1, 0))
-        south = jnp.where(first_col, before[:, f : f + 1], pltpu.roll(block, 1, 1))
-        north = jnp.where(last_col, after[:, f : f + 1], pltpu.roll(block, CY - 1, 1))
+        last_x_ref[f : f + 1] = block[CX - 1 : CX]
+        first_x_ref[f : f + 1] = block[0:1]
         out_ref[f] = (
-            own * block + low_w * west - high_e * east + low_s * south - high_n * north
+            own * block
+            + low_w * pltpu.roll(block, 1, 0)
+            - high_e * pltpu.roll(block, CX - 1, 0)
+            + low_s * pltpu.roll(block, 1, 1)
+            - high_n * pltpu.roll(block, CY - 1, 1)
         )
     for k, ref in enumerate(block_refs):
-        ref[...] = out_ref[lax.rem(lax.axis_index("gx") + k, GX)]
+        f = lax.rem(lax.axis_index("gx") + k, GX)
+        ref[0:CX] = out_ref[f]
+        ref[CX : CX + 1] = fields_ref[f, 0:1]
+        ref[CX + 1 : CX + 2] = fields_ref[f, CX - 1 : CX]
+        ref[CX + 2 : CX + 3] = velocity_ref[0, 0:1]
+        ref[CX + 3 :] = jnp.zeros((5, CY), jnp.float32)
+
+
+def side_kernel(first_ref, last_ref, south_ref, north_ref, out_ref):
+    gy = lax.axis_index("gy")
+    first, second = face(first_ref[F : F + 1])
+    low = (first * south_ref[...] + second * first_ref[0:F]) * jnp.where(gy > 0, 1.0, 0.0)
+    first, second = face(north_ref[F : F + 1])
+    high = (first * last_ref[...] + second * north_ref[0:F]) * jnp.where(gy < GY - 1, 1.0, 0.0)
+    for f in range(F):
+        out_ref[f, 0:1] = low[f : f + 1]
+        out_ref[f, 1:2] = -high[f : f + 1]
+        out_ref[f, 2:] = jnp.zeros((6, CX), jnp.float32)
+
+
+def add_sides(block, sides):
+    sides = jnp.transpose(sides)
+    col = lax.broadcasted_iota(jnp.int32, (CX, CY), 1)
+    return block + jnp.where(
+        col == 0, sides[:, 0:1], jnp.where(col == CY - 1, sides[:, 1:2], 0.0)
+    )
 
 
 def quarter_turn(index, t):
@@ -164,16 +199,26 @@
 
 
 def forward_kernel(*refs):
-    *block_refs, fore_x_ref, period_ref, fore_y_ref, height_ref, weight_ref = refs[:-3]
-    out_ref, columns_ref, parts_ref = refs[-3:]
+    *block_refs, sides_ref, fore_xh, fore_xl, period_ref, fore_yh, fore_yl, height_ref, weight_ref = (
+        refs[:-4]
+    )
+    out_ref, columns_ref, parts_ref, edges_ref = refs[-4:]
     for k, ref in enumerate(block_refs):
         source = lax.rem(lax.axis_index("gx") + (GX - k), GX)
-        columns_ref[pl.ds(pl.multiple_of(source * CX, CX), CX), :] = ref[...]
+        columns_ref[pl.ds(pl.multiple_of(source * CX, CX), CX), :] = add_sides(
+            ref[0:CX], sides_ref[source]
+        )
+        edges_ref[source] = ref[CX:]
+    for t in range(1, GX):
+        first, second = face(edges_ref[t, 2:3])
+        flux = first * edges_ref[t - 1, 1:2] + second * edges_ref[t, 0:1]
+        columns_ref[t * CX - 1 : t * CX] -= flux
+        columns_ref[t * CX : t * CX + 1] += flux
     q = lax.broadcasted_iota(jnp.int32, (HALF, CY), 0)
     real = jnp.zeros((HALF, CY), jnp.float32)
     imag = jnp.zeros((HALF, CY), jnp.float32)
     for t in range(4):
-        piece = dot(fore_x_ref[...], columns_ref[t * MX : (t + 1) * MX])
+        piece = split_dot((fore_xh[...], fore_xl[...]), columns_ref[t * MX : (t + 1) * MX])
         piece_r, piece_i = piece[:HALF], piece[HALF:]
         if t == 0:
             real, imag = piece_r, piece_i
@@ -191,7 +236,7 @@
     parts_ref[HALF:MX] = jnp.where(q == 0, last_r, dot(mirror, real))
     parts_ref[MX : MX + HALF] = imag
     parts_ref[MX + HALF :] = -jnp.where(q == 0, last_i, dot(mirror, imag))
-    mixed = dot(fore_y_ref[...], parts_ref[...], ((1,), (1,)))
+    mixed = split_dot((fore_yh[...], fore_yl[...]), parts_ref[...], ((1,), (1,)))
     modes = (mixed[:MY, :MX] + mixed[MY:, MX:], mixed[:MY, MX:] - mixed[MY:, :MX])
     group = lax.broadcasted_iota(jnp.int32, (GY, 128), 1) // 32
     for low in range(4):
@@ -224,7 +269,7 @@
         sine = turn_ref[1, quarter, low]
         straight, crossed = [], []
         for f in range(F):
-            block = got_ref[f * GY : (f + 1) * GY, low * 128 : (low + 1) * 128]
+            block = got_ref[f * GY : (f + 1) * GY, 0, low * 128 : (low + 1) * 128]
             straight.append(jnp.sum(block * cosine, axis=0, keepdims=True))
             crossed.append(jnp.sum(block * sine, axis=0, keepdims=True))
         crossed = pltpu.roll(jnp.concatenate(crossed, axis=0), 64, 1)
@@ -251,13 +296,13 @@
             )
 
 
-def backward_kernel(got_ref, back_y_ref, back_x_ref, *refs):
+def backward_kernel(got_ref, back_yh, back_yl, back_xh, back_xl, *refs):
     *out_refs, modes_ref, field_ref = refs
     group = lax.broadcasted_iota(jnp.int32, (GY, 128), 1) // 32
     for low in range(4):
         for half in range(2):
             tiles = [
-                got_ref[gx * GY : (gx + 1) * GY, low * 128 : (low + 1) * 128]
+                got_ref[gx * GY : (gx + 1) * GY, 0, low * 128 : (low + 1) * 128]
                 for gx in range(4 * half, 4 * half + 4)
             ]
             for part in range(2):
@@ -271,7 +316,7 @@
                     lanes = part * MX + half * 128
                     start = high * 128 + low * 32
                     modes_ref[start : start + 32, lanes : lanes + 128] = value
-    mixed = dot(back_y_ref[...], modes_ref[...])
+    mixed = split_dot((back_yh[...], back_yl[...]), modes_ref[...])
     real = mixed[:CY, :MX] - mixed[CY:, MX:]
     imag = mixed[:CY, MX:] + mixed[CY:, :MX]
     index = lax.broadcasted_iota(jnp.int32, (CY, MX), 1)
@@ -283,17 +328,29 @@
             turned = jnp.concatenate(
                 (real * cosine - imag * sine, imag * cosine + real * sine), axis=1
             )
-        field_ref[t * MX : (t + 1) * MX] = dot(back_x_ref[...], turned, ((1,), (1,)))
+        field_ref[t * MX : (t + 1) * MX] = split_dot(
+            (back_xh[...], back_xl[...]), turned, ((1,), (1,))
+        )
     for k, ref in enumerate(out_refs):
         owner = lax.rem(lax.axis_index("gx") + k, GX)
         ref[...] = field_ref[pl.ds(pl.multiple_of(owner * CX, CX), CX), :]
 
 
 def finish_kernel(*refs):
-    stepped_ref, *block_refs, w_0, w_1, wh_0, wh_1, out_ref, gradient_ref = refs
+    stepped_ref, *block_refs, sides_ref, west_ref, east_ref, first_ref, last_ref = refs[:-6]
+    w_0, w_1, wh_0, wh_1 = refs[-6:-2]
+    out_ref, gradient_ref = refs[-2:]
+    gx = lax.axis_index("gx")
     for k, ref in enumerate(block_refs):
-        f = lax.rem(lax.axis_index("gx") + (GX - k), GX)
-        out_ref[f] = stepped_ref[f] + ref[...]
+        f = lax.rem(gx + (GX - k), GX)
+        out_ref[f] = add_sides(stepped_ref[f] + ref[...], sides_ref[f])
+    first, second = face(first_ref[F : F + 1])
+    left = (first * west_ref[...] + second * first_ref[0:F]) * jnp.where(gx > 0, 1.0, 0.0)
+    first, second = face(east_ref[F : F + 1])
+    right = (first * last_ref[...] + second * east_ref[0:F]) * jnp.where(gx < GX - 1, 1.0, 0.0)
+    for f in range(F):
+        out_ref[f, 0:1] += left[f : f + 1]
+        out_ref[f, CX - 1 : CX] -= right[f : f + 1]
     gradient_ref[...] = out_ref[0] * (w_0[...] + w_1[...]) - (wh_0[...] + wh_1[...])
 
 
@@ -304,34 +361,12 @@
     return [moved[k] for k in range(GX)]
 
 
-def advance(fields, velocity):
-    up_x = [(i, i + 1) for i in range(GX - 1)]
-    down_x = [(i + 1, i) for i in range(GX - 1)]
-    up_y = [(i, i + 1) for i in range(GY - 1)]
-    down_y = [(i + 1, i) for i in range(GY - 1)]
-    last_x, first_x, last_y, first_y = local_kernel(
-        edge_kernel, [shape(F, CY), shape(16, CY), shape(F, CX), shape(16, CX)], (fields, velocity)
-    )
-    west = lax.ppermute(last_x, "gx", up_x)
-    east = lax.ppermute(first_x, "gx", down_x)
-    south = lax.ppermute(last_y, "gy", up_y)
-    north = lax.ppermute(first_y, "gy", down_y)
-    stepped, *blocks = local_kernel(
-        step_kernel,
-        [shape(F, CX, CY)] + [shape(CX, CY)] * GX,
-        (fields, velocity, west, east, south, north),
-    )
-    return stepped, blocks
-
-
-CHUNK = 16
-CPTS = CHUNK * 128
-
-
-def scatter_kernel(rows_ref, cols_ref, weight_ref, height_ref, sum_w_ref, sum_wh_ref, a_ref, b_ref, acc_ref):
+def scatter_kernel(
+    rows_ref, cols_ref, live_ref, got_ref, sum_w_ref, sum_wh_ref, a_ref, b_ref, acc_ref
+):
     step = pl.program_id(0)
-    weight = weight_ref[...]
-    product = weight * height_ref[...]
+    weight = got_ref[:, 0, 640:] * live_ref[...]
+    product = weight * got_ref[:, 0, 512:640]
     pieces = []
     for value in (weight, product):
         for _ in range(3):
@@ -345,7 +380,7 @@
     zero = jnp.zeros((CX, 128), jnp.bfloat16)
     one_c = jnp.ones((CY, 128), jnp.bfloat16)
     zero_c = jnp.zeros((CY, 128), jnp.bfloat16)
-    for s in range(CHUNK):
+    for s in range(rows.shape[0]):
         lanes = pl.ds(s * 128, 128)
         hit = spot_r == jnp.broadcast_to(rows[s : s + 1], (CX, 128))
         for k, piece in enumerate(pieces):
@@ -374,28 +409,28 @@
         )
 
 
-def scatter(rows, cols, weight, height):
-    steps = rows.shape[0] // CHUNK
-    block = pl.BlockSpec((CHUNK, 128), lambda i: (i, 0))
+def scatter(rows, cols, live, got, start, stop, chunk):
+    steps = (stop - start) // chunk
+    block = pl.BlockSpec((chunk, 128), lambda i: (start // chunk + i, 0))
     whole = pl.BlockSpec((CX, CY), lambda i: (0, 0))
     return pl.pallas_call(
         scatter_kernel,
         grid=(steps,),
-        in_specs=[block] * 4,
+        in_specs=[block] * 3 + [pl.BlockSpec((chunk, 1, 768), lambda i: (start // chunk + i, 0, 0))],
         out_specs=[whole, whole],
-        out_shape=[jax.ShapeDtypeStruct((CX, CY), jnp.float32)] * 2,
+        out_shape=[shape(CX, CY)] * 2,
         scratch_shapes=[
-            pltpu.VMEM((6 * CX, CPTS), jnp.bfloat16),
-            pltpu.VMEM((CY, CPTS), jnp.bfloat16),
+            pltpu.VMEM((6 * CX, chunk * 128), jnp.bfloat16),
+            pltpu.VMEM((CY, chunk * 128), jnp.bfloat16),
             pltpu.VMEM((6 * CX, CY), jnp.float32),
         ],
-        compiler_params=pltpu.CompilerParams(vmem_limit_bytes=24 * 1024 * 1024),
+        compiler_params=pltpu.CompilerParams(vmem_limit_bytes=32 * 1024 * 1024),
         cost_estimate=pl.CostEstimate(
-            flops=2 * 6 * CX * CY * 128 * rows.shape[0],
-            bytes_accessed=4 * 128 * 4 * rows.shape[0],
+            flops=2 * 6 * CX * CY * 128 * (stop - start),
+            bytes_accessed=4 * 128 * 4 * (stop - start),
             transcendentals=0,
         ),
-    )(rows, cols, weight, height)
+    )(rows, cols, live, got)
 
 
 def body(
@@ -410,15 +445,50 @@
     cell_cols,
     counts,
 ):
-    stepped, blocks = advance(fields, velocity)
+    up_x = [(i, i + 1) for i in range(GX - 1)]
+    down_x = [(i + 1, i) for i in range(GX - 1)]
+    up_y = [(i, i + 1) for i in range(GY - 1)]
+    down_y = [(i + 1, i) for i in range(GY - 1)]
+    stepped, last_x, first_x, last_y, first_y, *blocks = local_kernel(
+        step_kernel,
+        [shape(F, CX, CY), shape(F, CY), shape(16, CY), shape(F, CX), shape(16, CX)]
+        + [shape(CX + 8, CY)] * GX,
+        (fields, velocity),
+        scratch=[
+            pltpu.VMEM((F, CX, CY), jnp.float32),
+            pltpu.VMEM((2, CX, CY), jnp.float32),
+            pltpu.SemaphoreType.DMA((F + 1,)),
+        ],
+        in_place=True,
+        limit=56,
+    )
+    south = lax.ppermute(last_y, "gy", up_y)
+    north = lax.ppermute(first_y, "gy", down_y)
+    blocks = exchange(blocks)
+    sides = local_kernel(side_kernel, [shape(F, 8, CX)], (first_y, last_y, south, north))[0]
+    all_sides = all_to_all(sides, "gx")
     sent = local_kernel(
         forward_kernel,
         [shape(DEV, 1, 768)],
-        (*exchange(blocks), *map(jnp.asarray, (FORE_X, PERIOD, FORE_Y)), obs_height[0], obs_weight[0]),
-        flops=6 * 2 * (256 * NX * CY + 512 * 256 * 512),
-        scratch=[pltpu.VMEM((NX, CY), jnp.float32), pltpu.VMEM((2 * MX, CY), jnp.float32)],
+        (
+            *blocks,
+            all_sides,
+            *map(jnp.asarray, (*FORE_X, PERIOD, *FORE_Y)),
+            obs_height[0],
+            obs_weight[0],
+        ),
+        flops=3 * 2 * (256 * NX * CY + 512 * 256 * 512),
+        scratch=[
+            pltpu.VMEM((NX, CY), jnp.float32),
+            pltpu.VMEM((2 * MX, CY), jnp.float32),
+            pltpu.VMEM((GX, 8, CY), jnp.float32),
+        ],
     )[0]
-    got = all_to_all(sent, ("gx", "gy")).reshape(DEV, 768)
+    sent, last_x, first_x = lax.optimization_barrier((sent, last_x, first_x))
+    west = lax.ppermute(last_x, "gx", up_x)
+    east = lax.ppermute(first_x, "gx", down_x)
+    got = all_to_all(sent, ("gx", "gy"))
+    got, west, east = lax.optimization_barrier((got, west, east))
     sent = local_kernel(
         mix_kernel,
         [shape(DEV, 1, 512)],
@@ -432,28 +502,38 @@
         flops=6 * 2 * 512 * 128 * 16,
     )[0]
 
-    live = jnp.arange(128, dtype=jnp.int32)[None, :] < counts[0][:, None]
-    weight = jnp.where(live, got[:, 640:], 0.0)
-    height = got[:, 512:640]
-    cut = 112
-    w_0, wh_0 = scatter(cell_rows[0, :cut], cell_cols[0, :cut], weight[:cut], height[:cut])
-
-    back = all_to_all(sent, ("gx", "gy")).reshape(DEV, 512)
+    live = (jnp.arange(128, dtype=jnp.int32)[None, :] < counts[0][:, None]).astype(jnp.float32)
+    points = (cell_rows[0], cell_cols[0], live)
+    w_0, wh_0 = scatter(*points, got, 0, 224, 56)
+
+    back = all_to_all(sent, ("gx", "gy"))
     back, w_0, wh_0 = lax.optimization_barrier((back, w_0, wh_0))
     blocks = local_kernel(
         backward_kernel,
         [shape(CX, CY)] * GX,
-        (back, jnp.asarray(BACK_Y), jnp.asarray(BACK_X)),
-        flops=6 * 2 * (512 * NX * CY + 512 * 256 * 512),
+        (back, *map(jnp.asarray, (*BACK_Y, *BACK_X))),
+        flops=3 * 2 * (512 * NX * CY + 512 * 256 * 512),
         scratch=[pltpu.VMEM((MY, 2 * MX), jnp.float32), pltpu.VMEM((NX, CY), jnp.float32)],
     )
-    weight, w_0 = lax.optimization_barrier((weight, w_0))
-    w_1, wh_1 = scatter(cell_rows[0, cut:], cell_cols[0, cut:], weight[cut:], height[cut:])
+    got, w_0 = lax.optimization_barrier((got, w_0))
+    w_1, wh_1 = scatter(*points, got, 224, 256, 32)
     return tuple(
         local_kernel(
             finish_kernel,
             [shape(F, CX, CY), shape(CX, CY)],
-            (stepped, *exchange(blocks), w_0, w_1, wh_0, wh_1),
+            (
+                stepped,
+                *exchange(blocks),
+                sides,
+                west,
+                east,
+                first_x,
+                last_x,
+                w_0,
+                w_1,
+                wh_0,
+                wh_1,
+            ),
         )
     )
 

time: 146 us -> 131 us (0.90)
  waiting for transfers between devices: 55.7 us -> 35.8 us
  blocking collectives: 0 us -> 8.74 us
  local copies, waits for them, and re-layouts: 4.84 us -> 1.57 us
  Pallas kernels: 34.1 us -> 31.7 us
  starting transfers between devices: 49.3 us -> 51.6 us
    all_to_all x2, waiting for transfers between devices: 35.2 us -> 22.5 us  [all_to_all(): return lax.all_to_all(array, axis, split_axis=0, concat_axis=0, tiled=True)]
    ppermute x14, waiting for transfers between devices: 19.8 us -> 10 us  [exchange(): lax.ppermute(blocks[k], 'gx', [(i, (i + k) % GX) for i in range(GX)])]
    all_to_all x0 -> x1, blocking collectives: none -> 8.74 us  [all_to_all(): return lax.all_to_all(array, axis, split_axis=0, concat_axis=0, tiled=True)]
    unnamed x35 -> x49, local copies, waits for them, and re-layouts: 4.79 us -> 1.57 us
    ppermute x14, starting transfers between devices: 15.9 us -> 18.6 us  [exchange(): lax.ppermute(blocks[k], 'gx', [(i, (i + k) % GX) for i in range(GX)])]
    ppermute x4, waiting for transfers between devices: 0.74 us -> 3.25 us  [the longest x1 3.24 us: body(): east = lax.ppermute(first_x, 'gx', down_x)]
    pallas_call x8, Pallas kernels: 34.1 us -> 31.7 us  [the longest x2 16 us: scatter(): pl.pallas_call(scatter_kernel, grid=(steps,), in_specs=[block] * 3 + [pl....]
    ppermute x4, starting transfers between devices: 12.5 us -> 10.9 us  [the longest x1 3.99 us: body(): south = lax.ppermute(last_y, 'gy', up_y)]
  transfers between devices with their start and end apart: 20 -> 20, of which waited for: 8 -> 5; matrix products, arithmetic and copies ran while one was open for 0% -> 0% of each run, Pallas kernels for 13% -> 12%
where the time goes in v3:
time: 131 us
  starting transfers between devices  51.6 us (39%)
  waiting for transfers between devices  35.8 us (27%)
  Pallas kernels  31.7 us (24%)
  blocking collectives  8.74 us (7%)
  local copies, waits for them, and re-layouts  1.57 us (1%)
    all_to_all x2, waiting for transfers between devices, all_to_all(): return lax.all_to_all(array, axis, split_axis=0, concat_axis=0, tiled=True)  22.5 us
    all_to_all x2, starting transfers between devices, all_to_all(): return lax.all_to_all(array, axis, split_axis=0, concat_axis=0, tiled=True)  22.1 us
    ppermute x14, starting transfers between devices, exchange(): lax.ppermute(blocks[k], 'gx', [(i, (i + k) % GX) for i in range(GX)])  18.6 us
    pallas_call x2, Pallas kernels, scatter(): pl.pallas_call(scatter_kernel, grid=(steps,), in_specs=[block] * 3 + [pl....  16 us
    pallas_call x6, Pallas kernels, local_kernel(): pl.pallas_call(kernel, in_specs=[place] * len(operands), out_specs=[vmem]...  15.7 us
    ppermute x14, waiting for transfers between devices, exchange(): lax.ppermute(blocks[k], 'gx', [(i, (i + k) % GX) for i in range(GX)])  10 us
    all_to_all x1, blocking collectives, all_to_all(): return lax.all_to_all(array, axis, split_axis=0, concat_axis=0, tiled=True)  8.74 us
    ppermute x1, starting transfers between devices, body(): south = lax.ppermute(last_y, 'gy', up_y)  3.99 us
  transfers between devices with their start and end apart: 20, of which 5 were waited for; matrix products, arithmetic and copies ran while one was open for 0% of the time, Pallas kernels for 12%

profile of v3, /device:TPU:1, one launch (start us, length us, event | category | flops | bytes accessed | tf_op | source)
XLA Modules:
  0.0 130.6 jit_solution(15621934646318255948)
XLA Ops:
  0.7 5.2 %shard_map.203 = (f32[8,128,256]{2,1,0:T(8,128)}, f32[8,256]{1,0:T(8,128)}, f32[16,256]{1,0:T(8,128)}, f32[8,128]{1,0:T(8,128)}, f32[16,128]{1,0:T(8,128)}, /*in...) custom-call(f32[8,128,256]{2,1,0:T(8,128)} %fields_hbm.1, ...), custom_call_target="tpu_custom_call" | custom-call | bytes 3510272 | tf_op jit(solution)/shard_map/pallas_call | solution.py:103
  5.9 2.6 %collective-permute-start = (f32[136,256]{1,0:T(8,128)}, f32[136,256]{1,0:T(8,128)S(1)}, u32[]{:S(2)}, u32[]{:S(2)}) collective-permute-start(f32[136,256]{1,0:T(8,128)} %get-tuple-element.40), channel_id=1, source_target_pairs={{0,32},{32,64},{64,96},{96,128},{128,160},{160,192},{192,224},{224... | collective-permute-start | bytes 417800 | tf_op jit(solution)/shard_map/ppermute | solution.py:360
  11.0 4.0 %collective-permute-start.7 = (f32[8,128]{1,0:T(8,128)}, f32[8,128]{1,0:T(8,128)S(1)}, u32[]{:S(2)}, u32[]{:S(2)}) collective-permute-start(f32[8,128]{1,0:T(8,128)} %get-tuple-element.48.last_ref), channel_id=1, source_target_pairs={{0,1},{1,2},{2,3},{3,4},{4,5},{5,6},{6,7},{7,8},{8,9},{9,10},{10,1... | collective-permute-start | bytes 12296 | tf_op jit(solution)/shard_map/ppermute | solution.py:465
  15.0 2.2 %collective-permute-start.2 = (f32[136,256]{1,0:T(8,128)}, f32[136,256]{1,0:T(8,128)S(1)}, u32[]{:S(2)}, u32[]{:S(2)}) collective-permute-start(f32[136,256]{1,0:T(8,128)} %get-tuple-element.42), channel_id=1, source_target_pairs={{0,96},{32,128},{64,160},{96,192},{128,224},{160,0},{192,32},{224,... | collective-permute-start | bytes 417800 | tf_op jit(solution)/shard_map/ppermute | solution.py:360
  17.3 1.9 %collective-permute-start.3 = (f32[136,256]{1,0:T(8,128)}, f32[136,256]{1,0:T(8,128)S(1)}, u32[]{:S(2)}, u32[]{:S(2)}) collective-permute-start(f32[136,256]{1,0:T(8,128)} %get-tuple-element.43), channel_id=1, source_target_pairs={{0,128},{32,160},{64,192},{96,224},{128,0},{160,32},{192,64},{224,... | collective-permute-start | bytes 417800 | tf_op jit(solution)/shard_map/ppermute | solution.py:360
  19.1 1.8 %collective-permute-start.4 = (f32[136,256]{1,0:T(8,128)}, f32[136,256]{1,0:T(8,128)S(1)}, u32[]{:S(2)}, u32[]{:S(2)}) collective-permute-start(f32[136,256]{1,0:T(8,128)} %get-tuple-element.44), channel_id=1, source_target_pairs={{0,160},{32,192},{64,224},{96,0},{128,32},{160,64},{192,96},{224,1... | collective-permute-start | bytes 417800 | tf_op jit(solution)/shard_map/ppermute | solution.py:360
  23.5 8.7 %all_to_all.15.refs_8_ = f32[8,8,128]{2,1,0:T(8,128)S(1)} all-to-all(f32[8,8,128]{2,1,0:T(8,128)S(1)} %shard_map.204.refs_9_), channel_id=1, replica_groups=mesh['gx'=8,'gy'=32] {'gx'}, dimensions={0} | all-to-all | bytes 65536 | tf_op jit(solution)/shard_map/all_to_all | solution.py:73
  32.3 3.7 %shard_map.205 = f32[256,1,768]{2,1,0:T(1,128)} custom-call(f32[136,256]{1,0:T(8,128)S(1)} %copy-done.4, f32[136,256]{1,0:T(8,128)S(1)} %collective-permute-done.refs_1_, f32[136,256]{1,0:T(8,128)S(1)} %collective-permute-done.1.refs_2_, f32[136,256]{1,0:T(8,128)S(1)} %collective-permute-done.2.refs_3_, f32[136,256]{1,0:T(8,128)S(1)} %collective-permute-done.3.refs_4_, ...), custom_call_target="tpu_custom_call" | custom-call | flops 805306368 | bytes 3784704 | tf_op jit(solution)/shard_map/pallas_call | solution.py:103
  36.0 15.8 %all-to-all-start.1 = ((f32[256,1,768]{2,1,0:T(1,128)}), f32[256,1,768]{2,1,0:T(1,128)S(1)}, u32[]{:S(2)}, u32[]{:S(2)}) async-start(f32[256,1,768]{2,1,0:T(1,128)} %shard_map.205), calls=%async_computation.1 | async-start | bytes 1572864 | tf_op jit(solution)/shard_map/all_to_all | solution.py:73
  51.8 3.7 %collective-permute-start.9 = (f32[8,256]{1,0:T(8,128)S(1)}, f32[8,256]{1,0:T(8,128)S(1)}, u32[]{:S(2)}, u32[]{:S(2)}) collective-permute-start(f32[8,256]{1,0:T(8,128)S(1)} %copy-done.11), channel_id=1, source_target_pairs={{0,32},{32,64},{64,96},{96,128},{128,160},{160,192},{192,224},{1,3... | collective-permute-start | bytes 24584 | tf_op jit(solution)/shard_map/ppermute | solution.py:488
  55.5 1.9 %collective-permute-start.10 = (f32[16,256]{1,0:T(8,128)S(1)}, f32[16,256]{1,0:T(8,128)S(1)}, u32[]{:S(2)}, u32[]{:S(2)}) collective-permute-start(f32[16,256]{1,0:T(8,128)S(1)} %copy-done.9), channel_id=1, source_target_pairs={{32,0},{64,32},{96,64},{128,96},{160,128},{192,160},{224,192},{33,... | collective-permute-start | bytes 49160 | tf_op jit(solution)/shard_map/ppermute | solution.py:489
  57.7 3.2 %collective-permute-done.10.refs_11_ = f32[16,256]{1,0:T(8,128)S(1)} collective-permute-done((f32[16,256]{1,0:T(8,128)S(1)}, f32[16,256]{1,0:T(8,128)S(1)}, u32[]{:S(2)}, u32[]{:S(2)}) %collective-permute-start.10) | collective-permute-done | bytes 16416 | tf_op jit(solution)/shard_map/ppermute | solution.py:489
  61.0 16.4 %all-to-all-done.1.got_ref = f32[256,1,768]{2,1,0:T(1,128)S(1)} async-done(((f32[256,1,768]{2,1,0:T(1,128)}), f32[256,1,768]{2,1,0:T(1,128)S(1)}, u32[]{:S(2)}, u32[]{:S(2)}) %all-to-all-start.1) | async-done | bytes 786464 | tf_op jit(solution)/shard_map/all_to_all | solution.py:73
  77.4 2.4 %shard_map.206 = f32[256,1,512]{2,1,0:T(1,128)} custom-call(f32[256,1,768]{2,1,0:T(1,128)S(1)} %all-to-all-done.1.got_ref, f32[2,4,4,32,128]{4,3,2,1,0:T(8,128)S(1)} %copy-done.1, f32[2,8,32,128]{3,2,1,0:T(8,128)S(1)} %bitcast.9, f32[8,128]{1,0:T(8,128)S(1)} %copy-done.13, f32[8,128]{1,0:T(8,128)S(1)} %bitcast.12), custom_call_target="tpu_custom_call" | custom-call | flops 12582912 | bytes 2105344 | tf_op jit(solution)/shard_map/pallas_call | solution.py:103
  79.8 6.4 %all-to-all-start.2 = ((f32[256,1,512]{2,1,0:T(1,128)}), f32[256,1,512]{2,1,0:T(1,128)S(1)}, u32[]{:S(2)}, u32[]{:S(2)}) async-start(f32[256,1,512]{2,1,0:T(1,128)} %shard_map.206), calls=%async_computation.2 | async-start | bytes 1048576 | tf_op jit(solution)/shard_map/all_to_all | solution.py:73
  86.2 13.8 %shard_map.207 = (f32[128,256]{1,0:T(8,128)S(1)}, f32[128,256]{1,0:T(8,128)S(1)}) custom-call(s32[256,128]{1,0:T(8,128)S(1)} %bitcast.13, s32[256,128]{1,0:T(8,128)S(1)} %bitcast.15, f32[256,128]{1,0:T(8,128)S(1)} %fusion.live_ref, f32[256,1,768]{2,1,0:T(1,128)S(1)} %all-to-all-done.1.got_ref), custom_call_target="tpu_custom_call" | custom-call | flops 11274289152 | bytes 458752 | tf_op jit(solution)/shard_map/pallas_call | solution.py:416
  100.0 6.1 %all-to-all-done.2.got_ref = f32[256,1,512]{2,1,0:T(1,128)S(1)} async-done(((f32[256,1,512]{2,1,0:T(1,128)}), f32[256,1,512]{2,1,0:T(1,128)S(1)}, u32[]{:S(2)}, u32[]{:S(2)}) %all-to-all-start.2) | async-done | bytes 524320 | tf_op jit(solution)/shard_map/all_to_all | solution.py:73
  106.2 2.8 %shard_map.208 = (f32[128,256]{1,0:T(8,128)S(1)}, f32[128,256]{1,0:T(8,128)S(1)}, f32[128,256]{1,0:T(8,128)S(1)}, f32[128,256]{1,0:T(8,128)S(1)}, f32[128,256]{1...) custom-call(f32[256,1,512]{2,1,0:T(1,128)S(1)} %all-to-all-done.2.got_ref, ...), custom_call_target="tpu_custom_call" | custom-call | flops 1207959552 | bytes 3670016 | tf_op jit(solution)/shard_map/pallas_call | solution.py:103
  112.4 1.8 %collective-permute-start.14 = (f32[128,256]{1,0:T(8,128)S(1)}, f32[128,256]{1,0:T(8,128)S(1)}, u32[]{:S(2)}, u32[]{:S(2)}) collective-permute-start(f32[128,256]{1,0:T(8,128)S(1)} %get-tuple-element.62), channel_id=1, source_target_pairs={{0,128},{32,160},{64,192},{96,224},{128,0},{160,32},{192,64},{224,... | collective-permute-start | bytes 393224 | tf_op jit(solution)/shard_map/ppermute | solution.py:360
  114.1 2.6 %collective-permute-start.15 = (f32[128,256]{1,0:T(8,128)S(1)}, f32[128,256]{1,0:T(8,128)S(1)}, u32[]{:S(2)}, u32[]{:S(2)}) collective-permute-start(f32[128,256]{1,0:T(8,128)S(1)} %get-tuple-element.63), channel_id=1, source_target_pairs={{0,160},{32,192},{64,224},{96,0},{128,32},{160,64},{192,96},{224,1... | collective-permute-start | bytes 393224 | tf_op jit(solution)/shard_map/ppermute | solution.py:360
  116.8 7.8 %collective-permute-done.12.refs_3_ = f32[128,256]{1,0:T(8,128)S(1)} collective-permute-done((f32[128,256]{1,0:T(8,128)S(1)}, f32[128,256]{1,0:T(8,128)S(1)}, u32[]{:S(2)}, u32[]{:S(2)}) %collective-permute-start.12) | collective-permute-done | bytes 131104 | tf_op jit(solution)/shard_map/ppermute | solution.py:360
  124.6 2.1 %shard_map.209 = (f32[128,256]{1,0:T(8,128)S(1)}, f32[128,256]{1,0:T(8,128)S(1)}) custom-call(s32[256,128]{1,0:T(8,128)S(1)} %bitcast.14, s32[256,128]{1,0:T(8,128)S(1)} %bitcast.16, f32[256,128]{1,0:T(8,128)S(1)} %fusion.live_ref, f32[256,1,768]{2,1,0:T(1,128)S(1)} %all-to-all-done.1.got_ref), custom_call_target="tpu_custom_call" | custom-call | flops 1610612736 | bytes 65536 | tf_op jit(solution)/shard_map/pallas_call | solution.py:416
  126.8 2.2 %collective-permute-done.17.refs_8_ = f32[128,256]{1,0:T(8,128)S(1)} collective-permute-done((f32[128,256]{1,0:T(8,128)S(1)}, f32[128,256]{1,0:T(8,128)S(1)}, u32[]{:S(2)}, u32[]{:S(2)}) %collective-permute-start.17) | collective-permute-done | bytes 131104 | tf_op jit(solution)/shard_map/ppermute | solution.py:360
  129.0 1.6 %shard_map.210 = (f32[8,128,256]{2,1,0:T(8,128)}, f32[128,256]{1,0:T(8,128)}) custom-call(f32[8,128,256]{2,1,0:T(8,128)S(1)} %copy-done, f32[128,256]{1,0:T(8,128)S(1)} %get-tuple-element.58.refs_1_, f32[128,256]{1,0:T(8,128)S(1)} %collective-permute-done.11.refs_2_, f32[128,256]{1,0:T(8,128)S(1)} %collective-permute-done.12.refs_3_, ...), custom_call_target="tpu_custom_call" | custom-call | bytes 3883008 | tf_op jit(solution)/shard_map/pallas_call | solution.py:103
  (75 shorter events, 8.7 us)
Async XLA Ops:
  0.6 31.6 %copy-start.2 = (bf16[512,256]{1,0:T(8,128)(2,1)S(1)}, bf16[512,256]{1,0:T(8,128)(2,1)}, u32[]{:S(2)}) copy-start(bf16[512,256]{1,0:T(8,128)(2,1)} %constant.24.clone.refs_13_) | copy-start | bytes 786436
  0.6 31.6 %copy-start.3 = (bf16[512,256]{1,0:T(8,128)(2,1)S(1)}, bf16[512,256]{1,0:T(8,128)(2,1)}, u32[]{:S(2)}) copy-start(bf16[512,256]{1,0:T(8,128)(2,1)} %constant.23.clone.refs_12_) | copy-start | bytes 786436
  0.7 31.6 %copy-start.5 = (f32[1,256,128]{2,1,0:T(8,128)S(1)}, f32[1,256,128]{2,1,0:T(8,128)}, u32[]{:S(2)}) copy-start(f32[1,256,128]{2,1,0:T(8,128)} %param.25) | copy-start | bytes 393220
  0.7 31.6 %copy-start.6 = (f32[1,256,128]{2,1,0:T(8,128)S(1)}, f32[1,256,128]{2,1,0:T(8,128)}, u32[]{:S(2)}) copy-start(f32[1,256,128]{2,1,0:T(8,128)} %param.26) | copy-start | bytes 393220
  5.9 15.0 %collective-permute-start = (f32[136,256]{1,0:T(8,128)}, f32[136,256]{1,0:T(8,128)S(1)}, u32[]{:S(2)}, u32[]{:S(2)}) collective-permute-start(f32[136,256]{1,0:T(8,128)} %get-tuple-element.40), channel_id=1, source_target_pairs={{0,32},{32,64},{64,96},{96,128},{128,160},{160,192},{192,224},{224... | collective-permute-start | bytes 417800 | tf_op jit(solution)/shard_map/ppermute | solution.py:360
  8.5 12.6 %collective-permute-start.1 = (f32[136,256]{1,0:T(8,128)}, f32[136,256]{1,0:T(8,128)S(1)}, u32[]{:S(2)}, u32[]{:S(2)}) collective-permute-start(f32[136,256]{1,0:T(8,128)} %get-tuple-element.41), channel_id=1, source_target_pairs={{0,64},{32,96},{64,128},{96,160},{128,192},{160,224},{192,0},{224,... | collective-permute-start | bytes 417800 | tf_op jit(solution)/shard_map/ppermute | solution.py:360
  9.7 9.4 %collective-permute-start.8 = (f32[16,128]{1,0:T(8,128)}, f32[16,128]{1,0:T(8,128)S(1)}, u32[]{:S(2)}, u32[]{:S(2)}) collective-permute-start(f32[16,128]{1,0:T(8,128)} %get-tuple-element.47.first_ref), channel_id=1, source_target_pairs={{1,0},{2,1},{3,2},{4,3},{5,4},{6,5},{7,6},{8,7},{9,8},{10,9},{11,1... | collective-permute-start | bytes 24584 | tf_op jit(solution)/shard_map/ppermute | solution.py:466
  11.0 6.2 %collective-permute-start.7 = (f32[8,128]{1,0:T(8,128)}, f32[8,128]{1,0:T(8,128)S(1)}, u32[]{:S(2)}, u32[]{:S(2)}) collective-permute-start(f32[8,128]{1,0:T(8,128)} %get-tuple-element.48.last_ref), channel_id=1, source_target_pairs={{0,1},{1,2},{2,3},{3,4},{4,5},{5,6},{6,7},{7,8},{8,9},{9,10},{10,1... | collective-permute-start | bytes 12296 | tf_op jit(solution)/shard_map/ppermute | solution.py:465
  15.0 17.2 %collective-permute-start.2 = (f32[136,256]{1,0:T(8,128)}, f32[136,256]{1,0:T(8,128)S(1)}, u32[]{:S(2)}, u32[]{:S(2)}) collective-permute-start(f32[136,256]{1,0:T(8,128)} %get-tuple-element.42), channel_id=1, source_target_pairs={{0,96},{32,128},{64,160},{96,192},{128,224},{160,0},{192,32},{224,... | collective-permute-start | bytes 417800 | tf_op jit(solution)/shard_map/ppermute | solution.py:360
  17.3 14.9 %collective-permute-start.3 = (f32[136,256]{1,0:T(8,128)}, f32[136,256]{1,0:T(8,128)S(1)}, u32[]{:S(2)}, u32[]{:S(2)}) collective-permute-start(f32[136,256]{1,0:T(8,128)} %get-tuple-element.43), channel_id=1, source_target_pairs={{0,128},{32,160},{64,192},{96,224},{128,0},{160,32},{192,64},{224,... | collective-permute-start | bytes 417800 | tf_op jit(solution)/shard_map/ppermute | solution.py:360
  19.1 13.1 %collective-permute-start.4 = (f32[136,256]{1,0:T(8,128)}, f32[136,256]{1,0:T(8,128)S(1)}, u32[]{:S(2)}, u32[]{:S(2)}) collective-permute-start(f32[136,256]{1,0:T(8,128)} %get-tuple-element.44), channel_id=1, source_target_pairs={{0,160},{32,192},{64,224},{96,0},{128,32},{160,64},{192,96},{224,1... | collective-permute-start | bytes 417800 | tf_op jit(solution)/shard_map/ppermute | solution.py:360
  20.9 11.3 %collective-permute-start.5 = (f32[136,256]{1,0:T(8,128)}, f32[136,256]{1,0:T(8,128)S(1)}, u32[]{:S(2)}, u32[]{:S(2)}) collective-permute-start(f32[136,256]{1,0:T(8,128)} %get-tuple-element.45), channel_id=1, source_target_pairs={{0,192},{32,224},{64,0},{96,32},{128,64},{160,96},{192,128},{224,1... | collective-permute-start | bytes 417800 | tf_op jit(solution)/shard_map/ppermute | solution.py:360
  21.1 11.1 %collective-permute-start.6 = (f32[136,256]{1,0:T(8,128)}, f32[136,256]{1,0:T(8,128)S(1)}, u32[]{:S(2)}, u32[]{:S(2)}) collective-permute-start(f32[136,256]{1,0:T(8,128)} %get-tuple-element.46), channel_id=1, source_target_pairs={{0,224},{32,0},{64,32},{96,64},{128,96},{160,128},{192,160},{224,1... | collective-permute-start | bytes 417800 | tf_op jit(solution)/shard_map/ppermute | solution.py:360
  36.0 41.3 %all-to-all-start.1 = ((f32[256,1,768]{2,1,0:T(1,128)}), f32[256,1,768]{2,1,0:T(1,128)S(1)}, u32[]{:S(2)}, u32[]{:S(2)}) async-start(f32[256,1,768]{2,1,0:T(1,128)} %shard_map.205), calls=%async_computation.1 | async-start | bytes 1572864 | tf_op jit(solution)/shard_map/all_to_all | solution.py:73
  51.8 5.9 %collective-permute-start.9 = (f32[8,256]{1,0:T(8,128)S(1)}, f32[8,256]{1,0:T(8,128)S(1)}, u32[]{:S(2)}, u32[]{:S(2)}) collective-permute-start(f32[8,256]{1,0:T(8,128)S(1)} %copy-done.11), channel_id=1, source_target_pairs={{0,32},{32,64},{64,96},{96,128},{128,160},{160,192},{192,224},{1,3... | collective-permute-start | bytes 24584 | tf_op jit(solution)/shard_map/ppermute | solution.py:488
  55.5 5.4 %collective-permute-start.10 = (f32[16,256]{1,0:T(8,128)S(1)}, f32[16,256]{1,0:T(8,128)S(1)}, u32[]{:S(2)}, u32[]{:S(2)}) collective-permute-start(f32[16,256]{1,0:T(8,128)S(1)} %copy-done.9), channel_id=1, source_target_pairs={{32,0},{64,32},{96,64},{128,96},{160,128},{192,160},{224,192},{33,... | collective-permute-start | bytes 49160 | tf_op jit(solution)/shard_map/ppermute | solution.py:489
  79.8 26.4 %all-to-all-start.2 = ((f32[256,1,512]{2,1,0:T(1,128)}), f32[256,1,512]{2,1,0:T(1,128)S(1)}, u32[]{:S(2)}, u32[]{:S(2)}) async-start(f32[256,1,512]{2,1,0:T(1,128)} %shard_map.206), calls=%async_computation.2 | async-start | bytes 1048576 | tf_op jit(solution)/shard_map/all_to_all | solution.py:73
  109.0 7.8 %collective-permute-start.11 = (f32[128,256]{1,0:T(8,128)S(1)}, f32[128,256]{1,0:T(8,128)S(1)}, u32[]{:S(2)}, u32[]{:S(2)}) collective-permute-start(f32[128,256]{1,0:T(8,128)S(1)} %get-tuple-element.59), channel_id=1, source_target_pairs={{0,32},{32,64},{64,96},{96,128},{128,160},{160,192},{192,224},{224... | collective-permute-start | bytes 393224 | tf_op jit(solution)/shard_map/ppermute | solution.py:360
  110.2 14.3 %collective-permute-start.12 = (f32[128,256]{1,0:T(8,128)S(1)}, f32[128,256]{1,0:T(8,128)S(1)}, u32[]{:S(2)}, u32[]{:S(2)}) collective-permute-start(f32[128,256]{1,0:T(8,128)S(1)} %get-tuple-element.60), channel_id=1, source_target_pairs={{0,64},{32,96},{64,128},{96,160},{128,192},{160,224},{192,0},{224,... | collective-permute-start | bytes 393224 | tf_op jit(solution)/shard_map/ppermute | solution.py:360
  111.2 15.6 %collective-permute-start.13 = (f32[128,256]{1,0:T(8,128)S(1)}, f32[128,256]{1,0:T(8,128)S(1)}, u32[]{:S(2)}, u32[]{:S(2)}) collective-permute-start(f32[128,256]{1,0:T(8,128)S(1)} %get-tuple-element.61), channel_id=1, source_target_pairs={{0,96},{32,128},{64,160},{96,192},{128,224},{160,0},{192,32},{224,... | collective-permute-start | bytes 393224 | tf_op jit(solution)/shard_map/ppermute | solution.py:360
  112.4 14.4 %collective-permute-start.14 = (f32[128,256]{1,0:T(8,128)S(1)}, f32[128,256]{1,0:T(8,128)S(1)}, u32[]{:S(2)}, u32[]{:S(2)}) collective-permute-start(f32[128,256]{1,0:T(8,128)S(1)} %get-tuple-element.62), channel_id=1, source_target_pairs={{0,128},{32,160},{64,192},{96,224},{128,0},{160,32},{192,64},{224,... | collective-permute-start | bytes 393224 | tf_op jit(solution)/shard_map/ppermute | solution.py:360
  114.1 12.6 %collective-permute-start.15 = (f32[128,256]{1,0:T(8,128)S(1)}, f32[128,256]{1,0:T(8,128)S(1)}, u32[]{:S(2)}, u32[]{:S(2)}) collective-permute-start(f32[128,256]{1,0:T(8,128)S(1)} %get-tuple-element.63), channel_id=1, source_target_pairs={{0,160},{32,192},{64,224},{96,0},{128,32},{160,64},{192,96},{224,1... | collective-permute-start | bytes 393224 | tf_op jit(solution)/shard_map/ppermute | solution.py:360
  116.8 10.0 %collective-permute-start.16 = (f32[128,256]{1,0:T(8,128)S(1)}, f32[128,256]{1,0:T(8,128)S(1)}, u32[]{:S(2)}, u32[]{:S(2)}) collective-permute-start(f32[128,256]{1,0:T(8,128)S(1)} %get-tuple-element.64), channel_id=1, source_target_pairs={{0,192},{32,224},{64,0},{96,32},{128,64},{160,96},{192,128},{224,1... | collective-permute-start | bytes 393224 | tf_op jit(solution)/shard_map/ppermute | solution.py:360
  124.6 4.4 %collective-permute-start.17 = (f32[128,256]{1,0:T(8,128)S(1)}, f32[128,256]{1,0:T(8,128)S(1)}, u32[]{:S(2)}, u32[]{:S(2)}) collective-permute-start(f32[128,256]{1,0:T(8,128)S(1)} %get-tuple-element.65), channel_id=1, source_target_pairs={{0,224},{32,0},{64,32},{96,64},{128,96},{160,128},{192,160},{224,1... | collective-permute-start | bytes 393224 | tf_op jit(solution)/shard_map/ppermute | solution.py:360
  (20 other events, 363.1 us)

commit v4 on v3

--- a/solution.py
+++ b/solution.py
@@ -19,6 +19,7 @@
 GY = 32
 DEV = GX * GY
 HALF = MY // 2
+PARTNERS = (0, 2, 6, 3, 7, 4, 5, 1)
 
 time_step = 0.2
 diffusion = 0.25
@@ -38,7 +39,7 @@
     m = np.arange(MX)
     q = np.where(m < MX // 2, m, m - MX)
     ang = 2.0 * np.pi * (x[:, None] * q[None, :]) / NX
-    back_x = np.concatenate((np.cos(ang), -np.sin(ang)), axis=1)
+    back_x = np.concatenate((np.cos(ang), -np.sin(ang)))
     ang = 2.0 * np.pi * np.arange(8) / 8.0
     period = np.stack([np.tile(row[:, None], (1, CY)) for row in (np.cos(ang), -np.sin(ang))])
     ang = 2.0 * np.pi * (ORDER[:, None] * np.arange(CY)[None, :]) / NY
@@ -57,14 +58,17 @@
         high = array.astype(np.float32).astype(jnp.bfloat16)
         return high, (array - high.astype(np.float64)).astype(np.float32).astype(jnp.bfloat16)
 
+    fore = np.concatenate((*pair(fore_x), *pair(fore_y)))
+    back = np.concatenate((*pair(back_y), *pair(back_x)))
     return (
-        *map(pair, (fore_x, back_x, fore_y, back_y)),
+        fore,
+        back,
         period.astype(np.float32),
         turn.astype(np.float32),
     )
 
 
-FORE_X, BACK_X, FORE_Y, BACK_Y, PERIOD, TURN = tables()
+FORE, BACK, PERIOD, TURN = tables()
 SCALE_IN = 1.0 / math.sqrt(NX * NY)
 SCALE_OUT = 1.0 / math.sqrt(MX * MY)
 
@@ -118,77 +122,84 @@
     )
 
 
-def step_kernel(fields_hbm, velocity_hbm, *refs):
-    out_ref, last_x_ref, first_x_ref, last_y_ref, first_y_ref = refs[:5]
-    block_refs = refs[5:-3]
-    fields_ref, velocity_ref, sems = refs[-3:]
-    copies = [pltpu.make_async_copy(velocity_hbm, velocity_ref, sems.at[F])]
+def edge_kernel(
+    fields_hbm, velocity_hbm, last_x_ref, first_x_ref, last_y_ref, first_y_ref, block_ref, row_ref, sems
+):
+    copies = [
+        pltpu.make_async_copy(fields_hbm.at[f], block_ref.at[f], sems.at[f]) for f in range(F)
+    ]
     copies += [
-        pltpu.make_async_copy(fields_hbm.at[f], fields_ref.at[f], sems.at[f]) for f in range(F)
+        pltpu.make_async_copy(velocity_hbm.at[1], block_ref.at[F], sems.at[F]),
+        pltpu.make_async_copy(velocity_hbm.at[0, pl.ds(0, 8)], row_ref, sems.at[F + 1]),
     ]
     for copy in copies:
         copy.start()
+    first_x_ref[F + 1 :] = jnp.zeros((7, CY), jnp.float32)
+    lane = lax.broadcasted_iota(jnp.int32, (CX, 128), 1)
+    sides = jnp.zeros((CX, 128), jnp.float32)
+    for f in range(F + 1):
+        copies[f].wait()
+        tile = block_ref[f, :, 0:128]
+        sides = jnp.where(lane == f, pltpu.roll(tile, f, 1) if f else tile, sides)
+        if f < F:
+            sides = jnp.where(
+                lane == 16 + f, pltpu.roll(block_ref[f, :, 128:256], 17 + f, 1), sides
+            )
+            last_x_ref[f : f + 1] = block_ref[f, CX - 1 : CX]
+            first_x_ref[f : f + 1] = block_ref[f, 0:1]
+    sides = jnp.transpose(sides)
+    first_y_ref[...] = sides[0:16]
+    last_y_ref[...] = sides[16 : 16 + F]
+    copies[F + 1].wait()
+    first_x_ref[F : F + 1] = row_ref[0:1]
+
+
+def step_kernel(fields_ref, velocity_ref, south_ref, north_ref, *refs):
+    *block_refs, held_ref = refs
     row = lax.broadcasted_iota(jnp.int32, (CX, CY), 0)
     col = lax.broadcasted_iota(jnp.int32, (CX, CY), 1)
-    pick_row = lax.broadcasted_iota(jnp.int32, (8, CY), 0)
-    pick_col = lax.broadcasted_iota(jnp.int32, (8, CY), 1)
-    pick = jnp.where(pick_col == pick_row * (CY - 1), 1.0, 0.0).astype(jnp.float32)
-    first_x_ref[...] = jnp.zeros((16, CY), jnp.float32)
-    first_y_ref[...] = jnp.zeros((16, CX), jnp.float32)
-    copies[0].wait()
-    first_x_ref[F : F + 1] = velocity_ref[0, 0:1]
-    first_y_ref[F : F + 1] = dot(pick, velocity_ref[1], ((1,), (1,)))[0:1]
+    first_col, last_col = col == 0, col == CY - 1
+    gx, gy = lax.axis_index("gx"), lax.axis_index("gy")
+    open_s = jnp.where(gy > 0, 1.0, 0.0)
+    open_n = jnp.where(gy < GY - 1, 1.0, 0.0)
+    before = jnp.transpose(south_ref[...])
+    after = jnp.transpose(north_ref[...])
     low_w, high_w = (jnp.where(row == 0, 0.0, value) for value in face(velocity_ref[0]))
     low_e, high_e = (
         jnp.where(row == CX - 1, 0.0, pltpu.roll(value, CX - 1, 0)) for value in (low_w, high_w)
     )
-    low_s, high_s = (jnp.where(col == 0, 0.0, value) for value in face(velocity_ref[1]))
+    low_s, high_s = (
+        jnp.where(first_col, value * open_s, value) for value in face(velocity_ref[1])
+    )
     low_n, high_n = (
-        jnp.where(col == CY - 1, 0.0, pltpu.roll(value, CY - 1, 1)) for value in (low_s, high_s)
+        jnp.where(last_col, edge * open_n, pltpu.roll(value, CY - 1, 1))
+        for value, edge in zip((low_s, high_s), face(after[:, F : F + 1]))
     )
     own = 1.0 - low_e + high_w - low_n + high_s
     for f in range(F):
-        copies[f + 1].wait()
         block = fields_ref[f]
-        ends = dot(pick, block, ((1,), (1,)))
-        first_y_ref[f : f + 1] = ends[0:1]
-        last_y_ref[f : f + 1] = ends[1:2]
-        last_x_ref[f : f + 1] = block[CX - 1 : CX]
-        first_x_ref[f : f + 1] = block[0:1]
-        out_ref[f] = (
+        south = jnp.where(first_col, before[:, f : f + 1], pltpu.roll(block, 1, 1))
+        north = jnp.where(last_col, after[:, f : f + 1], pltpu.roll(block, CY - 1, 1))
+        value = (
             own * block
             + low_w * pltpu.roll(block, 1, 0)
             - high_e * pltpu.roll(block, CX - 1, 0)
-            + low_s * pltpu.roll(block, 1, 1)
-            - high_n * pltpu.roll(block, CY - 1, 1)
+            + low_s * south
+            - high_n * north
         )
-    for k, ref in enumerate(block_refs):
-        f = lax.rem(lax.axis_index("gx") + k, GX)
-        ref[0:CX] = out_ref[f]
-        ref[CX : CX + 1] = fields_ref[f, 0:1]
-        ref[CX + 1 : CX + 2] = fields_ref[f, CX - 1 : CX]
-        ref[CX + 2 : CX + 3] = velocity_ref[0, 0:1]
-        ref[CX + 3 :] = jnp.zeros((5, CY), jnp.float32)
-
-
-def side_kernel(first_ref, last_ref, south_ref, north_ref, out_ref):
-    gy = lax.axis_index("gy")
-    first, second = face(first_ref[F : F + 1])
-    low = (first * south_ref[...] + second * first_ref[0:F]) * jnp.where(gy > 0, 1.0, 0.0)
-    first, second = face(north_ref[F : F + 1])
-    high = (first * last_ref[...] + second * north_ref[0:F]) * jnp.where(gy < GY - 1, 1.0, 0.0)
-    for f in range(F):
-        out_ref[f, 0:1] = low[f : f + 1]
-        out_ref[f, 1:2] = -high[f : f + 1]
-        out_ref[f, 2:] = jnp.zeros((6, CX), jnp.float32)
-
-
-def add_sides(block, sides):
-    sides = jnp.transpose(sides)
-    col = lax.broadcasted_iota(jnp.int32, (CX, CY), 1)
-    return block + jnp.where(
-        col == 0, sides[:, 0:1], jnp.where(col == CY - 1, sides[:, 1:2], 0.0)
-    )
+        extra = jnp.concatenate(
+            (
+                block[0:1],
+                block[CX - 1 : CX],
+                velocity_ref[0, 0:1],
+                jnp.zeros((5, CY), jnp.float32),
+            ),
+            axis=0,
+        )
+        held_ref[f, 0:CX] = value
+        held_ref[f, CX:] = extra
+    for k, ref in zip(PARTNERS, block_refs):
+        ref[...] = held_ref[lax.bitwise_xor(gx, k)]
 
 
 def quarter_turn(index, t):
@@ -199,15 +210,11 @@
 
 
 def forward_kernel(*refs):
-    *block_refs, sides_ref, fore_xh, fore_xl, period_ref, fore_yh, fore_yl, height_ref, weight_ref = (
-        refs[:-4]
-    )
+    *block_refs, table_ref, period_ref, height_ref, weight_ref = refs[:-4]
     out_ref, columns_ref, parts_ref, edges_ref = refs[-4:]
-    for k, ref in enumerate(block_refs):
-        source = lax.rem(lax.axis_index("gx") + (GX - k), GX)
-        columns_ref[pl.ds(pl.multiple_of(source * CX, CX), CX), :] = add_sides(
-            ref[0:CX], sides_ref[source]
-        )
+    for k, ref in zip(PARTNERS, block_refs):
+        source = lax.bitwise_xor(lax.axis_index("gx"), k)
+        columns_ref[pl.ds(pl.multiple_of(source * CX, CX), CX), :] = ref[0:CX]
         edges_ref[source] = ref[CX:]
     for t in range(1, GX):
         first, second = face(edges_ref[t, 2:3])
@@ -218,7 +225,9 @@
     real = jnp.zeros((HALF, CY), jnp.float32)
     imag = jnp.zeros((HALF, CY), jnp.float32)
     for t in range(4):
-        piece = split_dot((fore_xh[...], fore_xl[...]), columns_ref[t * MX : (t + 1) * MX])
+        piece = split_dot(
+            (table_ref[0:256], table_ref[256:512]), columns_ref[t * MX : (t + 1) * MX]
+        )
         piece_r, piece_i = piece[:HALF], piece[HALF:]
         if t == 0:
             real, imag = piece_r, piece_i
@@ -236,7 +245,7 @@
     parts_ref[HALF:MX] = jnp.where(q == 0, last_r, dot(mirror, real))
     parts_ref[MX : MX + HALF] = imag
     parts_ref[MX + HALF :] = -jnp.where(q == 0, last_i, dot(mirror, imag))
-    mixed = split_dot((fore_yh[...], fore_yl[...]), parts_ref[...], ((1,), (1,)))
+    mixed = split_dot((table_ref[512:1024], table_ref[1024:]), parts_ref[...], ((1,), (1,)))
     modes = (mixed[:MY, :MX] + mixed[MY:, MX:], mixed[:MY, MX:] - mixed[MY:, :MX])
     group = lax.broadcasted_iota(jnp.int32, (GY, 128), 1) // 32
     for low in range(4):
@@ -296,7 +305,7 @@
             )
 
 
-def backward_kernel(got_ref, back_yh, back_yl, back_xh, back_xl, *refs):
+def backward_kernel(got_ref, table_ref, *refs):
     *out_refs, modes_ref, field_ref = refs
     group = lax.broadcasted_iota(jnp.int32, (GY, 128), 1) // 32
     for low in range(4):
@@ -316,34 +325,30 @@
                     lanes = part * MX + half * 128
                     start = high * 128 + low * 32
                     modes_ref[start : start + 32, lanes : lanes + 128] = value
-    mixed = split_dot((back_yh[...], back_yl[...]), modes_ref[...])
+    mixed = split_dot((table_ref[0:512], table_ref[512:1024]), modes_ref[...])
     real = mixed[:CY, :MX] - mixed[CY:, MX:]
     imag = mixed[:CY, MX:] + mixed[CY:, :MX]
     index = lax.broadcasted_iota(jnp.int32, (CY, MX), 1)
     for t in range(4):
-        if t == 0:
-            turned = jnp.concatenate((real, imag), axis=1)
-        else:
+        turned_r, turned_i = real, imag
+        if t:
             cosine, sine = quarter_turn(index, t)
-            turned = jnp.concatenate(
-                (real * cosine - imag * sine, imag * cosine + real * sine), axis=1
-            )
+            turned_r = real * cosine - imag * sine
+            turned_i = imag * cosine + real * sine
         field_ref[t * MX : (t + 1) * MX] = split_dot(
-            (back_xh[...], back_xl[...]), turned, ((1,), (1,))
-        )
-    for k, ref in enumerate(out_refs):
-        owner = lax.rem(lax.axis_index("gx") + k, GX)
+            (table_ref[1024:1280], table_ref[1536:1792]), turned_r, ((1,), (1,))
+        ) + split_dot((table_ref[1280:1536], table_ref[1792:]), turned_i, ((1,), (1,)))
+    for k, ref in zip(PARTNERS, out_refs):
+        owner = lax.bitwise_xor(lax.axis_index("gx"), k)
         ref[...] = field_ref[pl.ds(pl.multiple_of(owner * CX, CX), CX), :]
 
 
 def finish_kernel(*refs):
-    stepped_ref, *block_refs, sides_ref, west_ref, east_ref, first_ref, last_ref = refs[:-6]
-    w_0, w_1, wh_0, wh_1 = refs[-6:-2]
-    out_ref, gradient_ref = refs[-2:]
+    step_refs, block_refs, refs = refs[:GX], refs[GX : 2 * GX], refs[2 * GX :]
+    west_ref, east_ref, first_ref, last_ref, w_0, w_1, wh_0, wh_1, out_ref, gradient_ref = refs
     gx = lax.axis_index("gx")
-    for k, ref in enumerate(block_refs):
-        f = lax.rem(gx + (GX - k), GX)
-        out_ref[f] = add_sides(stepped_ref[f] + ref[...], sides_ref[f])
+    for k, step_ref, block_ref in zip(PARTNERS, step_refs, block_refs):
+        out_ref[lax.bitwise_xor(gx, k)] = step_ref[0:CX] + block_ref[...]
     first, second = face(first_ref[F : F + 1])
     left = (first * west_ref[...] + second * first_ref[0:F]) * jnp.where(gx > 0, 1.0, 0.0)
     first, second = face(east_ref[F : F + 1])
@@ -355,10 +360,10 @@
 
 
 def exchange(blocks):
-    moved = {0: blocks[0]}
-    for k in (4, 3, 5, 2, 6, 7, 1):
-        moved[k] = lax.ppermute(blocks[k], "gx", [(i, (i + k) % GX) for i in range(GX)])
-    return [moved[k] for k in range(GX)]
+    return [blocks[0]] + [
+        lax.ppermute(block, "gx", [(i, i ^ k) for i in range(GX)])
+        for k, block in zip(PARTNERS[1:], blocks[1:])
+    ]
 
 
 def scatter_kernel(
@@ -449,31 +454,34 @@
     down_x = [(i + 1, i) for i in range(GX - 1)]
     up_y = [(i, i + 1) for i in range(GY - 1)]
     down_y = [(i + 1, i) for i in range(GY - 1)]
-    stepped, last_x, first_x, last_y, first_y, *blocks = local_kernel(
-        step_kernel,
-        [shape(F, CX, CY), shape(F, CY), shape(16, CY), shape(F, CX), shape(16, CX)]
-        + [shape(CX + 8, CY)] * GX,
+    last_x, first_x, last_y, first_y = local_kernel(
+        edge_kernel,
+        [shape(F, CY), shape(16, CY), shape(F, CX), shape(16, CX)],
         (fields, velocity),
         scratch=[
-            pltpu.VMEM((F, CX, CY), jnp.float32),
-            pltpu.VMEM((2, CX, CY), jnp.float32),
-            pltpu.SemaphoreType.DMA((F + 1,)),
+            pltpu.VMEM((F + 1, CX, CY), jnp.float32),
+            pltpu.VMEM((8, CY), jnp.float32),
+            pltpu.SemaphoreType.DMA((F + 2,)),
         ],
         in_place=True,
         limit=56,
     )
     south = lax.ppermute(last_y, "gy", up_y)
     north = lax.ppermute(first_y, "gy", down_y)
-    blocks = exchange(blocks)
-    sides = local_kernel(side_kernel, [shape(F, 8, CX)], (first_y, last_y, south, north))[0]
-    all_sides = all_to_all(sides, "gx")
+    stepped = local_kernel(
+        step_kernel,
+        [shape(CX + 8, CY)] * GX,
+        (fields, velocity, south, north),
+        scratch=[pltpu.VMEM((F, CX + 8, CY), jnp.float32)],
+    )
+    blocks = exchange(stepped)
     sent = local_kernel(
         forward_kernel,
         [shape(DEV, 1, 768)],
         (
             *blocks,
-            all_sides,
-            *map(jnp.asarray, (*FORE_X, PERIOD, *FORE_Y)),
+            jnp.asarray(FORE),
+            jnp.asarray(PERIOD),
             obs_height[0],
             obs_weight[0],
         ),
@@ -511,7 +519,7 @@
     blocks = local_kernel(
         backward_kernel,
         [shape(CX, CY)] * GX,
-        (back, *map(jnp.asarray, (*BACK_Y, *BACK_X))),
+        (back, jnp.asarray(BACK)),
         flops=3 * 2 * (512 * NX * CY + 512 * 256 * 512),
         scratch=[pltpu.VMEM((MY, 2 * MX), jnp.float32), pltpu.VMEM((NX, CY), jnp.float32)],
     )
@@ -522,9 +530,8 @@
             finish_kernel,
             [shape(F, CX, CY), shape(CX, CY)],
             (
-                stepped,
+                *stepped,
                 *exchange(blocks),
-                sides,
                 west,
                 east,
                 first_x,

time: 131 us -> 126 us (0.962)
  blocking collectives: 8.74 us -> 0 us
  starting transfers between devices: 51.6 us -> 54.9 us
  waiting for transfers between devices: 35.8 us -> 38.7 us
  Pallas kernels: 31.7 us -> 29.6 us
    all_to_all x1 -> x0, blocking collectives: 8.74 us -> none  [all_to_all(): return lax.all_to_all(array, axis, split_axis=0, concat_axis=0, tiled=True)]
    pallas_call x6, Pallas kernels: 15.7 us -> 13.6 us  [local_kernel(): pl.pallas_call(kernel, in_specs=[place] * len(operands), out_specs=[vmem]...]
    ppermute x14, waiting for transfers between devices: 10 us -> 11.9 us  [exchange(): lax.ppermute(block, 'gx', [(i, i ^ k) for i in range(GX)])]
    ppermute x14, starting transfers between devices: 18.6 us -> 20.2 us  [exchange(): lax.ppermute(block, 'gx', [(i, i ^ k) for i in range(GX)])]
  transfers between devices with their start and end apart: 20 -> 20, of which waited for: 5 -> 7; matrix products, arithmetic and copies ran while one was open for 0% -> 0% of each run, Pallas kernels for 12% -> 13%
where the time goes in v4:
time: 126 us
  starting transfers between devices  54.9 us (44%)
  waiting for transfers between devices  38.7 us (31%)
  Pallas kernels  29.6 us (23%)
  local copies, waits for them, and re-layouts  1.39 us (1%)
    all_to_all x2, starting transfers between devices, all_to_all(): return lax.all_to_all(array, axis, split_axis=0, concat_axis=0, tiled=True)  22.9 us
    all_to_all x2, waiting for transfers between devices, all_to_all(): return lax.all_to_all(array, axis, split_axis=0, concat_axis=0, tiled=True)  22.6 us
    ppermute x14, starting transfers between devices, exchange(): lax.ppermute(block, 'gx', [(i, i ^ k) for i in range(GX)])  20.2 us
    pallas_call x2, Pallas kernels, scatter(): pl.pallas_call(scatter_kernel, grid=(steps,), in_specs=[block] * 3 + [pl....  16 us
    pallas_call x6, Pallas kernels, local_kernel(): pl.pallas_call(kernel, in_specs=[place] * len(operands), out_specs=[vmem]...  13.6 us
    ppermute x14, waiting for transfers between devices, exchange(): lax.ppermute(block, 'gx', [(i, i ^ k) for i in range(GX)])  11.9 us
    ppermute x1, starting transfers between devices, body(): south = lax.ppermute(last_y, 'gy', up_y)  4.79 us
    ppermute x1, starting transfers between devices, body(): west = lax.ppermute(last_x, 'gx', up_x)  3.67 us
  transfers between devices with their start and end apart: 20, of which 7 were waited for; matrix products, arithmetic and copies ran while one was open for 0% of the time, Pallas kernels for 13%

profile of v4, /device:TPU:1, one launch (start us, length us, event | category | flops | bytes accessed | tf_op | source)
XLA Modules:
  0.0 125.6 jit_solution(1807483682296175121)
XLA Ops:
  0.6 2.6 %shard_map.149 = (f32[8,256]{1,0:T(8,128)}, f32[16,256]{1,0:T(8,128)}, f32[8,128]{1,0:T(8,128)}, f32[16,128]{1,0:T(8,128)}) custom-call(f32[8,128,256]{2,1,0:T(8,128)} %fields_ref.1, f32[2,128,256]{2,1,0:T(8,128)} %velocity_ref.1), custom_call_target="tpu_custom_call" | custom-call | bytes 1347584 | tf_op jit(solution)/shard_map/pallas_call | solution.py:107
  3.3 1.4 %collective-permute-start.1 = (f32[16,128]{1,0:T(8,128)}, f32[16,128]{1,0:T(8,128)S(1)}, u32[]{:S(2)}, u32[]{:S(2)}) collective-permute-start(f32[16,128]{1,0:T(8,128)} %get-tuple-element.38), channel_id=1, source_target_pairs={{1,0},{2,1},{3,2},{4,3},{5,4},{6,5},{7,6},{8,7},{9,8},{10,9},{11,1... | collective-permute-start | bytes 24584 | tf_op jit(solution)/shard_map/ppermute | solution.py:470
  4.8 4.8 %collective-permute-start = (f32[8,128]{1,0:T(8,128)}, f32[8,128]{1,0:T(8,128)S(1)}, u32[]{:S(2)}, u32[]{:S(2)}) collective-permute-start(f32[8,128]{1,0:T(8,128)} %get-tuple-element.37), channel_id=1, source_target_pairs={{0,1},{1,2},{2,3},{3,4},{4,5},{5,6},{6,7},{7,8},{8,9},{9,10},{10,1... | collective-permute-start | bytes 12296 | tf_op jit(solution)/shard_map/ppermute | solution.py:469
  11.9 1.5 %collective-permute-start.2 = (f32[136,256]{1,0:T(8,128)S(1)}, f32[136,256]{1,0:T(8,128)S(1)}, u32[]{:S(2)}, u32[]{:S(2)}) collective-permute-start(f32[136,256]{1,0:T(8,128)S(1)} %get-tuple-element.40.refs_1_), channel_id=1, source_target_pairs={{0,64},{32,96},{64,0},{96,32},{128,192},{160,224},{192,128},{224,1... | collective-permute-start | bytes 417800 | tf_op jit(solution)/shard_map/ppermute | solution.py:364
  13.4 1.8 %collective-permute-start.3 = (f32[136,256]{1,0:T(8,128)S(1)}, f32[136,256]{1,0:T(8,128)S(1)}, u32[]{:S(2)}, u32[]{:S(2)}) collective-permute-start(f32[136,256]{1,0:T(8,128)S(1)} %get-tuple-element.41.refs_2_), channel_id=1, source_target_pairs={{0,192},{32,224},{64,128},{96,160},{128,64},{160,96},{192,0},{224,... | collective-permute-start | bytes 417800 | tf_op jit(solution)/shard_map/ppermute | solution.py:364
  15.2 2.6 %collective-permute-start.4 = (f32[136,256]{1,0:T(8,128)S(1)}, f32[136,256]{1,0:T(8,128)S(1)}, u32[]{:S(2)}, u32[]{:S(2)}) collective-permute-start(f32[136,256]{1,0:T(8,128)S(1)} %get-tuple-element.42.refs_3_), channel_id=1, source_target_pairs={{0,96},{32,64},{64,32},{96,0},{128,224},{160,192},{192,160},{224,1... | collective-permute-start | bytes 417800 | tf_op jit(solution)/shard_map/ppermute | solution.py:364
  19.9 3.4 %collective-permute-start.7 = (f32[136,256]{1,0:T(8,128)S(1)}, f32[136,256]{1,0:T(8,128)S(1)}, u32[]{:S(2)}, u32[]{:S(2)}) collective-permute-start(f32[136,256]{1,0:T(8,128)S(1)} %get-tuple-element.45.refs_6_), channel_id=1, source_target_pairs={{0,160},{32,128},{64,224},{96,192},{128,32},{160,0},{192,96},{224,... | collective-permute-start | bytes 417800 | tf_op jit(solution)/shard_map/ppermute | solution.py:364
  23.6 6.8 %collective-permute-done.5.refs_4_ = f32[136,256]{1,0:T(8,128)S(1)} collective-permute-done((f32[136,256]{1,0:T(8,128)S(1)}, f32[136,256]{1,0:T(8,128)S(1)}, u32[]{:S(2)}, u32[]{:S(2)}) %collective-permute-start.5) | collective-permute-done | bytes 139296 | tf_op jit(solution)/shard_map/ppermute | solution.py:364
  30.4 3.2 %shard_map.151 = f32[256,1,768]{2,1,0:T(1,128)} custom-call(f32[136,256]{1,0:T(8,128)S(1)} %get-tuple-element.39.refs_0_, f32[136,256]{1,0:T(8,128)S(1)} %collective-permute-done.2.refs_1_, f32[136,256]{1,0:T(8,128)S(1)} %collective-permute-done.3.refs_2_, f32[136,256]{1,0:T(8,128)S(1)} %collective-permute-done.4.refs_3_, ...), custom_call_target="tpu_custom_call" | custom-call | flops 805306368 | bytes 3751936 | tf_op jit(solution)/shard_map/pallas_call | solution.py:107
  33.6 16.5 %all-to-all-start = ((f32[256,1,768]{2,1,0:T(1,128)}), f32[256,1,768]{2,1,0:T(1,128)S(1)}, u32[]{:S(2)}, u32[]{:S(2)}) async-start(f32[256,1,768]{2,1,0:T(1,128)} %shard_map.151), calls=%async_computation | async-start | bytes 1572864 | tf_op jit(solution)/shard_map/all_to_all | solution.py:77
  50.2 3.7 %collective-permute-start.9 = (f32[8,256]{1,0:T(8,128)S(1)}, f32[8,256]{1,0:T(8,128)S(1)}, u32[]{:S(2)}, u32[]{:S(2)}) collective-permute-start(f32[8,256]{1,0:T(8,128)S(1)} %copy-done.4), channel_id=1, source_target_pairs={{0,32},{32,64},{64,96},{96,128},{128,160},{160,192},{192,224},{1,3... | collective-permute-start | bytes 24584 | tf_op jit(solution)/shard_map/ppermute | solution.py:496
  53.9 1.9 %collective-permute-start.10 = (f32[16,256]{1,0:T(8,128)S(1)}, f32[16,256]{1,0:T(8,128)S(1)}, u32[]{:S(2)}, u32[]{:S(2)}) collective-permute-start(f32[16,256]{1,0:T(8,128)S(1)} %copy-done.3), channel_id=1, source_target_pairs={{32,0},{64,32},{96,64},{128,96},{160,128},{192,160},{224,192},{33,... | collective-permute-start | bytes 49160 | tf_op jit(solution)/shard_map/ppermute | solution.py:497
  56.1 3.2 %collective-permute-done.10.refs_17_ = f32[16,256]{1,0:T(8,128)S(1)} collective-permute-done((f32[16,256]{1,0:T(8,128)S(1)}, f32[16,256]{1,0:T(8,128)S(1)}, u32[]{:S(2)}, u32[]{:S(2)}) %collective-permute-start.10) | collective-permute-done | bytes 16416 | tf_op jit(solution)/shard_map/ppermute | solution.py:497
  59.3 16.4 %all-to-all-done.got_ref = f32[256,1,768]{2,1,0:T(1,128)S(1)} async-done(((f32[256,1,768]{2,1,0:T(1,128)}), f32[256,1,768]{2,1,0:T(1,128)S(1)}, u32[]{:S(2)}, u32[]{:S(2)}) %all-to-all-start) | async-done | bytes 786464 | tf_op jit(solution)/shard_map/all_to_all | solution.py:77
  75.7 2.4 %shard_map.152 = f32[256,1,512]{2,1,0:T(1,128)} custom-call(f32[256,1,768]{2,1,0:T(1,128)S(1)} %all-to-all-done.got_ref, f32[2,4,4,32,128]{4,3,2,1,0:T(8,128)S(1)} %copy-done.2, f32[2,8,32,128]{3,2,1,0:T(8,128)S(1)} %bitcast.9, f32[8,128]{1,0:T(8,128)S(1)} %copy-done.5, f32[8,128]{1,0:T(8,128)S(1)} %bitcast.10), custom_call_target="tpu_custom_call" | custom-call | flops 12582912 | bytes 2105344 | tf_op jit(solution)/shard_map/pallas_call | solution.py:107
  78.1 6.4 %all-to-all-start.1 = ((f32[256,1,512]{2,1,0:T(1,128)}), f32[256,1,512]{2,1,0:T(1,128)S(1)}, u32[]{:S(2)}, u32[]{:S(2)}) async-start(f32[256,1,512]{2,1,0:T(1,128)} %shard_map.152), calls=%async_computation.1 | async-start | bytes 1048576 | tf_op jit(solution)/shard_map/all_to_all | solution.py:77
  84.5 13.8 %shard_map.153 = (f32[128,256]{1,0:T(8,128)S(1)}, f32[128,256]{1,0:T(8,128)S(1)}) custom-call(s32[256,128]{1,0:T(8,128)S(1)} %bitcast.13, s32[256,128]{1,0:T(8,128)S(1)} %bitcast.15, f32[256,128]{1,0:T(8,128)S(1)} %fusion.live_ref, f32[256,1,768]{2,1,0:T(1,128)S(1)} %all-to-all-done.got_ref), custom_call_target="tpu_custom_call" | custom-call | flops 11274289152 | bytes 458752 | tf_op jit(solution)/shard_map/pallas_call | solution.py:421
  98.3 6.2 %all-to-all-done.1.got_ref = f32[256,1,512]{2,1,0:T(1,128)S(1)} async-done(((f32[256,1,512]{2,1,0:T(1,128)}), f32[256,1,512]{2,1,0:T(1,128)S(1)}, u32[]{:S(2)}, u32[]{:S(2)}) %all-to-all-start.1) | async-done | bytes 524320 | tf_op jit(solution)/shard_map/all_to_all | solution.py:77
  105.7 2.8 %shard_map.154 = (f32[128,256]{1,0:T(8,128)S(1)}, f32[128,256]{1,0:T(8,128)S(1)}, f32[128,256]{1,0:T(8,128)S(1)}, f32[128,256]{1,0:T(8,128)S(1)}, f32[128,256]{1...) custom-call(f32[256,1,512]{2,1,0:T(1,128)S(1)} %all-to-all-done.1.got_ref, ...), custom_call_target="tpu_custom_call" | custom-call | flops 1207959552 | bytes 3670016 | tf_op jit(solution)/shard_map/pallas_call | solution.py:107
  109.6 1.5 %collective-permute-start.12 = (f32[128,256]{1,0:T(8,128)S(1)}, f32[128,256]{1,0:T(8,128)S(1)}, u32[]{:S(2)}, u32[]{:S(2)}) collective-permute-start(f32[128,256]{1,0:T(8,128)S(1)} %get-tuple-element.58), channel_id=1, source_target_pairs={{0,192},{32,224},{64,128},{96,160},{128,64},{160,96},{192,0},{224,... | collective-permute-start | bytes 393224 | tf_op jit(solution)/shard_map/ppermute | solution.py:364
  113.1 1.5 %collective-permute-start.15 = (f32[128,256]{1,0:T(8,128)S(1)}, f32[128,256]{1,0:T(8,128)S(1)}, u32[]{:S(2)}, u32[]{:S(2)}) collective-permute-start(f32[128,256]{1,0:T(8,128)S(1)} %get-tuple-element.61), channel_id=1, source_target_pairs={{0,128},{32,160},{64,192},{96,224},{128,0},{160,32},{192,64},{224,... | collective-permute-start | bytes 393224 | tf_op jit(solution)/shard_map/ppermute | solution.py:364
  114.6 2.9 %collective-permute-start.16 = (f32[128,256]{1,0:T(8,128)S(1)}, f32[128,256]{1,0:T(8,128)S(1)}, u32[]{:S(2)}, u32[]{:S(2)}) collective-permute-start(f32[128,256]{1,0:T(8,128)S(1)} %get-tuple-element.62), channel_id=1, source_target_pairs={{0,160},{32,128},{64,224},{96,192},{128,32},{160,0},{192,96},{224,... | collective-permute-start | bytes 393224 | tf_op jit(solution)/shard_map/ppermute | solution.py:364
  117.5 2.1 %shard_map.155 = (f32[128,256]{1,0:T(8,128)S(1)}, f32[128,256]{1,0:T(8,128)S(1)}) custom-call(s32[256,128]{1,0:T(8,128)S(1)} %bitcast.14, s32[256,128]{1,0:T(8,128)S(1)} %bitcast.16, f32[256,128]{1,0:T(8,128)S(1)} %fusion.live_ref, f32[256,1,768]{2,1,0:T(1,128)S(1)} %all-to-all-done.got_ref), custom_call_target="tpu_custom_call" | custom-call | flops 1610612736 | bytes 65536 | tf_op jit(solution)/shard_map/pallas_call | solution.py:421
  119.7 4.8 %collective-permute-done.14.refs_12_ = f32[128,256]{1,0:T(8,128)S(1)} collective-permute-done((f32[128,256]{1,0:T(8,128)S(1)}, f32[128,256]{1,0:T(8,128)S(1)}, u32[]{:S(2)}, u32[]{:S(2)}) %collective-permute-start.14) | collective-permute-done | bytes 131104 | tf_op jit(solution)/shard_map/ppermute | solution.py:364
  (58 shorter events, 10.4 us)
Async XLA Ops:
  3.3 27.1 %copy-start.12 = (bf16[1536,256]{1,0:T(8,128)(2,1)S(1)}, bf16[1536,256]{1,0:T(8,128)(2,1)}, u32[]{:S(2)}) copy-start(bf16[1536,256]{1,0:T(8,128)(2,1)} %constant.8.clone.refs_8_) | copy-start | bytes 2359300
  3.3 7.2 %collective-permute-start.1 = (f32[16,128]{1,0:T(8,128)}, f32[16,128]{1,0:T(8,128)S(1)}, u32[]{:S(2)}, u32[]{:S(2)}) collective-permute-start(f32[16,128]{1,0:T(8,128)} %get-tuple-element.38), channel_id=1, source_target_pairs={{1,0},{2,1},{3,2},{4,3},{5,4},{6,5},{7,6},{8,7},{9,8},{10,9},{11,1... | collective-permute-start | bytes 24584 | tf_op jit(solution)/shard_map/ppermute | solution.py:470
  4.8 25.6 %copy-start.7 = (f32[1,256,128]{2,1,0:T(8,128)S(1)}, f32[1,256,128]{2,1,0:T(8,128)}, u32[]{:S(2)}) copy-start(f32[1,256,128]{2,1,0:T(8,128)} %param.19) | copy-start | bytes 393220
  4.8 25.6 %copy-start.8 = (f32[1,256,128]{2,1,0:T(8,128)S(1)}, f32[1,256,128]{2,1,0:T(8,128)}, u32[]{:S(2)}) copy-start(f32[1,256,128]{2,1,0:T(8,128)} %param.20) | copy-start | bytes 393220
  4.8 5.7 %collective-permute-start = (f32[8,128]{1,0:T(8,128)}, f32[8,128]{1,0:T(8,128)S(1)}, u32[]{:S(2)}, u32[]{:S(2)}) collective-permute-start(f32[8,128]{1,0:T(8,128)} %get-tuple-element.37), channel_id=1, source_target_pairs={{0,1},{1,2},{2,3},{3,4},{4,5},{5,6},{6,7},{7,8},{8,9},{9,10},{10,1... | collective-permute-start | bytes 12296 | tf_op jit(solution)/shard_map/ppermute | solution.py:469
  11.9 7.9 %collective-permute-start.2 = (f32[136,256]{1,0:T(8,128)S(1)}, f32[136,256]{1,0:T(8,128)S(1)}, u32[]{:S(2)}, u32[]{:S(2)}) collective-permute-start(f32[136,256]{1,0:T(8,128)S(1)} %get-tuple-element.40.refs_1_), channel_id=1, source_target_pairs={{0,64},{32,96},{64,0},{96,32},{128,192},{160,224},{192,128},{224,1... | collective-permute-start | bytes 417800 | tf_op jit(solution)/shard_map/ppermute | solution.py:364
  13.4 9.9 %collective-permute-start.3 = (f32[136,256]{1,0:T(8,128)S(1)}, f32[136,256]{1,0:T(8,128)S(1)}, u32[]{:S(2)}, u32[]{:S(2)}) collective-permute-start(f32[136,256]{1,0:T(8,128)S(1)} %get-tuple-element.41.refs_2_), channel_id=1, source_target_pairs={{0,192},{32,224},{64,128},{96,160},{128,64},{160,96},{192,0},{224,... | collective-permute-start | bytes 417800 | tf_op jit(solution)/shard_map/ppermute | solution.py:364
  15.2 8.3 %collective-permute-start.4 = (f32[136,256]{1,0:T(8,128)S(1)}, f32[136,256]{1,0:T(8,128)S(1)}, u32[]{:S(2)}, u32[]{:S(2)}) collective-permute-start(f32[136,256]{1,0:T(8,128)S(1)} %get-tuple-element.42.refs_3_), channel_id=1, source_target_pairs={{0,96},{32,64},{64,32},{96,0},{128,224},{160,192},{192,160},{224,1... | collective-permute-start | bytes 417800 | tf_op jit(solution)/shard_map/ppermute | solution.py:364
  17.8 12.6 %collective-permute-start.5 = (f32[136,256]{1,0:T(8,128)S(1)}, f32[136,256]{1,0:T(8,128)S(1)}, u32[]{:S(2)}, u32[]{:S(2)}) collective-permute-start(f32[136,256]{1,0:T(8,128)S(1)} %get-tuple-element.43.refs_4_), channel_id=1, source_target_pairs={{0,224},{32,192},{64,160},{96,128},{128,96},{160,64},{192,32},{224... | collective-permute-start | bytes 417800 | tf_op jit(solution)/shard_map/ppermute | solution.py:364
  18.7 11.7 %collective-permute-start.6 = (f32[136,256]{1,0:T(8,128)S(1)}, f32[136,256]{1,0:T(8,128)S(1)}, u32[]{:S(2)}, u32[]{:S(2)}) collective-permute-start(f32[136,256]{1,0:T(8,128)S(1)} %get-tuple-element.44.refs_5_), channel_id=1, source_target_pairs={{0,128},{32,160},{64,192},{96,224},{128,0},{160,32},{192,64},{224,... | collective-permute-start | bytes 417800 | tf_op jit(solution)/shard_map/ppermute | solution.py:364
  19.9 10.5 %collective-permute-start.7 = (f32[136,256]{1,0:T(8,128)S(1)}, f32[136,256]{1,0:T(8,128)S(1)}, u32[]{:S(2)}, u32[]{:S(2)}) collective-permute-start(f32[136,256]{1,0:T(8,128)S(1)} %get-tuple-element.45.refs_6_), channel_id=1, source_target_pairs={{0,160},{32,128},{64,224},{96,192},{128,32},{160,0},{192,96},{224,... | collective-permute-start | bytes 417800 | tf_op jit(solution)/shard_map/ppermute | solution.py:364
  23.3 7.1 %collective-permute-start.8 = (f32[136,256]{1,0:T(8,128)S(1)}, f32[136,256]{1,0:T(8,128)S(1)}, u32[]{:S(2)}, u32[]{:S(2)}) collective-permute-start(f32[136,256]{1,0:T(8,128)S(1)} %get-tuple-element.46.refs_7_), channel_id=1, source_target_pairs={{0,32},{32,0},{64,96},{96,64},{128,160},{160,128},{192,224},{224,1... | collective-permute-start | bytes 417800 | tf_op jit(solution)/shard_map/ppermute | solution.py:364
  33.6 42.1 %all-to-all-start = ((f32[256,1,768]{2,1,0:T(1,128)}), f32[256,1,768]{2,1,0:T(1,128)S(1)}, u32[]{:S(2)}, u32[]{:S(2)}) async-start(f32[256,1,768]{2,1,0:T(1,128)} %shard_map.151), calls=%async_computation | async-start | bytes 1572864 | tf_op jit(solution)/shard_map/all_to_all | solution.py:77
  50.2 25.5 %copy-start.2 = (f32[2,4,4,32,128]{4,3,2,1,0:T(8,128)S(1)}, f32[2,4,4,32,128]{4,3,2,1,0:T(8,128)}, u32[]{:S(2)}) copy-start(f32[2,4,4,32,128]{4,3,2,1,0:T(8,128)} %constant.10.clone.turn_ref) | copy-start | bytes 1572868
  50.2 5.9 %collective-permute-start.9 = (f32[8,256]{1,0:T(8,128)S(1)}, f32[8,256]{1,0:T(8,128)S(1)}, u32[]{:S(2)}, u32[]{:S(2)}) collective-permute-start(f32[8,256]{1,0:T(8,128)S(1)} %copy-done.4), channel_id=1, source_target_pairs={{0,32},{32,64},{64,96},{96,128},{128,160},{160,192},{192,224},{1,3... | collective-permute-start | bytes 24584 | tf_op jit(solution)/shard_map/ppermute | solution.py:496
  53.9 5.4 %collective-permute-start.10 = (f32[16,256]{1,0:T(8,128)S(1)}, f32[16,256]{1,0:T(8,128)S(1)}, u32[]{:S(2)}, u32[]{:S(2)}) collective-permute-start(f32[16,256]{1,0:T(8,128)S(1)} %copy-done.3), channel_id=1, source_target_pairs={{32,0},{64,32},{96,64},{128,96},{160,128},{192,160},{224,192},{33,... | collective-permute-start | bytes 49160 | tf_op jit(solution)/shard_map/ppermute | solution.py:497
  78.1 26.4 %all-to-all-start.1 = ((f32[256,1,512]{2,1,0:T(1,128)}), f32[256,1,512]{2,1,0:T(1,128)S(1)}, u32[]{:S(2)}, u32[]{:S(2)}) async-start(f32[256,1,512]{2,1,0:T(1,128)} %shard_map.152), calls=%async_computation.1 | async-start | bytes 1048576 | tf_op jit(solution)/shard_map/all_to_all | solution.py:77
  108.6 6.1 %collective-permute-start.11 = (f32[128,256]{1,0:T(8,128)S(1)}, f32[128,256]{1,0:T(8,128)S(1)}, u32[]{:S(2)}, u32[]{:S(2)}) collective-permute-start(f32[128,256]{1,0:T(8,128)S(1)} %get-tuple-element.57), channel_id=1, source_target_pairs={{0,64},{32,96},{64,0},{96,32},{128,192},{160,224},{192,128},{224,1... | collective-permute-start | bytes 393224 | tf_op jit(solution)/shard_map/ppermute | solution.py:364
  109.6 7.9 %collective-permute-start.12 = (f32[128,256]{1,0:T(8,128)S(1)}, f32[128,256]{1,0:T(8,128)S(1)}, u32[]{:S(2)}, u32[]{:S(2)}) collective-permute-start(f32[128,256]{1,0:T(8,128)S(1)} %get-tuple-element.58), channel_id=1, source_target_pairs={{0,192},{32,224},{64,128},{96,160},{128,64},{160,96},{192,0},{224,... | collective-permute-start | bytes 393224 | tf_op jit(solution)/shard_map/ppermute | solution.py:364
  111.1 8.6 %collective-permute-start.13 = (f32[128,256]{1,0:T(8,128)S(1)}, f32[128,256]{1,0:T(8,128)S(1)}, u32[]{:S(2)}, u32[]{:S(2)}) collective-permute-start(f32[128,256]{1,0:T(8,128)S(1)} %get-tuple-element.59), channel_id=1, source_target_pairs={{0,96},{32,64},{64,32},{96,0},{128,224},{160,192},{192,160},{224,1... | collective-permute-start | bytes 393224 | tf_op jit(solution)/shard_map/ppermute | solution.py:364
  111.9 12.6 %collective-permute-start.14 = (f32[128,256]{1,0:T(8,128)S(1)}, f32[128,256]{1,0:T(8,128)S(1)}, u32[]{:S(2)}, u32[]{:S(2)}) collective-permute-start(f32[128,256]{1,0:T(8,128)S(1)} %get-tuple-element.60), channel_id=1, source_target_pairs={{0,224},{32,192},{64,160},{96,128},{128,96},{160,64},{192,32},{224... | collective-permute-start | bytes 393224 | tf_op jit(solution)/shard_map/ppermute | solution.py:364
  113.1 11.3 %collective-permute-start.15 = (f32[128,256]{1,0:T(8,128)S(1)}, f32[128,256]{1,0:T(8,128)S(1)}, u32[]{:S(2)}, u32[]{:S(2)}) collective-permute-start(f32[128,256]{1,0:T(8,128)S(1)} %get-tuple-element.61), channel_id=1, source_target_pairs={{0,128},{32,160},{64,192},{96,224},{128,0},{160,32},{192,64},{224,... | collective-permute-start | bytes 393224 | tf_op jit(solution)/shard_map/ppermute | solution.py:364
  114.6 9.8 %collective-permute-start.16 = (f32[128,256]{1,0:T(8,128)S(1)}, f32[128,256]{1,0:T(8,128)S(1)}, u32[]{:S(2)}, u32[]{:S(2)}) collective-permute-start(f32[128,256]{1,0:T(8,128)S(1)} %get-tuple-element.62), channel_id=1, source_target_pairs={{0,160},{32,128},{64,224},{96,192},{128,32},{160,0},{192,96},{224,... | collective-permute-start | bytes 393224 | tf_op jit(solution)/shard_map/ppermute | solution.py:364
  117.5 6.9 %collective-permute-start.17 = (f32[128,256]{1,0:T(8,128)S(1)}, f32[128,256]{1,0:T(8,128)S(1)}, u32[]{:S(2)}, u32[]{:S(2)}) collective-permute-start(f32[128,256]{1,0:T(8,128)S(1)} %get-tuple-element.63), channel_id=1, source_target_pairs={{0,32},{32,0},{64,96},{96,64},{128,160},{160,128},{192,224},{224,1... | collective-permute-start | bytes 393224 | tf_op jit(solution)/shard_map/ppermute | solution.py:364
  (12 other events, 173.0 us)

commit v5 on v4

--- a/solution.py
+++ b/solution.py
@@ -123,7 +123,7 @@
 
 
 def edge_kernel(
-    fields_hbm, velocity_hbm, last_x_ref, first_x_ref, last_y_ref, first_y_ref, block_ref, row_ref, sems
+    fields_hbm, velocity_hbm, last_x_ref, first_x_ref, even_ref, odd_ref, block_ref, row_ref, sems
 ):
     copies = [
         pltpu.make_async_copy(fields_hbm.at[f], block_ref.at[f], sems.at[f]) for f in range(F)
@@ -148,13 +148,15 @@
             last_x_ref[f : f + 1] = block_ref[f, CX - 1 : CX]
             first_x_ref[f : f + 1] = block_ref[f, 0:1]
     sides = jnp.transpose(sides)
-    first_y_ref[...] = sides[0:16]
-    last_y_ref[...] = sides[16 : 16 + F]
+    is_even = lax.rem(lax.axis_index("gy"), 2) == 0
+    first, last = sides[0:16], sides[16:32]
+    even_ref[...] = jnp.where(is_even, last, first)
+    odd_ref[...] = jnp.where(is_even, first, last)
     copies[F + 1].wait()
     first_x_ref[F : F + 1] = row_ref[0:1]
 
 
-def step_kernel(fields_ref, velocity_ref, south_ref, north_ref, *refs):
+def step_kernel(fields_ref, velocity_ref, even_ref, odd_ref, *refs):
     *block_refs, held_ref = refs
     row = lax.broadcasted_iota(jnp.int32, (CX, CY), 0)
     col = lax.broadcasted_iota(jnp.int32, (CX, CY), 1)
@@ -162,8 +164,9 @@
     gx, gy = lax.axis_index("gx"), lax.axis_index("gy")
     open_s = jnp.where(gy > 0, 1.0, 0.0)
     open_n = jnp.where(gy < GY - 1, 1.0, 0.0)
-    before = jnp.transpose(south_ref[...])
-    after = jnp.transpose(north_ref[...])
+    is_even = lax.rem(gy, 2) == 0
+    before = jnp.transpose(jnp.where(is_even, odd_ref[...], even_ref[...]))
+    after = jnp.transpose(jnp.where(is_even, even_ref[...], odd_ref[...]))
     low_w, high_w = (jnp.where(row == 0, 0.0, value) for value in face(velocity_ref[0]))
     low_e, high_e = (
         jnp.where(row == CX - 1, 0.0, pltpu.roll(value, CX - 1, 0)) for value in (low_w, high_w)
@@ -452,11 +455,11 @@
 ):
     up_x = [(i, i + 1) for i in range(GX - 1)]
     down_x = [(i + 1, i) for i in range(GX - 1)]
-    up_y = [(i, i + 1) for i in range(GY - 1)]
-    down_y = [(i + 1, i) for i in range(GY - 1)]
-    last_x, first_x, last_y, first_y = local_kernel(
+    even_pairs = [(i, i ^ 1) for i in range(GY)]
+    odd_pairs = [(i, (i + 1) % GY if i % 2 else (i - 1) % GY) for i in range(GY)]
+    last_x, first_x, even, odd = local_kernel(
         edge_kernel,
-        [shape(F, CY), shape(16, CY), shape(F, CX), shape(16, CX)],
+        [shape(F, CY), shape(16, CY), shape(16, CX), shape(16, CX)],
         (fields, velocity),
         scratch=[
             pltpu.VMEM((F + 1, CX, CY), jnp.float32),
@@ -466,12 +469,12 @@
         in_place=True,
         limit=56,
     )
-    south = lax.ppermute(last_y, "gy", up_y)
-    north = lax.ppermute(first_y, "gy", down_y)
+    even = lax.ppermute(even, "gy", even_pairs)
+    odd = lax.ppermute(odd, "gy", odd_pairs)
     stepped = local_kernel(
         step_kernel,
         [shape(CX + 8, CY)] * GX,
-        (fields, velocity, south, north),
+        (fields, velocity, even, odd),
         scratch=[pltpu.VMEM((F, CX + 8, CY), jnp.float32)],
     )
     blocks = exchange(stepped)

time: 126 us -> 121 us (0.960)
  starting transfers between devices: 54.9 us -> 49.8 us
    all_to_all x2, starting transfers between devices: 22.9 us -> 15.3 us  [all_to_all(): return lax.all_to_all(array, axis, split_axis=0, concat_axis=0, tiled=True)]
    ppermute x2, starting transfers between devices: 6.21 us -> 9.41 us  [the longest x1 7.19 us: body(): odd = lax.ppermute(odd, 'gy', odd_pairs)]
  transfers between devices with their start and end apart: 20 -> 20, of which waited for: 7 -> 6; matrix products, arithmetic and copies ran while one was open for 0% -> 0% of each run, Pallas kernels for 13% -> 13%
where the time goes in v5:
time: 121 us
  starting transfers between devices  49.8 us (41%)
  waiting for transfers between devices  39.3 us (32%)
  Pallas kernels  29.6 us (24%)
  local copies, waits for them, and re-layouts  1.38 us (1%)
    all_to_all x2, waiting for transfers between devices, all_to_all(): return lax.all_to_all(array, axis, split_axis=0, concat_axis=0, tiled=True)  22.6 us
    ppermute x14, starting transfers between devices, exchange(): lax.ppermute(block, 'gx', [(i, i ^ k) for i in range(GX)])  19.5 us
    pallas_call x2, Pallas kernels, scatter(): pl.pallas_call(scatter_kernel, grid=(steps,), in_specs=[block] * 3 + [pl....  16 us
    all_to_all x2, starting transfers between devices, all_to_all(): return lax.all_to_all(array, axis, split_axis=0, concat_axis=0, tiled=True)  15.3 us
    pallas_call x6, Pallas kernels, local_kernel(): pl.pallas_call(kernel, in_specs=[place] * len(operands), out_specs=[vmem]...  13.6 us
    ppermute x14, waiting for transfers between devices, exchange(): lax.ppermute(block, 'gx', [(i, i ^ k) for i in range(GX)])  12.2 us
    ppermute x1, starting transfers between devices, body(): odd = lax.ppermute(odd, 'gy', odd_pairs)  7.19 us
    ppermute x1, starting transfers between devices, body(): west = lax.ppermute(last_x, 'gx', up_x)  3.67 us
  transfers between devices with their start and end apart: 20, of which 6 were waited for; matrix products, arithmetic and copies ran while one was open for 0% of the time, Pallas kernels for 13%

profile of v5, /device:TPU:1, one launch (start us, length us, event | category | flops | bytes accessed | tf_op | source)
XLA Modules:
  0.0 121.0 jit_solution(4538625301749829632)
XLA Ops:
  0.6 2.7 %shard_map.149 = (f32[8,256]{1,0:T(8,128)}, f32[16,256]{1,0:T(8,128)}, f32[16,128]{1,0:T(8,128)}, f32[16,128]{1,0:T(8,128)}) custom-call(f32[8,128,256]{2,1,0:T(8,128)} %fields_ref.1, f32[2,128,256]{2,1,0:T(8,128)} %velocity_ref.1), custom_call_target="tpu_custom_call" | custom-call | bytes 1351680 | tf_op jit(solution)/shard_map/pallas_call | solution.py:107
  3.3 2.2 %collective-permute-start = (f32[16,128]{1,0:T(8,128)}, f32[16,128]{1,0:T(8,128)S(1)}, u32[]{:S(2)}, u32[]{:S(2)}) collective-permute-start(f32[16,128]{1,0:T(8,128)} %get-tuple-element.37), channel_id=1, source_target_pairs={{0,1},{1,0},{2,3},{3,2},{4,5},{5,4},{6,7},{7,6},{8,9},{9,8},{10,11... | collective-permute-start | bytes 24584 | tf_op jit(solution)/shard_map/ppermute | solution.py:472
  5.5 7.2 %collective-permute-start.1 = (f32[16,128]{1,0:T(8,128)}, f32[16,128]{1,0:T(8,128)S(1)}, u32[]{:S(2)}, u32[]{:S(2)}) collective-permute-start(f32[16,128]{1,0:T(8,128)} %get-tuple-element.38), channel_id=1, source_target_pairs={{0,31},{1,2},{2,1},{3,4},{4,3},{5,6},{6,5},{7,8},{8,7},{9,10},{10,... | collective-permute-start | bytes 24584 | tf_op jit(solution)/shard_map/ppermute | solution.py:473
  14.0 1.4 %shard_map.150 = (f32[136,256]{1,0:T(8,128)S(1)}, f32[136,256]{1,0:T(8,128)S(1)}, f32[136,256]{1,0:T(8,128)S(1)}, f32[136,256]{1,0:T(8,128)S(1)}, f32[136,256]{1...) custom-call(f32[8,128,256]{2,1,0:T(8,128)S(1)} %copy-done, ...), custom_call_target="tpu_custom_call" | custom-call | bytes 2441216 | tf_op jit(solution)/shard_map/pallas_call | solution.py:107
  16.7 1.8 %collective-permute-start.3 = (f32[136,256]{1,0:T(8,128)S(1)}, f32[136,256]{1,0:T(8,128)S(1)}, u32[]{:S(2)}, u32[]{:S(2)}) collective-permute-start(f32[136,256]{1,0:T(8,128)S(1)} %get-tuple-element.41.refs_2_), channel_id=1, source_target_pairs={{0,192},{32,224},{64,128},{96,160},{128,64},{160,96},{192,0},{224,... | collective-permute-start | bytes 417800 | tf_op jit(solution)/shard_map/ppermute | solution.py:367
  18.5 2.6 %collective-permute-start.4 = (f32[136,256]{1,0:T(8,128)S(1)}, f32[136,256]{1,0:T(8,128)S(1)}, u32[]{:S(2)}, u32[]{:S(2)}) collective-permute-start(f32[136,256]{1,0:T(8,128)S(1)} %get-tuple-element.42.refs_3_), channel_id=1, source_target_pairs={{0,96},{32,64},{64,32},{96,0},{128,224},{160,192},{192,160},{224,1... | collective-permute-start | bytes 417800 | tf_op jit(solution)/shard_map/ppermute | solution.py:367
  22.9 3.0 %collective-permute-start.7 = (f32[136,256]{1,0:T(8,128)S(1)}, f32[136,256]{1,0:T(8,128)S(1)}, u32[]{:S(2)}, u32[]{:S(2)}) collective-permute-start(f32[136,256]{1,0:T(8,128)S(1)} %get-tuple-element.45.refs_6_), channel_id=1, source_target_pairs={{0,160},{32,128},{64,224},{96,192},{128,32},{160,0},{192,96},{224,... | collective-permute-start | bytes 417800 | tf_op jit(solution)/shard_map/ppermute | solution.py:367
  25.9 7.4 %collective-permute-done.5.refs_4_ = f32[136,256]{1,0:T(8,128)S(1)} collective-permute-done((f32[136,256]{1,0:T(8,128)S(1)}, f32[136,256]{1,0:T(8,128)S(1)}, u32[]{:S(2)}, u32[]{:S(2)}) %collective-permute-start.5) | collective-permute-done | bytes 139296 | tf_op jit(solution)/shard_map/ppermute | solution.py:367
  33.4 3.2 %shard_map.151 = f32[256,1,768]{2,1,0:T(1,128)} custom-call(f32[136,256]{1,0:T(8,128)S(1)} %get-tuple-element.39.refs_0_, f32[136,256]{1,0:T(8,128)S(1)} %collective-permute-done.2.refs_1_, f32[136,256]{1,0:T(8,128)S(1)} %collective-permute-done.3.refs_2_, f32[136,256]{1,0:T(8,128)S(1)} %collective-permute-done.4.refs_3_, ...), custom_call_target="tpu_custom_call" | custom-call | flops 805306368 | bytes 3751936 | tf_op jit(solution)/shard_map/pallas_call | solution.py:107
  36.6 9.0 %all-to-all-start = ((f32[256,1,768]{2,1,0:T(1,128)}), f32[256,1,768]{2,1,0:T(1,128)S(1)}, u32[]{:S(2)}, u32[]{:S(2)}) async-start(f32[256,1,768]{2,1,0:T(1,128)} %shard_map.151), calls=%async_computation | async-start | bytes 1572864 | tf_op jit(solution)/shard_map/all_to_all | solution.py:77
  45.6 3.7 %collective-permute-start.9 = (f32[8,256]{1,0:T(8,128)S(1)}, f32[8,256]{1,0:T(8,128)S(1)}, u32[]{:S(2)}, u32[]{:S(2)}) collective-permute-start(f32[8,256]{1,0:T(8,128)S(1)} %copy-done.4), channel_id=1, source_target_pairs={{0,32},{32,64},{64,96},{96,128},{128,160},{160,192},{192,224},{1,3... | collective-permute-start | bytes 24584 | tf_op jit(solution)/shard_map/ppermute | solution.py:499
  49.3 1.9 %collective-permute-start.10 = (f32[16,256]{1,0:T(8,128)S(1)}, f32[16,256]{1,0:T(8,128)S(1)}, u32[]{:S(2)}, u32[]{:S(2)}) collective-permute-start(f32[16,256]{1,0:T(8,128)S(1)} %copy-done.3), channel_id=1, source_target_pairs={{32,0},{64,32},{96,64},{128,96},{160,128},{192,160},{224,192},{33,... | collective-permute-start | bytes 49160 | tf_op jit(solution)/shard_map/ppermute | solution.py:500
  51.5 3.2 %collective-permute-done.10.refs_17_ = f32[16,256]{1,0:T(8,128)S(1)} collective-permute-done((f32[16,256]{1,0:T(8,128)S(1)}, f32[16,256]{1,0:T(8,128)S(1)}, u32[]{:S(2)}, u32[]{:S(2)}) %collective-permute-start.10) | collective-permute-done | bytes 16416 | tf_op jit(solution)/shard_map/ppermute | solution.py:500
  54.7 16.4 %all-to-all-done.got_ref = f32[256,1,768]{2,1,0:T(1,128)S(1)} async-done(((f32[256,1,768]{2,1,0:T(1,128)}), f32[256,1,768]{2,1,0:T(1,128)S(1)}, u32[]{:S(2)}, u32[]{:S(2)}) %all-to-all-start) | async-done | bytes 786464 | tf_op jit(solution)/shard_map/all_to_all | solution.py:77
  71.1 2.4 %shard_map.152 = f32[256,1,512]{2,1,0:T(1,128)} custom-call(f32[256,1,768]{2,1,0:T(1,128)S(1)} %all-to-all-done.got_ref, f32[2,4,4,32,128]{4,3,2,1,0:T(8,128)S(1)} %copy-done.2, f32[2,8,32,128]{3,2,1,0:T(8,128)S(1)} %bitcast.9, f32[8,128]{1,0:T(8,128)S(1)} %copy-done.5, f32[8,128]{1,0:T(8,128)S(1)} %bitcast.10), custom_call_target="tpu_custom_call" | custom-call | flops 12582912 | bytes 2105344 | tf_op jit(solution)/shard_map/pallas_call | solution.py:107
  73.5 6.3 %all-to-all-start.1 = ((f32[256,1,512]{2,1,0:T(1,128)}), f32[256,1,512]{2,1,0:T(1,128)S(1)}, u32[]{:S(2)}, u32[]{:S(2)}) async-start(f32[256,1,512]{2,1,0:T(1,128)} %shard_map.152), calls=%async_computation.1 | async-start | bytes 1048576 | tf_op jit(solution)/shard_map/all_to_all | solution.py:77
  79.9 13.8 %shard_map.153 = (f32[128,256]{1,0:T(8,128)S(1)}, f32[128,256]{1,0:T(8,128)S(1)}) custom-call(s32[256,128]{1,0:T(8,128)S(1)} %bitcast.13, s32[256,128]{1,0:T(8,128)S(1)} %bitcast.15, f32[256,128]{1,0:T(8,128)S(1)} %fusion.live_ref, f32[256,1,768]{2,1,0:T(1,128)S(1)} %all-to-all-done.got_ref), custom_call_target="tpu_custom_call" | custom-call | flops 11274289152 | bytes 458752 | tf_op jit(solution)/shard_map/pallas_call | solution.py:424
  93.7 6.2 %all-to-all-done.1.got_ref = f32[256,1,512]{2,1,0:T(1,128)S(1)} async-done(((f32[256,1,512]{2,1,0:T(1,128)}), f32[256,1,512]{2,1,0:T(1,128)S(1)}, u32[]{:S(2)}, u32[]{:S(2)}) %all-to-all-start.1) | async-done | bytes 524320 | tf_op jit(solution)/shard_map/all_to_all | solution.py:77
  101.1 2.8 %shard_map.154 = (f32[128,256]{1,0:T(8,128)S(1)}, f32[128,256]{1,0:T(8,128)S(1)}, f32[128,256]{1,0:T(8,128)S(1)}, f32[128,256]{1,0:T(8,128)S(1)}, f32[128,256]{1...) custom-call(f32[256,1,512]{2,1,0:T(1,128)S(1)} %all-to-all-done.1.got_ref, ...), custom_call_target="tpu_custom_call" | custom-call | flops 1207959552 | bytes 3670016 | tf_op jit(solution)/shard_map/pallas_call | solution.py:107
  105.0 1.5 %collective-permute-start.12 = (f32[128,256]{1,0:T(8,128)S(1)}, f32[128,256]{1,0:T(8,128)S(1)}, u32[]{:S(2)}, u32[]{:S(2)}) collective-permute-start(f32[128,256]{1,0:T(8,128)S(1)} %get-tuple-element.58), channel_id=1, source_target_pairs={{0,192},{32,224},{64,128},{96,160},{128,64},{160,96},{192,0},{224,... | collective-permute-start | bytes 393224 | tf_op jit(solution)/shard_map/ppermute | solution.py:367
  108.5 1.5 %collective-permute-start.15 = (f32[128,256]{1,0:T(8,128)S(1)}, f32[128,256]{1,0:T(8,128)S(1)}, u32[]{:S(2)}, u32[]{:S(2)}) collective-permute-start(f32[128,256]{1,0:T(8,128)S(1)} %get-tuple-element.61), channel_id=1, source_target_pairs={{0,128},{32,160},{64,192},{96,224},{128,0},{160,32},{192,64},{224,... | collective-permute-start | bytes 393224 | tf_op jit(solution)/shard_map/ppermute | solution.py:367
  110.0 2.9 %collective-permute-start.16 = (f32[128,256]{1,0:T(8,128)S(1)}, f32[128,256]{1,0:T(8,128)S(1)}, u32[]{:S(2)}, u32[]{:S(2)}) collective-permute-start(f32[128,256]{1,0:T(8,128)S(1)} %get-tuple-element.62), channel_id=1, source_target_pairs={{0,160},{32,128},{64,224},{96,192},{128,32},{160,0},{192,96},{224,... | collective-permute-start | bytes 393224 | tf_op jit(solution)/shard_map/ppermute | solution.py:367
  112.9 2.1 %shard_map.155 = (f32[128,256]{1,0:T(8,128)S(1)}, f32[128,256]{1,0:T(8,128)S(1)}) custom-call(s32[256,128]{1,0:T(8,128)S(1)} %bitcast.14, s32[256,128]{1,0:T(8,128)S(1)} %bitcast.16, f32[256,128]{1,0:T(8,128)S(1)} %fusion.live_ref, f32[256,1,768]{2,1,0:T(1,128)S(1)} %all-to-all-done.got_ref), custom_call_target="tpu_custom_call" | custom-call | flops 1610612736 | bytes 65536 | tf_op jit(solution)/shard_map/pallas_call | solution.py:424
  115.1 4.8 %collective-permute-done.14.refs_12_ = f32[128,256]{1,0:T(8,128)S(1)} collective-permute-done((f32[128,256]{1,0:T(8,128)S(1)}, f32[128,256]{1,0:T(8,128)S(1)}, u32[]{:S(2)}, u32[]{:S(2)}) %collective-permute-start.14) | collective-permute-done | bytes 131104 | tf_op jit(solution)/shard_map/ppermute | solution.py:367
  (58 shorter events, 10.1 us)
Async XLA Ops:
  3.3 30.0 %copy-start.12 = (bf16[1536,256]{1,0:T(8,128)(2,1)S(1)}, bf16[1536,256]{1,0:T(8,128)(2,1)}, u32[]{:S(2)}) copy-start(bf16[1536,256]{1,0:T(8,128)(2,1)} %constant.8.clone.refs_8_) | copy-start | bytes 2359300
  3.3 9.4 %collective-permute-start = (f32[16,128]{1,0:T(8,128)}, f32[16,128]{1,0:T(8,128)S(1)}, u32[]{:S(2)}, u32[]{:S(2)}) collective-permute-start(f32[16,128]{1,0:T(8,128)} %get-tuple-element.37), channel_id=1, source_target_pairs={{0,1},{1,0},{2,3},{3,2},{4,5},{5,4},{6,7},{7,6},{8,9},{9,8},{10,11... | collective-permute-start | bytes 24584 | tf_op jit(solution)/shard_map/ppermute | solution.py:472
  5.5 27.8 %copy-start.7 = (f32[1,256,128]{2,1,0:T(8,128)S(1)}, f32[1,256,128]{2,1,0:T(8,128)}, u32[]{:S(2)}) copy-start(f32[1,256,128]{2,1,0:T(8,128)} %param.19) | copy-start | bytes 393220
  5.5 27.8 %copy-start.8 = (f32[1,256,128]{2,1,0:T(8,128)S(1)}, f32[1,256,128]{2,1,0:T(8,128)}, u32[]{:S(2)}) copy-start(f32[1,256,128]{2,1,0:T(8,128)} %param.20) | copy-start | bytes 393220
  5.5 8.4 %collective-permute-start.1 = (f32[16,128]{1,0:T(8,128)}, f32[16,128]{1,0:T(8,128)S(1)}, u32[]{:S(2)}, u32[]{:S(2)}) collective-permute-start(f32[16,128]{1,0:T(8,128)} %get-tuple-element.38), channel_id=1, source_target_pairs={{0,31},{1,2},{2,1},{3,4},{4,3},{5,6},{6,5},{7,8},{8,7},{9,10},{10,... | collective-permute-start | bytes 24584 | tf_op jit(solution)/shard_map/ppermute | solution.py:473
  15.4 7.5 %collective-permute-start.2 = (f32[136,256]{1,0:T(8,128)S(1)}, f32[136,256]{1,0:T(8,128)S(1)}, u32[]{:S(2)}, u32[]{:S(2)}) collective-permute-start(f32[136,256]{1,0:T(8,128)S(1)} %get-tuple-element.40.refs_1_), channel_id=1, source_target_pairs={{0,64},{32,96},{64,0},{96,32},{128,192},{160,224},{192,128},{224,1... | collective-permute-start | bytes 417800 | tf_op jit(solution)/shard_map/ppermute | solution.py:367
  16.7 9.2 %collective-permute-start.3 = (f32[136,256]{1,0:T(8,128)S(1)}, f32[136,256]{1,0:T(8,128)S(1)}, u32[]{:S(2)}, u32[]{:S(2)}) collective-permute-start(f32[136,256]{1,0:T(8,128)S(1)} %get-tuple-element.41.refs_2_), channel_id=1, source_target_pairs={{0,192},{32,224},{64,128},{96,160},{128,64},{160,96},{192,0},{224,... | collective-permute-start | bytes 417800 | tf_op jit(solution)/shard_map/ppermute | solution.py:367
  18.5 7.4 %collective-permute-start.4 = (f32[136,256]{1,0:T(8,128)S(1)}, f32[136,256]{1,0:T(8,128)S(1)}, u32[]{:S(2)}, u32[]{:S(2)}) collective-permute-start(f32[136,256]{1,0:T(8,128)S(1)} %get-tuple-element.42.refs_3_), channel_id=1, source_target_pairs={{0,96},{32,64},{64,32},{96,0},{128,224},{160,192},{192,160},{224,1... | collective-permute-start | bytes 417800 | tf_op jit(solution)/shard_map/ppermute | solution.py:367
  21.1 12.3 %collective-permute-start.5 = (f32[136,256]{1,0:T(8,128)S(1)}, f32[136,256]{1,0:T(8,128)S(1)}, u32[]{:S(2)}, u32[]{:S(2)}) collective-permute-start(f32[136,256]{1,0:T(8,128)S(1)} %get-tuple-element.43.refs_4_), channel_id=1, source_target_pairs={{0,224},{32,192},{64,160},{96,128},{128,96},{160,64},{192,32},{224... | collective-permute-start | bytes 417800 | tf_op jit(solution)/shard_map/ppermute | solution.py:367
  21.6 11.7 %collective-permute-start.6 = (f32[136,256]{1,0:T(8,128)S(1)}, f32[136,256]{1,0:T(8,128)S(1)}, u32[]{:S(2)}, u32[]{:S(2)}) collective-permute-start(f32[136,256]{1,0:T(8,128)S(1)} %get-tuple-element.44.refs_5_), channel_id=1, source_target_pairs={{0,128},{32,160},{64,192},{96,224},{128,0},{160,32},{192,64},{224,... | collective-permute-start | bytes 417800 | tf_op jit(solution)/shard_map/ppermute | solution.py:367
  22.9 10.5 %collective-permute-start.7 = (f32[136,256]{1,0:T(8,128)S(1)}, f32[136,256]{1,0:T(8,128)S(1)}, u32[]{:S(2)}, u32[]{:S(2)}) collective-permute-start(f32[136,256]{1,0:T(8,128)S(1)} %get-tuple-element.45.refs_6_), channel_id=1, source_target_pairs={{0,160},{32,128},{64,224},{96,192},{128,32},{160,0},{192,96},{224,... | collective-permute-start | bytes 417800 | tf_op jit(solution)/shard_map/ppermute | solution.py:367
  25.9 7.5 %collective-permute-start.8 = (f32[136,256]{1,0:T(8,128)S(1)}, f32[136,256]{1,0:T(8,128)S(1)}, u32[]{:S(2)}, u32[]{:S(2)}) collective-permute-start(f32[136,256]{1,0:T(8,128)S(1)} %get-tuple-element.46.refs_7_), channel_id=1, source_target_pairs={{0,32},{32,0},{64,96},{96,64},{128,160},{160,128},{192,224},{224,1... | collective-permute-start | bytes 417800 | tf_op jit(solution)/shard_map/ppermute | solution.py:367
  36.6 34.5 %all-to-all-start = ((f32[256,1,768]{2,1,0:T(1,128)}), f32[256,1,768]{2,1,0:T(1,128)S(1)}, u32[]{:S(2)}, u32[]{:S(2)}) async-start(f32[256,1,768]{2,1,0:T(1,128)} %shard_map.151), calls=%async_computation | async-start | bytes 1572864 | tf_op jit(solution)/shard_map/all_to_all | solution.py:77
  45.6 25.5 %copy-start.2 = (f32[2,4,4,32,128]{4,3,2,1,0:T(8,128)S(1)}, f32[2,4,4,32,128]{4,3,2,1,0:T(8,128)}, u32[]{:S(2)}) copy-start(f32[2,4,4,32,128]{4,3,2,1,0:T(8,128)} %constant.10.clone.turn_ref) | copy-start | bytes 1572868
  45.6 5.9 %collective-permute-start.9 = (f32[8,256]{1,0:T(8,128)S(1)}, f32[8,256]{1,0:T(8,128)S(1)}, u32[]{:S(2)}, u32[]{:S(2)}) collective-permute-start(f32[8,256]{1,0:T(8,128)S(1)} %copy-done.4), channel_id=1, source_target_pairs={{0,32},{32,64},{64,96},{96,128},{128,160},{160,192},{192,224},{1,3... | collective-permute-start | bytes 24584 | tf_op jit(solution)/shard_map/ppermute | solution.py:499
  49.3 5.4 %collective-permute-start.10 = (f32[16,256]{1,0:T(8,128)S(1)}, f32[16,256]{1,0:T(8,128)S(1)}, u32[]{:S(2)}, u32[]{:S(2)}) collective-permute-start(f32[16,256]{1,0:T(8,128)S(1)} %copy-done.3), channel_id=1, source_target_pairs={{32,0},{64,32},{96,64},{128,96},{160,128},{192,160},{224,192},{33,... | collective-permute-start | bytes 49160 | tf_op jit(solution)/shard_map/ppermute | solution.py:500
  73.5 26.4 %all-to-all-start.1 = ((f32[256,1,512]{2,1,0:T(1,128)}), f32[256,1,512]{2,1,0:T(1,128)S(1)}, u32[]{:S(2)}, u32[]{:S(2)}) async-start(f32[256,1,512]{2,1,0:T(1,128)} %shard_map.152), calls=%async_computation.1 | async-start | bytes 1048576 | tf_op jit(solution)/shard_map/all_to_all | solution.py:77
  104.0 6.1 %collective-permute-start.11 = (f32[128,256]{1,0:T(8,128)S(1)}, f32[128,256]{1,0:T(8,128)S(1)}, u32[]{:S(2)}, u32[]{:S(2)}) collective-permute-start(f32[128,256]{1,0:T(8,128)S(1)} %get-tuple-element.57), channel_id=1, source_target_pairs={{0,64},{32,96},{64,0},{96,32},{128,192},{160,224},{192,128},{224,1... | collective-permute-start | bytes 393224 | tf_op jit(solution)/shard_map/ppermute | solution.py:367
  105.0 7.9 %collective-permute-start.12 = (f32[128,256]{1,0:T(8,128)S(1)}, f32[128,256]{1,0:T(8,128)S(1)}, u32[]{:S(2)}, u32[]{:S(2)}) collective-permute-start(f32[128,256]{1,0:T(8,128)S(1)} %get-tuple-element.58), channel_id=1, source_target_pairs={{0,192},{32,224},{64,128},{96,160},{128,64},{160,96},{192,0},{224,... | collective-permute-start | bytes 393224 | tf_op jit(solution)/shard_map/ppermute | solution.py:367
  106.5 8.6 %collective-permute-start.13 = (f32[128,256]{1,0:T(8,128)S(1)}, f32[128,256]{1,0:T(8,128)S(1)}, u32[]{:S(2)}, u32[]{:S(2)}) collective-permute-start(f32[128,256]{1,0:T(8,128)S(1)} %get-tuple-element.59), channel_id=1, source_target_pairs={{0,96},{32,64},{64,32},{96,0},{128,224},{160,192},{192,160},{224,1... | collective-permute-start | bytes 393224 | tf_op jit(solution)/shard_map/ppermute | solution.py:367
  107.3 12.6 %collective-permute-start.14 = (f32[128,256]{1,0:T(8,128)S(1)}, f32[128,256]{1,0:T(8,128)S(1)}, u32[]{:S(2)}, u32[]{:S(2)}) collective-permute-start(f32[128,256]{1,0:T(8,128)S(1)} %get-tuple-element.60), channel_id=1, source_target_pairs={{0,224},{32,192},{64,160},{96,128},{128,96},{160,64},{192,32},{224... | collective-permute-start | bytes 393224 | tf_op jit(solution)/shard_map/ppermute | solution.py:367
  108.5 11.3 %collective-permute-start.15 = (f32[128,256]{1,0:T(8,128)S(1)}, f32[128,256]{1,0:T(8,128)S(1)}, u32[]{:S(2)}, u32[]{:S(2)}) collective-permute-start(f32[128,256]{1,0:T(8,128)S(1)} %get-tuple-element.61), channel_id=1, source_target_pairs={{0,128},{32,160},{64,192},{96,224},{128,0},{160,32},{192,64},{224,... | collective-permute-start | bytes 393224 | tf_op jit(solution)/shard_map/ppermute | solution.py:367
  110.0 9.8 %collective-permute-start.16 = (f32[128,256]{1,0:T(8,128)S(1)}, f32[128,256]{1,0:T(8,128)S(1)}, u32[]{:S(2)}, u32[]{:S(2)}) collective-permute-start(f32[128,256]{1,0:T(8,128)S(1)} %get-tuple-element.62), channel_id=1, source_target_pairs={{0,160},{32,128},{64,224},{96,192},{128,32},{160,0},{192,96},{224,... | collective-permute-start | bytes 393224 | tf_op jit(solution)/shard_map/ppermute | solution.py:367
  112.9 6.9 %collective-permute-start.17 = (f32[128,256]{1,0:T(8,128)S(1)}, f32[128,256]{1,0:T(8,128)S(1)}, u32[]{:S(2)}, u32[]{:S(2)}) collective-permute-start(f32[128,256]{1,0:T(8,128)S(1)} %get-tuple-element.63), channel_id=1, source_target_pairs={{0,32},{32,0},{64,96},{96,64},{128,160},{160,128},{192,224},{224,1... | collective-permute-start | bytes 393224 | tf_op jit(solution)/shard_map/ppermute | solution.py:367
  (12 other events, 149.3 us)

commit v6 on v5

--- a/solution.py
+++ b/solution.py
@@ -20,6 +20,7 @@
 DEV = GX * GY
 HALF = MY // 2
 PARTNERS = (0, 2, 6, 3, 7, 4, 5, 1)
+SIDE = 48
 
 time_step = 0.2
 diffusion = 0.25
@@ -83,10 +84,14 @@
     )
 
 
+def pieces(array):
+    high = array.astype(jnp.bfloat16)
+    return high, (array - high.astype(jnp.float32)).astype(jnp.bfloat16)
+
+
 def split_dot(table, b, contract=((1,), (0,))):
     table_high, table_low = table
-    b_high = b.astype(jnp.bfloat16)
-    b_low = (b - b_high.astype(jnp.float32)).astype(jnp.bfloat16)
+    b_high, b_low = pieces(b)
 
     def one(left, right):
         return lax.dot_general(
@@ -100,7 +105,7 @@
     return jax.ShapeDtypeStruct(dims, jnp.float32)
 
 
-def local_kernel(kernel, out_shape, operands, flops=0, scratch=(), in_place=False, limit=24):
+def local_kernel(kernel, out_shape, operands, flops=0, scratch=(), in_place=False, limit=16):
     vmem = pl.BlockSpec(memory_space=pltpu.VMEM)
     place = pl.BlockSpec(memory_space=pl.ANY) if in_place else vmem
     size = sum(4 * math.prod(a.shape) for a in (*operands, *out_shape))
@@ -123,7 +128,7 @@
 
 
 def edge_kernel(
-    fields_hbm, velocity_hbm, last_x_ref, first_x_ref, even_ref, odd_ref, block_ref, row_ref, sems
+    fields_hbm, velocity_hbm, even_x_ref, odd_x_ref, even_ref, odd_ref, block_ref, row_ref, sems
 ):
     copies = [
         pltpu.make_async_copy(fields_hbm.at[f], block_ref.at[f], sems.at[f]) for f in range(F)
@@ -134,7 +139,6 @@
     ]
     for copy in copies:
         copy.start()
-    first_x_ref[F + 1 :] = jnp.zeros((7, CY), jnp.float32)
     lane = lax.broadcasted_iota(jnp.int32, (CX, 128), 1)
     sides = jnp.zeros((CX, 128), jnp.float32)
     for f in range(F + 1):
@@ -145,31 +149,46 @@
             sides = jnp.where(
                 lane == 16 + f, pltpu.roll(block_ref[f, :, 128:256], 17 + f, 1), sides
             )
-            last_x_ref[f : f + 1] = block_ref[f, CX - 1 : CX]
-            first_x_ref[f : f + 1] = block_ref[f, 0:1]
     sides = jnp.transpose(sides)
     is_even = lax.rem(lax.axis_index("gy"), 2) == 0
     first, last = sides[0:16], sides[16:32]
-    even_ref[...] = jnp.where(is_even, last, first)
-    odd_ref[...] = jnp.where(is_even, first, last)
+    even_ref[0:16] = jnp.where(is_even, last, first)
+    odd_ref[0:16] = jnp.where(is_even, first, last)
+    for ref in (even_ref, odd_ref):
+        ref[16:] = jnp.zeros((SIDE - 16, CX), jnp.float32)
     copies[F + 1].wait()
-    first_x_ref[F : F + 1] = row_ref[0:1]
-
-
-def step_kernel(fields_ref, velocity_ref, even_ref, odd_ref, *refs):
-    *block_refs, held_ref = refs
+    rest = jnp.zeros((7, CY), jnp.float32)
+    first = [block_ref[f, 0:1] for f in range(F)] + [row_ref[0:1], rest]
+    last = [block_ref[f, CX - 1 : CX] for f in range(F)] + [row_ref[0:1], rest]
+    first, last = jnp.concatenate(first, axis=0), jnp.concatenate(last, axis=0)
+    is_even = lax.rem(lax.axis_index("gx"), 2) == 0
+    even_x_ref[...] = jnp.where(is_even, last, first)
+    odd_x_ref[...] = jnp.where(is_even, first, last)
+
+
+def step_kernel(fields_ref, velocity_ref, odd_ref, even_ref, odd_x_ref, even_x_ref, *block_refs):
+    *block_refs, held_ref = block_refs
     row = lax.broadcasted_iota(jnp.int32, (CX, CY), 0)
     col = lax.broadcasted_iota(jnp.int32, (CX, CY), 1)
+    first_row, last_row = row == 0, row == CX - 1
     first_col, last_col = col == 0, col == CY - 1
     gx, gy = lax.axis_index("gx"), lax.axis_index("gy")
+    open_w = jnp.where(gx > 0, 1.0, 0.0)
+    open_e = jnp.where(gx < GX - 1, 1.0, 0.0)
     open_s = jnp.where(gy > 0, 1.0, 0.0)
     open_n = jnp.where(gy < GY - 1, 1.0, 0.0)
+    is_even = lax.rem(gx, 2) == 0
+    above = jnp.where(is_even, odd_x_ref[...], even_x_ref[...])
+    below = jnp.where(is_even, even_x_ref[...], odd_x_ref[...])
     is_even = lax.rem(gy, 2) == 0
-    before = jnp.transpose(jnp.where(is_even, odd_ref[...], even_ref[...]))
-    after = jnp.transpose(jnp.where(is_even, even_ref[...], odd_ref[...]))
-    low_w, high_w = (jnp.where(row == 0, 0.0, value) for value in face(velocity_ref[0]))
+    before = jnp.transpose(jnp.where(is_even, odd_ref[0:16], even_ref[0:16]))
+    after = jnp.transpose(jnp.where(is_even, even_ref[0:16], odd_ref[0:16]))
+    low_w, high_w = (
+        jnp.where(first_row, value * open_w, value) for value in face(velocity_ref[0])
+    )
     low_e, high_e = (
-        jnp.where(row == CX - 1, 0.0, pltpu.roll(value, CX - 1, 0)) for value in (low_w, high_w)
+        jnp.where(last_row, edge * open_e, pltpu.roll(value, CX - 1, 0))
+        for value, edge in zip((low_w, high_w), face(below[F : F + 1]))
     )
     low_s, high_s = (
         jnp.where(first_col, value * open_s, value) for value in face(velocity_ref[1])
@@ -181,26 +200,13 @@
     own = 1.0 - low_e + high_w - low_n + high_s
     for f in range(F):
         block = fields_ref[f]
+        west = jnp.where(first_row, above[f : f + 1], pltpu.roll(block, 1, 0))
+        east = jnp.where(last_row, below[f : f + 1], pltpu.roll(block, CX - 1, 0))
         south = jnp.where(first_col, before[:, f : f + 1], pltpu.roll(block, 1, 1))
         north = jnp.where(last_col, after[:, f : f + 1], pltpu.roll(block, CY - 1, 1))
-        value = (
-            own * block
-            + low_w * pltpu.roll(block, 1, 0)
-            - high_e * pltpu.roll(block, CX - 1, 0)
-            + low_s * south
-            - high_n * north
+        held_ref[f] = (
+            own * block + low_w * west - high_e * east + low_s * south - high_n * north
         )
-        extra = jnp.concatenate(
-            (
-                block[0:1],
-                block[CX - 1 : CX],
-                velocity_ref[0, 0:1],
-                jnp.zeros((5, CY), jnp.float32),
-            ),
-            axis=0,
-        )
-        held_ref[f, 0:CX] = value
-        held_ref[f, CX:] = extra
     for k, ref in zip(PARTNERS, block_refs):
         ref[...] = held_ref[lax.bitwise_xor(gx, k)]
 
@@ -213,17 +219,11 @@
 
 
 def forward_kernel(*refs):
-    *block_refs, table_ref, period_ref, height_ref, weight_ref = refs[:-4]
-    out_ref, columns_ref, parts_ref, edges_ref = refs[-4:]
+    *block_refs, table_ref, period_ref, height_ref, weight_ref = refs[:-3]
+    out_ref, columns_ref, parts_ref = refs[-3:]
     for k, ref in zip(PARTNERS, block_refs):
         source = lax.bitwise_xor(lax.axis_index("gx"), k)
-        columns_ref[pl.ds(pl.multiple_of(source * CX, CX), CX), :] = ref[0:CX]
-        edges_ref[source] = ref[CX:]
-    for t in range(1, GX):
-        first, second = face(edges_ref[t, 2:3])
-        flux = first * edges_ref[t - 1, 1:2] + second * edges_ref[t, 0:1]
-        columns_ref[t * CX - 1 : t * CX] -= flux
-        columns_ref[t * CX : t * CX + 1] += flux
+        columns_ref[pl.ds(pl.multiple_of(source * CX, CX), CX), :] = ref[...]
     q = lax.broadcasted_iota(jnp.int32, (HALF, CY), 0)
     real = jnp.zeros((HALF, CY), jnp.float32)
     imag = jnp.zeros((HALF, CY), jnp.float32)
@@ -243,11 +243,18 @@
     last_i = jnp.sum(folded * period_ref[1], axis=0, keepdims=True)
     row = lax.broadcasted_iota(jnp.int32, (HALF, HALF), 0)
     col = lax.broadcasted_iota(jnp.int32, (HALF, HALF), 1)
-    mirror = jnp.where(row + col == HALF, 1.0, 0.0).astype(jnp.float32)
+    mirror = jnp.where(row + col == HALF, 1.0, 0.0).astype(jnp.bfloat16)
+
+    def reflect(block):
+        high, low = pieces(block)
+        return jnp.dot(mirror, high, preferred_element_type=jnp.float32) + jnp.dot(
+            mirror, low, preferred_element_type=jnp.float32
+        )
+
     parts_ref[0:HALF] = real
-    parts_ref[HALF:MX] = jnp.where(q == 0, last_r, dot(mirror, real))
+    parts_ref[HALF:MX] = jnp.where(q == 0, last_r, reflect(real))
     parts_ref[MX : MX + HALF] = imag
-    parts_ref[MX + HALF :] = -jnp.where(q == 0, last_i, dot(mirror, imag))
+    parts_ref[MX + HALF :] = -jnp.where(q == 0, last_i, reflect(imag))
     mixed = split_dot((table_ref[512:1024], table_ref[1024:]), parts_ref[...], ((1,), (1,)))
     modes = (mixed[:MY, :MX] + mixed[MY:, MX:], mixed[:MY, MX:] - mixed[MY:, :MX])
     group = lax.broadcasted_iota(jnp.int32, (GY, 128), 1) // 32
@@ -276,6 +283,7 @@
     lane = lax.broadcasted_iota(jnp.int32, (F, 128), 1)
     is_real = lane < 64
     high_zero = (lane // 32) % 2 == 0
+    coeffs = []
     for low in range(4):
         cosine = turn_ref[0, quarter, low]
         sine = turn_ref[1, quarter, low]
@@ -285,21 +293,38 @@
             straight.append(jnp.sum(block * cosine, axis=0, keepdims=True))
             crossed.append(jnp.sum(block * sine, axis=0, keepdims=True))
         crossed = pltpu.roll(jnp.concatenate(crossed, axis=0), 64, 1)
-        coeffs = jnp.concatenate(straight, axis=0) + jnp.where(is_real, crossed, -crossed)
-        lifted = dot(jnp.transpose(coeffs * SCALE_IN), lift_ref[...])
+        total = jnp.concatenate(straight, axis=0) + jnp.where(is_real, crossed, -crossed)
+        coeffs.append(jnp.transpose(total * SCALE_IN))
+    lift_high, lift_low = pieces(lift_ref[...])
+    high, low = pieces(jnp.concatenate(coeffs, axis=0))
+    lifted = jnp.dot(
+        jnp.concatenate((high, high, low), axis=1),
+        jnp.concatenate((lift_high, lift_low, lift_high), axis=0),
+        preferred_element_type=jnp.float32,
+    )
+    mixed = []
+    for low in range(4):
+        part = lifted[low * 128 : (low + 1) * 128]
         mixed_r, mixed_i = [], []
         for high in range(2):
-            lift_r = lifted[high * 32 : high * 32 + 32]
-            lift_i = lifted[64 + high * 32 : 96 + high * 32]
+            lift_r = part[high * 32 : high * 32 + 32]
+            lift_i = part[64 + high * 32 : 96 + high * 32]
             gain_r = gain_ref[0, 4 * high + low]
             gain_i = gain_ref[1, 4 * high + low]
             mixed_r.append(gain_r * lift_r - gain_i * lift_i)
             mixed_i.append(gain_r * lift_i + gain_i * lift_r)
-        mixed = jnp.concatenate(mixed_r + mixed_i, axis=0)
-        outgoing = dot(project_ref[...], mixed, ((1,), (1,)))
-        first = high_zero & (gy == 0) if low == 0 else None
-        scale = 2.0 * SCALE_OUT if first is None else jnp.where(first, SCALE_OUT, 2.0 * SCALE_OUT)
-        outgoing = outgoing * scale
+        mixed += mixed_r + mixed_i
+    mixed = jnp.concatenate(mixed, axis=0)
+    result = split_dot(pieces(project_ref[...]), mixed, ((1,), (1,)))
+    for low in range(4):
+        cosine = turn_ref[0, quarter, low]
+        sine = turn_ref[1, quarter, low]
+        outgoing = result[:, low * 128 : (low + 1) * 128]
+        if low == 0:
+            first = high_zero & (gy == 0)
+            outgoing = outgoing * jnp.where(first, SCALE_OUT, 2.0 * SCALE_OUT)
+        else:
+            outgoing = outgoing * (2.0 * SCALE_OUT)
         swapped = pltpu.roll(outgoing, 64, 1)
         swapped = jnp.where(is_real, -swapped, swapped)
         for f in range(F):
@@ -348,17 +373,10 @@
 
 def finish_kernel(*refs):
     step_refs, block_refs, refs = refs[:GX], refs[GX : 2 * GX], refs[2 * GX :]
-    west_ref, east_ref, first_ref, last_ref, w_0, w_1, wh_0, wh_1, out_ref, gradient_ref = refs
+    w_0, w_1, wh_0, wh_1, out_ref, gradient_ref = refs
     gx = lax.axis_index("gx")
     for k, step_ref, block_ref in zip(PARTNERS, step_refs, block_refs):
-        out_ref[lax.bitwise_xor(gx, k)] = step_ref[0:CX] + block_ref[...]
-    first, second = face(first_ref[F : F + 1])
-    left = (first * west_ref[...] + second * first_ref[0:F]) * jnp.where(gx > 0, 1.0, 0.0)
-    first, second = face(east_ref[F : F + 1])
-    right = (first * last_ref[...] + second * east_ref[0:F]) * jnp.where(gx < GX - 1, 1.0, 0.0)
-    for f in range(F):
-        out_ref[f, 0:1] += left[f : f + 1]
-        out_ref[f, CX - 1 : CX] -= right[f : f + 1]
+        out_ref[lax.bitwise_xor(gx, k)] = step_ref[...] + block_ref[...]
     gradient_ref[...] = out_ref[0] * (w_0[...] + w_1[...]) - (wh_0[...] + wh_1[...])
 
 
@@ -432,7 +450,7 @@
             pltpu.VMEM((CY, chunk * 128), jnp.bfloat16),
             pltpu.VMEM((6 * CX, CY), jnp.float32),
         ],
-        compiler_params=pltpu.CompilerParams(vmem_limit_bytes=32 * 1024 * 1024),
+        compiler_params=pltpu.CompilerParams(vmem_limit_bytes=20 * 1024 * 1024),
         cost_estimate=pl.CostEstimate(
             flops=2 * 6 * CX * CY * 128 * (stop - start),
             bytes_accessed=4 * 128 * 4 * (stop - start),
@@ -453,13 +471,13 @@
     cell_cols,
     counts,
 ):
-    up_x = [(i, i + 1) for i in range(GX - 1)]
-    down_x = [(i + 1, i) for i in range(GX - 1)]
+    even_pairs_x = [(i, i ^ 1) for i in range(GX)]
+    odd_pairs_x = [(i, (i + 1) % GX if i % 2 else (i - 1) % GX) for i in range(GX)]
     even_pairs = [(i, i ^ 1) for i in range(GY)]
     odd_pairs = [(i, (i + 1) % GY if i % 2 else (i - 1) % GY) for i in range(GY)]
-    last_x, first_x, even, odd = local_kernel(
+    even_x, odd_x, even, odd = local_kernel(
         edge_kernel,
-        [shape(F, CY), shape(16, CY), shape(16, CX), shape(16, CX)],
+        [shape(16, CY), shape(16, CY), shape(SIDE, CX), shape(SIDE, CX)],
         (fields, velocity),
         scratch=[
             pltpu.VMEM((F + 1, CX, CY), jnp.float32),
@@ -469,13 +487,15 @@
         in_place=True,
         limit=56,
     )
+    odd = lax.ppermute(odd, "gy", odd_pairs)
     even = lax.ppermute(even, "gy", even_pairs)
-    odd = lax.ppermute(odd, "gy", odd_pairs)
+    odd_x = lax.ppermute(odd_x, "gx", odd_pairs_x)
+    even_x = lax.ppermute(even_x, "gx", even_pairs_x)
     stepped = local_kernel(
         step_kernel,
-        [shape(CX + 8, CY)] * GX,
-        (fields, velocity, even, odd),
-        scratch=[pltpu.VMEM((F, CX + 8, CY), jnp.float32)],
+        [shape(CX, CY)] * GX,
+        (fields, velocity, odd, even, odd_x, even_x),
+        scratch=[pltpu.VMEM((F, CX, CY), jnp.float32)],
     )
     blocks = exchange(stepped)
     sent = local_kernel(
@@ -492,14 +512,9 @@
         scratch=[
             pltpu.VMEM((NX, CY), jnp.float32),
             pltpu.VMEM((2 * MX, CY), jnp.float32),
-            pltpu.VMEM((GX, 8, CY), jnp.float32),
         ],
     )[0]
-    sent, last_x, first_x = lax.optimization_barrier((sent, last_x, first_x))
-    west = lax.ppermute(last_x, "gx", up_x)
-    east = lax.ppermute(first_x, "gx", down_x)
     got = all_to_all(sent, ("gx", "gy"))
-    got, west, east = lax.optimization_barrier((got, west, east))
     sent = local_kernel(
         mix_kernel,
         [shape(DEV, 1, 512)],
@@ -535,10 +550,6 @@
             (
                 *stepped,
                 *exchange(blocks),
-                west,
-                east,
-                first_x,
-                last_x,
                 w_0,
                 w_1,
                 wh_0,

time: 121 us -> 120 us (level)
  starting transfers between devices: 49.8 us -> 43.2 us
  waiting for transfers between devices: 39.3 us -> 44 us
    all_to_all x2, waiting for transfers between devices: 22.6 us -> 30.7 us  [all_to_all(): return lax.all_to_all(array, axis, split_axis=0, concat_axis=0, tiled=True)]
    ppermute x2, starting transfers between devices: 5.59 us -> 2.87 us  [the longest x1 2.05 us: body(): odd_x = lax.ppermute(odd_x, 'gx', odd_pairs_x)]
    ppermute x1, starting transfers between devices: 2.21 us -> 0.01 us  [body(): even = lax.ppermute(even, 'gy', even_pairs)]
    ppermute x2, waiting for transfers between devices: 3.24 us -> 1.05 us  [the longest x1 0.81 us: body(): odd_x = lax.ppermute(odd_x, 'gx', odd_pairs_x)]
    all_to_all x2, starting transfers between devices: 15.3 us -> 13.2 us  [all_to_all(): return lax.all_to_all(array, axis, split_axis=0, concat_axis=0, tiled=True)]
    ppermute x1, starting transfers between devices: 7.19 us -> 8.94 us  [body(): odd = lax.ppermute(odd, 'gy', odd_pairs)]
    ppermute x14, starting transfers between devices: 19.5 us -> 18.2 us  [exchange(): lax.ppermute(block, 'gx', [(i, i ^ k) for i in range(GX)])]
    ppermute x1, waiting for transfers between devices: 1.25 us -> 0.01 us  [body(): odd = lax.ppermute(odd, 'gy', odd_pairs)]
  transfers between devices with their start and end apart: 20 -> 20, of which waited for: 6 -> 8; matrix products, arithmetic and copies ran while one was open for 0% -> 0% of each run, Pallas kernels for 13% -> 13%
where the time goes in v6:
time: 120 us; the launch traced here: 119 us
  waiting for transfers between devices  44 us (37%)
  starting transfers between devices  43.2 us (36%)
  Pallas kernels  29.1 us (24%)
  local copies, waits for them, and re-layouts  2.09 us (2%)
    all_to_all x2, waiting for transfers between devices, all_to_all(): return lax.all_to_all(array, axis, split_axis=0, concat_axis=0, tiled=True)  30.7 us
    ppermute x14, starting transfers between devices, exchange(): lax.ppermute(block, 'gx', [(i, i ^ k) for i in range(GX)])  18.2 us
    pallas_call x2, Pallas kernels, scatter(): pl.pallas_call(scatter_kernel, grid=(steps,), in_specs=[block] * 3 + [pl....  16 us
    all_to_all x2, starting transfers between devices, all_to_all(): return lax.all_to_all(array, axis, split_axis=0, concat_axis=0, tiled=True)  13.2 us
    pallas_call x6, Pallas kernels, local_kernel(): pl.pallas_call(kernel, in_specs=[place] * len(operands), out_specs=[vmem]...  13.1 us
    ppermute x14, waiting for transfers between devices, exchange(): lax.ppermute(block, 'gx', [(i, i ^ k) for i in range(GX)])  12.2 us
    ppermute x1, starting transfers between devices, body(): odd = lax.ppermute(odd, 'gy', odd_pairs)  8.94 us
  transfers between devices with their start and end apart: 20, of which 8 were waited for; matrix products, arithmetic and copies ran while one was open for 0% of the time, Pallas kernels for 13%

profile of v6, /device:TPU:1, one launch (start us, length us, event | category | flops | bytes accessed | tf_op | source)
XLA Modules:
  0.0 119.3 jit_solution(11425051431715279730)
XLA Ops:
  0.6 2.7 %shard_map.149 = (f32[16,256]{1,0:T(8,128)}, f32[16,256]{1,0:T(8,128)}, f32[48,128]{1,0:T(8,128)}, f32[48,128]{1,0:T(8,128)}) custom-call(f32[8,128,256]{2,1,0:T(8,128)} %fields_ref.1, f32[2,128,256]{2,1,0:T(8,128)} %velocity_ref.1), custom_call_target="tpu_custom_call" | custom-call | bytes 1392640 | tf_op jit(solution)/shard_map/pallas_call | solution.py:112
  3.3 8.9 %collective-permute-start = (f32[48,128]{1,0:T(8,128)}, f32[48,128]{1,0:T(8,128)S(1)}, u32[]{:S(2)}, u32[]{:S(2)}) collective-permute-start(f32[48,128]{1,0:T(8,128)} %get-tuple-element.31), channel_id=1, source_target_pairs={{0,31},{1,2},{2,1},{3,4},{4,3},{5,6},{6,5},{7,8},{8,7},{9,10},{10,... | collective-permute-start | bytes 73736 | tf_op jit(solution)/shard_map/ppermute | solution.py:490
  12.3 2.1 %collective-permute-start.2 = (f32[16,256]{1,0:T(8,128)}, f32[16,256]{1,0:T(8,128)S(1)}, u32[]{:S(2)}, u32[]{:S(2)}) collective-permute-start(f32[16,256]{1,0:T(8,128)} %get-tuple-element.33), channel_id=1, source_target_pairs={{0,224},{32,64},{64,32},{96,128},{128,96},{160,192},{192,160},{224... | collective-permute-start | bytes 49160 | tf_op jit(solution)/shard_map/ppermute | solution.py:492
  16.2 1.4 %shard_map.150 = (f32[128,256]{1,0:T(8,128)S(1)}, f32[128,256]{1,0:T(8,128)S(1)}, f32[128,256]{1,0:T(8,128)S(1)}, f32[128,256]{1,0:T(8,128)S(1)}, f32[128,256]{1...) custom-call(f32[8,128,256]{2,1,0:T(8,128)S(1)} %copy-done, ...), custom_call_target="tpu_custom_call" | custom-call | bytes 2441216 | tf_op jit(solution)/shard_map/pallas_call | solution.py:112
  18.9 2.0 %collective-permute-start.5 = (f32[128,256]{1,0:T(8,128)S(1)}, f32[128,256]{1,0:T(8,128)S(1)}, u32[]{:S(2)}, u32[]{:S(2)}) collective-permute-start(f32[128,256]{1,0:T(8,128)S(1)} %get-tuple-element.37.refs_2_), channel_id=1, source_target_pairs={{0,192},{32,224},{64,128},{96,160},{128,64},{160,96},{192,0},{224,... | collective-permute-start | bytes 393224 | tf_op jit(solution)/shard_map/ppermute | solution.py:385
  21.0 1.6 %collective-permute-start.6 = (f32[128,256]{1,0:T(8,128)S(1)}, f32[128,256]{1,0:T(8,128)S(1)}, u32[]{:S(2)}, u32[]{:S(2)}) collective-permute-start(f32[128,256]{1,0:T(8,128)S(1)} %get-tuple-element.38.refs_3_), channel_id=1, source_target_pairs={{0,96},{32,64},{64,32},{96,0},{128,224},{160,192},{192,160},{224,1... | collective-permute-start | bytes 393224 | tf_op jit(solution)/shard_map/ppermute | solution.py:385
  23.1 1.4 %collective-permute-start.8 = (f32[128,256]{1,0:T(8,128)S(1)}, f32[128,256]{1,0:T(8,128)S(1)}, u32[]{:S(2)}, u32[]{:S(2)}) collective-permute-start(f32[128,256]{1,0:T(8,128)S(1)} %get-tuple-element.40.refs_5_), channel_id=1, source_target_pairs={{0,128},{32,160},{64,192},{96,224},{128,0},{160,32},{192,64},{224,... | collective-permute-start | bytes 393224 | tf_op jit(solution)/shard_map/ppermute | solution.py:385
  24.5 2.4 %collective-permute-start.9 = (f32[128,256]{1,0:T(8,128)S(1)}, f32[128,256]{1,0:T(8,128)S(1)}, u32[]{:S(2)}, u32[]{:S(2)}) collective-permute-start(f32[128,256]{1,0:T(8,128)S(1)} %get-tuple-element.41.refs_6_), channel_id=1, source_target_pairs={{0,160},{32,128},{64,224},{96,192},{128,32},{160,0},{192,96},{224,... | collective-permute-start | bytes 393224 | tf_op jit(solution)/shard_map/ppermute | solution.py:385
  26.9 2.6 %collective-permute-done.7.refs_4_ = f32[128,256]{1,0:T(8,128)S(1)} collective-permute-done((f32[128,256]{1,0:T(8,128)S(1)}, f32[128,256]{1,0:T(8,128)S(1)}, u32[]{:S(2)}, u32[]{:S(2)}) %collective-permute-start.7) | collective-permute-done | bytes 131104 | tf_op jit(solution)/shard_map/ppermute | solution.py:385
  29.5 1.7 %collective-permute-done.8.refs_5_ = f32[128,256]{1,0:T(8,128)S(1)} collective-permute-done((f32[128,256]{1,0:T(8,128)S(1)}, f32[128,256]{1,0:T(8,128)S(1)}, u32[]{:S(2)}, u32[]{:S(2)}) %collective-permute-start.8) | collective-permute-done | bytes 131104 | tf_op jit(solution)/shard_map/ppermute | solution.py:385
  31.2 3.1 %collective-permute-done.9.refs_6_ = f32[128,256]{1,0:T(8,128)S(1)} collective-permute-done((f32[128,256]{1,0:T(8,128)S(1)}, f32[128,256]{1,0:T(8,128)S(1)}, u32[]{:S(2)}, u32[]{:S(2)}) %collective-permute-start.9) | collective-permute-done | bytes 131104 | tf_op jit(solution)/shard_map/ppermute | solution.py:385
  34.3 3.0 %shard_map.151 = f32[256,1,768]{2,1,0:T(1,128)} custom-call(f32[128,256]{1,0:T(8,128)S(1)} %get-tuple-element.35.refs_0_, f32[128,256]{1,0:T(8,128)S(1)} %collective-permute-done.4.refs_1_, f32[128,256]{1,0:T(8,128)S(1)} %collective-permute-done.5.refs_2_, f32[128,256]{1,0:T(8,128)S(1)} %collective-permute-done.6.refs_3_, ...), custom_call_target="tpu_custom_call" | custom-call | flops 805306368 | bytes 3686400 | tf_op jit(solution)/shard_map/pallas_call | solution.py:112
  37.3 6.9 %all-to-all-start = ((f32[256,1,768]{2,1,0:T(1,128)}), f32[256,1,768]{2,1,0:T(1,128)S(1)}, u32[]{:S(2)}, u32[]{:S(2)}) async-start(f32[256,1,768]{2,1,0:T(1,128)} %shard_map.151), calls=%async_computation | async-start | bytes 1572864 | tf_op jit(solution)/shard_map/all_to_all | solution.py:78
  45.2 24.6 %all-to-all-done.got_ref = f32[256,1,768]{2,1,0:T(1,128)S(1)} async-done(((f32[256,1,768]{2,1,0:T(1,128)}), f32[256,1,768]{2,1,0:T(1,128)S(1)}, u32[]{:S(2)}, u32[]{:S(2)}) %all-to-all-start) | async-done | bytes 786464 | tf_op jit(solution)/shard_map/all_to_all | solution.py:78
  69.8 2.0 %shard_map.152 = f32[256,1,512]{2,1,0:T(1,128)} custom-call(f32[256,1,768]{2,1,0:T(1,128)S(1)} %all-to-all-done.got_ref, f32[2,4,4,32,128]{4,3,2,1,0:T(8,128)S(1)} %copy-done.2, f32[2,8,32,128]{3,2,1,0:T(8,128)S(1)} %bitcast.9, f32[8,128]{1,0:T(8,128)S(1)} %copy-done.3, f32[8,128]{1,0:T(8,128)S(1)} %bitcast.10), custom_call_target="tpu_custom_call" | custom-call | flops 12582912 | bytes 2105344 | tf_op jit(solution)/shard_map/pallas_call | solution.py:112
  71.8 6.4 %all-to-all-start.1 = ((f32[256,1,512]{2,1,0:T(1,128)}), f32[256,1,512]{2,1,0:T(1,128)S(1)}, u32[]{:S(2)}, u32[]{:S(2)}) async-start(f32[256,1,512]{2,1,0:T(1,128)} %shard_map.152), calls=%async_computation.1 | async-start | bytes 1048576 | tf_op jit(solution)/shard_map/all_to_all | solution.py:78
  78.2 13.8 %shard_map.153 = (f32[128,256]{1,0:T(8,128)S(1)}, f32[128,256]{1,0:T(8,128)S(1)}) custom-call(s32[256,128]{1,0:T(8,128)S(1)} %bitcast.13, s32[256,128]{1,0:T(8,128)S(1)} %bitcast.15, f32[256,128]{1,0:T(8,128)S(1)} %fusion.live_ref, f32[256,1,768]{2,1,0:T(1,128)S(1)} %all-to-all-done.got_ref), custom_call_target="tpu_custom_call" | custom-call | flops 11274289152 | bytes 458752 | tf_op jit(solution)/shard_map/pallas_call | solution.py:442
  92.0 6.2 %all-to-all-done.1.got_ref = f32[256,1,512]{2,1,0:T(1,128)S(1)} async-done(((f32[256,1,512]{2,1,0:T(1,128)}), f32[256,1,512]{2,1,0:T(1,128)S(1)}, u32[]{:S(2)}, u32[]{:S(2)}) %all-to-all-start.1) | async-done | bytes 524320 | tf_op jit(solution)/shard_map/all_to_all | solution.py:78
  99.4 2.8 %shard_map.154 = (f32[128,256]{1,0:T(8,128)S(1)}, f32[128,256]{1,0:T(8,128)S(1)}, f32[128,256]{1,0:T(8,128)S(1)}, f32[128,256]{1,0:T(8,128)S(1)}, f32[128,256]{1...) custom-call(f32[256,1,512]{2,1,0:T(1,128)S(1)} %all-to-all-done.1.got_ref, ...), custom_call_target="tpu_custom_call" | custom-call | flops 1207959552 | bytes 3670016 | tf_op jit(solution)/shard_map/pallas_call | solution.py:112
  103.3 1.5 %collective-permute-start.12 = (f32[128,256]{1,0:T(8,128)S(1)}, f32[128,256]{1,0:T(8,128)S(1)}, u32[]{:S(2)}, u32[]{:S(2)}) collective-permute-start(f32[128,256]{1,0:T(8,128)S(1)} %get-tuple-element.48), channel_id=1, source_target_pairs={{0,192},{32,224},{64,128},{96,160},{128,64},{160,96},{192,0},{224,... | collective-permute-start | bytes 393224 | tf_op jit(solution)/shard_map/ppermute | solution.py:385
  106.8 1.5 %collective-permute-start.15 = (f32[128,256]{1,0:T(8,128)S(1)}, f32[128,256]{1,0:T(8,128)S(1)}, u32[]{:S(2)}, u32[]{:S(2)}) collective-permute-start(f32[128,256]{1,0:T(8,128)S(1)} %get-tuple-element.51), channel_id=1, source_target_pairs={{0,128},{32,160},{64,192},{96,224},{128,0},{160,32},{192,64},{224,... | collective-permute-start | bytes 393224 | tf_op jit(solution)/shard_map/ppermute | solution.py:385
  108.4 2.9 %collective-permute-start.16 = (f32[128,256]{1,0:T(8,128)S(1)}, f32[128,256]{1,0:T(8,128)S(1)}, u32[]{:S(2)}, u32[]{:S(2)}) collective-permute-start(f32[128,256]{1,0:T(8,128)S(1)} %get-tuple-element.52), channel_id=1, source_target_pairs={{0,160},{32,128},{64,224},{96,192},{128,32},{160,0},{192,96},{224,... | collective-permute-start | bytes 393224 | tf_op jit(solution)/shard_map/ppermute | solution.py:385
  111.2 2.1 %shard_map.155 = (f32[128,256]{1,0:T(8,128)S(1)}, f32[128,256]{1,0:T(8,128)S(1)}) custom-call(s32[256,128]{1,0:T(8,128)S(1)} %bitcast.14, s32[256,128]{1,0:T(8,128)S(1)} %bitcast.16, f32[256,128]{1,0:T(8,128)S(1)} %fusion.live_ref, f32[256,1,768]{2,1,0:T(1,128)S(1)} %all-to-all-done.got_ref), custom_call_target="tpu_custom_call" | custom-call | flops 1610612736 | bytes 65536 | tf_op jit(solution)/shard_map/pallas_call | solution.py:442
  113.4 4.8 %collective-permute-done.14.refs_12_ = f32[128,256]{1,0:T(8,128)S(1)} collective-permute-done((f32[128,256]{1,0:T(8,128)S(1)}, f32[128,256]{1,0:T(8,128)S(1)}, u32[]{:S(2)}, u32[]{:S(2)}) %collective-permute-start.14) | collective-permute-done | bytes 131104 | tf_op jit(solution)/shard_map/ppermute | solution.py:385
  (54 shorter events, 10.1 us)
Async XLA Ops:
  3.3 30.9 %copy-start.10 = (bf16[1536,256]{1,0:T(8,128)(2,1)S(1)}, bf16[1536,256]{1,0:T(8,128)(2,1)}, u32[]{:S(2)}) copy-start(bf16[1536,256]{1,0:T(8,128)(2,1)} %constant.8.clone.refs_8_) | copy-start | bytes 2359300
  3.3 12.9 %collective-permute-start = (f32[48,128]{1,0:T(8,128)}, f32[48,128]{1,0:T(8,128)S(1)}, u32[]{:S(2)}, u32[]{:S(2)}) collective-permute-start(f32[48,128]{1,0:T(8,128)} %get-tuple-element.31), channel_id=1, source_target_pairs={{0,31},{1,2},{2,1},{3,4},{4,3},{5,6},{6,5},{7,8},{8,7},{9,10},{10,... | collective-permute-start | bytes 73736 | tf_op jit(solution)/shard_map/ppermute | solution.py:490
  12.3 3.9 %collective-permute-start.1 = (f32[48,128]{1,0:T(8,128)}, f32[48,128]{1,0:T(8,128)S(1)}, u32[]{:S(2)}, u32[]{:S(2)}) collective-permute-start(f32[48,128]{1,0:T(8,128)} %get-tuple-element.32), channel_id=1, source_target_pairs={{0,1},{1,0},{2,3},{3,2},{4,5},{5,4},{6,7},{7,6},{8,9},{9,8},{10,11... | collective-permute-start | bytes 73736 | tf_op jit(solution)/shard_map/ppermute | solution.py:491
  12.3 3.7 %collective-permute-start.2 = (f32[16,256]{1,0:T(8,128)}, f32[16,256]{1,0:T(8,128)S(1)}, u32[]{:S(2)}, u32[]{:S(2)}) collective-permute-start(f32[16,256]{1,0:T(8,128)} %get-tuple-element.33), channel_id=1, source_target_pairs={{0,224},{32,64},{64,32},{96,128},{128,96},{160,192},{192,160},{224... | collective-permute-start | bytes 49160 | tf_op jit(solution)/shard_map/ppermute | solution.py:492
  14.3 1.9 %collective-permute-start.3 = (f32[16,256]{1,0:T(8,128)}, f32[16,256]{1,0:T(8,128)S(1)}, u32[]{:S(2)}, u32[]{:S(2)}) collective-permute-start(f32[16,256]{1,0:T(8,128)} %get-tuple-element.34), channel_id=1, source_target_pairs={{0,32},{32,0},{64,96},{96,64},{128,160},{160,128},{192,224},{224,1... | collective-permute-start | bytes 49160 | tf_op jit(solution)/shard_map/ppermute | solution.py:493
  17.6 6.9 %collective-permute-start.4 = (f32[128,256]{1,0:T(8,128)S(1)}, f32[128,256]{1,0:T(8,128)S(1)}, u32[]{:S(2)}, u32[]{:S(2)}) collective-permute-start(f32[128,256]{1,0:T(8,128)S(1)} %get-tuple-element.36.refs_1_), channel_id=1, source_target_pairs={{0,64},{32,96},{64,0},{96,32},{128,192},{160,224},{192,128},{224,1... | collective-permute-start | bytes 393224 | tf_op jit(solution)/shard_map/ppermute | solution.py:385
  18.9 7.9 %collective-permute-start.5 = (f32[128,256]{1,0:T(8,128)S(1)}, f32[128,256]{1,0:T(8,128)S(1)}, u32[]{:S(2)}, u32[]{:S(2)}) collective-permute-start(f32[128,256]{1,0:T(8,128)S(1)} %get-tuple-element.37.refs_2_), channel_id=1, source_target_pairs={{0,192},{32,224},{64,128},{96,160},{128,64},{160,96},{192,0},{224,... | collective-permute-start | bytes 393224 | tf_op jit(solution)/shard_map/ppermute | solution.py:385
  21.0 5.9 %collective-permute-start.6 = (f32[128,256]{1,0:T(8,128)S(1)}, f32[128,256]{1,0:T(8,128)S(1)}, u32[]{:S(2)}, u32[]{:S(2)}) collective-permute-start(f32[128,256]{1,0:T(8,128)S(1)} %get-tuple-element.38.refs_3_), channel_id=1, source_target_pairs={{0,96},{32,64},{64,32},{96,0},{128,224},{160,192},{192,160},{224,1... | collective-permute-start | bytes 393224 | tf_op jit(solution)/shard_map/ppermute | solution.py:385
  22.5 7.0 %collective-permute-start.7 = (f32[128,256]{1,0:T(8,128)S(1)}, f32[128,256]{1,0:T(8,128)S(1)}, u32[]{:S(2)}, u32[]{:S(2)}) collective-permute-start(f32[128,256]{1,0:T(8,128)S(1)} %get-tuple-element.39.refs_4_), channel_id=1, source_target_pairs={{0,224},{32,192},{64,160},{96,128},{128,96},{160,64},{192,32},{224... | collective-permute-start | bytes 393224 | tf_op jit(solution)/shard_map/ppermute | solution.py:385
  23.1 8.1 %collective-permute-start.8 = (f32[128,256]{1,0:T(8,128)S(1)}, f32[128,256]{1,0:T(8,128)S(1)}, u32[]{:S(2)}, u32[]{:S(2)}) collective-permute-start(f32[128,256]{1,0:T(8,128)S(1)} %get-tuple-element.40.refs_5_), channel_id=1, source_target_pairs={{0,128},{32,160},{64,192},{96,224},{128,0},{160,32},{192,64},{224,... | collective-permute-start | bytes 393224 | tf_op jit(solution)/shard_map/ppermute | solution.py:385
  24.5 9.8 %collective-permute-start.9 = (f32[128,256]{1,0:T(8,128)S(1)}, f32[128,256]{1,0:T(8,128)S(1)}, u32[]{:S(2)}, u32[]{:S(2)}) collective-permute-start(f32[128,256]{1,0:T(8,128)S(1)} %get-tuple-element.41.refs_6_), channel_id=1, source_target_pairs={{0,160},{32,128},{64,224},{96,192},{128,32},{160,0},{192,96},{224,... | collective-permute-start | bytes 393224 | tf_op jit(solution)/shard_map/ppermute | solution.py:385
  26.8 7.4 %collective-permute-start.10 = (f32[128,256]{1,0:T(8,128)S(1)}, f32[128,256]{1,0:T(8,128)S(1)}, u32[]{:S(2)}, u32[]{:S(2)}) collective-permute-start(f32[128,256]{1,0:T(8,128)S(1)} %get-tuple-element.42.refs_7_), channel_id=1, source_target_pairs={{0,32},{32,0},{64,96},{96,64},{128,160},{160,128},{192,224},{224,1... | collective-permute-start | bytes 393224 | tf_op jit(solution)/shard_map/ppermute | solution.py:385
  37.3 32.4 %all-to-all-start = ((f32[256,1,768]{2,1,0:T(1,128)}), f32[256,1,768]{2,1,0:T(1,128)S(1)}, u32[]{:S(2)}, u32[]{:S(2)}) async-start(f32[256,1,768]{2,1,0:T(1,128)} %shard_map.151), calls=%async_computation | async-start | bytes 1572864 | tf_op jit(solution)/shard_map/all_to_all | solution.py:78
  44.2 25.5 %copy-start.2 = (f32[2,4,4,32,128]{4,3,2,1,0:T(8,128)S(1)}, f32[2,4,4,32,128]{4,3,2,1,0:T(8,128)}, u32[]{:S(2)}) copy-start(f32[2,4,4,32,128]{4,3,2,1,0:T(8,128)} %constant.10.clone.turn_ref) | copy-start | bytes 1572868
  45.1 24.7 %copy-start.3 = (f32[8,128]{1,0:T(8,128)S(1)}, f32[8,128]{1,0:T(8,128)}, u32[]{:S(2)}) copy-start(f32[8,128]{1,0:T(8,128)} %lift_ref.1) | copy-start | bytes 12292
  45.1 24.7 %copy-start.4 = (f32[128,8]{0,1:T(8,128)S(1)}, f32[128,8]{0,1:T(8,128)}, u32[]{:S(2)}) copy-start(f32[128,8]{0,1:T(8,128)} %param.18) | copy-start | bytes 12292
  71.8 26.4 %all-to-all-start.1 = ((f32[256,1,512]{2,1,0:T(1,128)}), f32[256,1,512]{2,1,0:T(1,128)S(1)}, u32[]{:S(2)}, u32[]{:S(2)}) async-start(f32[256,1,512]{2,1,0:T(1,128)} %shard_map.152), calls=%async_computation.1 | async-start | bytes 1048576 | tf_op jit(solution)/shard_map/all_to_all | solution.py:78
  102.3 6.1 %collective-permute-start.11 = (f32[128,256]{1,0:T(8,128)S(1)}, f32[128,256]{1,0:T(8,128)S(1)}, u32[]{:S(2)}, u32[]{:S(2)}) collective-permute-start(f32[128,256]{1,0:T(8,128)S(1)} %get-tuple-element.47), channel_id=1, source_target_pairs={{0,64},{32,96},{64,0},{96,32},{128,192},{160,224},{192,128},{224,1... | collective-permute-start | bytes 393224 | tf_op jit(solution)/shard_map/ppermute | solution.py:385
  103.3 7.9 %collective-permute-start.12 = (f32[128,256]{1,0:T(8,128)S(1)}, f32[128,256]{1,0:T(8,128)S(1)}, u32[]{:S(2)}, u32[]{:S(2)}) collective-permute-start(f32[128,256]{1,0:T(8,128)S(1)} %get-tuple-element.48), channel_id=1, source_target_pairs={{0,192},{32,224},{64,128},{96,160},{128,64},{160,96},{192,0},{224,... | collective-permute-start | bytes 393224 | tf_op jit(solution)/shard_map/ppermute | solution.py:385
  104.8 8.6 %collective-permute-start.13 = (f32[128,256]{1,0:T(8,128)S(1)}, f32[128,256]{1,0:T(8,128)S(1)}, u32[]{:S(2)}, u32[]{:S(2)}) collective-permute-start(f32[128,256]{1,0:T(8,128)S(1)} %get-tuple-element.49), channel_id=1, source_target_pairs={{0,96},{32,64},{64,32},{96,0},{128,224},{160,192},{192,160},{224,1... | collective-permute-start | bytes 393224 | tf_op jit(solution)/shard_map/ppermute | solution.py:385
  105.6 12.6 %collective-permute-start.14 = (f32[128,256]{1,0:T(8,128)S(1)}, f32[128,256]{1,0:T(8,128)S(1)}, u32[]{:S(2)}, u32[]{:S(2)}) collective-permute-start(f32[128,256]{1,0:T(8,128)S(1)} %get-tuple-element.50), channel_id=1, source_target_pairs={{0,224},{32,192},{64,160},{96,128},{128,96},{160,64},{192,32},{224... | collective-permute-start | bytes 393224 | tf_op jit(solution)/shard_map/ppermute | solution.py:385
  106.8 11.3 %collective-permute-start.15 = (f32[128,256]{1,0:T(8,128)S(1)}, f32[128,256]{1,0:T(8,128)S(1)}, u32[]{:S(2)}, u32[]{:S(2)}) collective-permute-start(f32[128,256]{1,0:T(8,128)S(1)} %get-tuple-element.51), channel_id=1, source_target_pairs={{0,128},{32,160},{64,192},{96,224},{128,0},{160,32},{192,64},{224,... | collective-permute-start | bytes 393224 | tf_op jit(solution)/shard_map/ppermute | solution.py:385
  108.4 9.8 %collective-permute-start.16 = (f32[128,256]{1,0:T(8,128)S(1)}, f32[128,256]{1,0:T(8,128)S(1)}, u32[]{:S(2)}, u32[]{:S(2)}) collective-permute-start(f32[128,256]{1,0:T(8,128)S(1)} %get-tuple-element.52), channel_id=1, source_target_pairs={{0,160},{32,128},{64,224},{96,192},{128,32},{160,0},{192,96},{224,... | collective-permute-start | bytes 393224 | tf_op jit(solution)/shard_map/ppermute | solution.py:385
  111.2 6.9 %collective-permute-start.17 = (f32[128,256]{1,0:T(8,128)S(1)}, f32[128,256]{1,0:T(8,128)S(1)}, u32[]{:S(2)}, u32[]{:S(2)}) collective-permute-start(f32[128,256]{1,0:T(8,128)S(1)} %get-tuple-element.53), channel_id=1, source_target_pairs={{0,32},{32,0},{64,96},{96,64},{128,160},{160,128},{192,224},{224,1... | collective-permute-start | bytes 393224 | tf_op jit(solution)/shard_map/ppermute | solution.py:385
  (10 other events, 109.3 us)

commit v7 on v6

--- a/solution.py
+++ b/solution.py
@@ -497,7 +497,12 @@
         (fields, velocity, odd, even, odd_x, even_x),
         scratch=[pltpu.VMEM((F, CX, CY), jnp.float32)],
     )
-    blocks = exchange(stepped)
+    live = (jnp.arange(128, dtype=jnp.int32)[None, :] < counts[0][:, None]).astype(jnp.float32)
+    gains = mode_gain.transpose(2, 1, 0, 3)
+    project = project_weight.T
+    *blocks, live, gains, project = lax.optimization_barrier(
+        (*exchange(stepped), live, gains, project)
+    )
     sent = local_kernel(
         forward_kernel,
         [shape(DEV, 1, 768)],
@@ -521,14 +526,13 @@
         (
             got,
             jnp.asarray(TURN),
-            mode_gain.transpose(2, 1, 0, 3),
+            gains,
             lift_weight,
-            project_weight.T,
+            project,
         ),
         flops=6 * 2 * 512 * 128 * 16,
     )[0]
 
-    live = (jnp.arange(128, dtype=jnp.int32)[None, :] < counts[0][:, None]).astype(jnp.float32)
     points = (cell_rows[0], cell_cols[0], live)
     w_0, wh_0 = scatter(*points, got, 0, 224, 56)
 

time: 120 us -> 118 us (0.983)
  blocking collectives: 0 us -> 31.9 us
  waiting for transfers between devices: 44 us -> 19.4 us
  starting transfers between devices: 43.2 us -> 36.4 us
    all_to_all x0 -> x1, blocking collectives: none -> 31.9 us  [all_to_all(): return lax.all_to_all(array, axis, split_axis=0, concat_axis=0, tiled=True)]
    all_to_all x2 -> x1, waiting for transfers between devices: 30.7 us -> 6.17 us  [all_to_all(): return lax.all_to_all(array, axis, split_axis=0, concat_axis=0, tiled=True)]
    all_to_all x2 -> x1, starting transfers between devices: 13.2 us -> 6.35 us  [all_to_all(): return lax.all_to_all(array, axis, split_axis=0, concat_axis=0, tiled=True)]
  transfers between devices with their start and end apart: 20 -> 19, of which waited for: 8 -> 5; matrix products, arithmetic and copies ran while one was open for 0% -> 0% of each run, Pallas kernels for 13% -> 14%
where the time goes in v7:
time: 118 us
  starting transfers between devices  36.4 us (31%)
  blocking collectives  31.9 us (27%)
  Pallas kernels  28.2 us (24%)
  waiting for transfers between devices  19.4 us (16%)
  local copies, waits for them, and re-layouts  1.37 us (1%)
    all_to_all x1, blocking collectives, all_to_all(): return lax.all_to_all(array, axis, split_axis=0, concat_axis=0, tiled=True)  31.9 us
    ppermute x14, starting transfers between devices, exchange(): lax.ppermute(block, 'gx', [(i, i ^ k) for i in range(GX)])  18.3 us
    pallas_call x2, Pallas kernels, scatter(): pl.pallas_call(scatter_kernel, grid=(steps,), in_specs=[block] * 3 + [pl....  16 us
    ppermute x14, waiting for transfers between devices, exchange(): lax.ppermute(block, 'gx', [(i, i ^ k) for i in range(GX)])  12.2 us
    pallas_call x6, Pallas kernels, local_kernel(): pl.pallas_call(kernel, in_specs=[place] * len(operands), out_specs=[vmem]...  12.2 us
    ppermute x1, starting transfers between devices, body(): odd = lax.ppermute(odd, 'gy', odd_pairs)  8.94 us
    all_to_all x1, starting transfers between devices, all_to_all(): return lax.all_to_all(array, axis, split_axis=0, concat_axis=0, tiled=True)  6.35 us
    all_to_all x1, waiting for transfers between devices, all_to_all(): return lax.all_to_all(array, axis, split_axis=0, concat_axis=0, tiled=True)  6.17 us
  transfers between devices with their start and end apart: 19, of which 5 were waited for; matrix products, arithmetic and copies ran while one was open for 0% of the time, Pallas kernels for 14%

profile of v7, /device:TPU:1, one launch (start us, length us, event | category | flops | bytes accessed | tf_op | source)
XLA Modules:
  0.0 118.3 jit_solution(17730762124196219648)
XLA Ops:
  0.6 2.7 %shard_map.149 = (f32[16,256]{1,0:T(8,128)}, f32[16,256]{1,0:T(8,128)}, f32[48,128]{1,0:T(8,128)}, f32[48,128]{1,0:T(8,128)}) custom-call(f32[8,128,256]{2,1,0:T(8,128)} %fields_ref.1, f32[2,128,256]{2,1,0:T(8,128)} %velocity_ref.1), custom_call_target="tpu_custom_call" | custom-call | bytes 1392640 | tf_op jit(solution)/shard_map/pallas_call | solution.py:112
  3.3 8.9 %collective-permute-start = (f32[48,128]{1,0:T(8,128)}, f32[48,128]{1,0:T(8,128)S(1)}, u32[]{:S(2)}, u32[]{:S(2)}) collective-permute-start(f32[48,128]{1,0:T(8,128)} %get-tuple-element.42), channel_id=1, source_target_pairs={{0,31},{1,2},{2,1},{3,4},{4,3},{5,6},{6,5},{7,8},{8,7},{9,10},{10,... | collective-permute-start | bytes 73736 | tf_op jit(solution)/shard_map/ppermute | solution.py:490
  12.3 2.1 %collective-permute-start.2 = (f32[16,256]{1,0:T(8,128)}, f32[16,256]{1,0:T(8,128)S(1)}, u32[]{:S(2)}, u32[]{:S(2)}) collective-permute-start(f32[16,256]{1,0:T(8,128)} %get-tuple-element.44), channel_id=1, source_target_pairs={{0,224},{32,64},{64,32},{96,128},{128,96},{160,192},{192,160},{224... | collective-permute-start | bytes 49160 | tf_op jit(solution)/shard_map/ppermute | solution.py:492
  16.2 1.4 %shard_map.150 = (f32[128,256]{1,0:T(8,128)S(1)}, f32[128,256]{1,0:T(8,128)S(1)}, f32[128,256]{1,0:T(8,128)S(1)}, f32[128,256]{1,0:T(8,128)S(1)}, f32[128,256]{1...) custom-call(f32[8,128,256]{2,1,0:T(8,128)S(1)} %copy-done, ...), custom_call_target="tpu_custom_call" | custom-call | bytes 2441216 | tf_op jit(solution)/shard_map/pallas_call | solution.py:112
  17.6 1.3 %collective-permute-start.4 = (f32[128,256]{1,0:T(8,128)S(1)}, f32[128,256]{1,0:T(8,128)S(1)}, u32[]{:S(2)}, u32[]{:S(2)}) collective-permute-start(f32[128,256]{1,0:T(8,128)S(1)} %get-tuple-element.47.refs_1_), channel_id=1, source_target_pairs={{0,64},{32,96},{64,0},{96,32},{128,192},{160,224},{192,128},{224,1... | collective-permute-start | bytes 393224 | tf_op jit(solution)/shard_map/ppermute | solution.py:385
  18.9 2.0 %collective-permute-start.5 = (f32[128,256]{1,0:T(8,128)S(1)}, f32[128,256]{1,0:T(8,128)S(1)}, u32[]{:S(2)}, u32[]{:S(2)}) collective-permute-start(f32[128,256]{1,0:T(8,128)S(1)} %get-tuple-element.48.refs_2_), channel_id=1, source_target_pairs={{0,192},{32,224},{64,128},{96,160},{128,64},{160,96},{192,0},{224,... | collective-permute-start | bytes 393224 | tf_op jit(solution)/shard_map/ppermute | solution.py:385
  21.0 1.7 %collective-permute-start.6 = (f32[128,256]{1,0:T(8,128)S(1)}, f32[128,256]{1,0:T(8,128)S(1)}, u32[]{:S(2)}, u32[]{:S(2)}) collective-permute-start(f32[128,256]{1,0:T(8,128)S(1)} %get-tuple-element.49.refs_3_), channel_id=1, source_target_pairs={{0,96},{32,64},{64,32},{96,0},{128,224},{160,192},{192,160},{224,1... | collective-permute-start | bytes 393224 | tf_op jit(solution)/shard_map/ppermute | solution.py:385
  23.3 1.3 %collective-permute-start.8 = (f32[128,256]{1,0:T(8,128)S(1)}, f32[128,256]{1,0:T(8,128)S(1)}, u32[]{:S(2)}, u32[]{:S(2)}) collective-permute-start(f32[128,256]{1,0:T(8,128)S(1)} %get-tuple-element.51.refs_5_), channel_id=1, source_target_pairs={{0,128},{32,160},{64,192},{96,224},{128,0},{160,32},{192,64},{224,... | collective-permute-start | bytes 393224 | tf_op jit(solution)/shard_map/ppermute | solution.py:385
  24.7 2.4 %collective-permute-start.9 = (f32[128,256]{1,0:T(8,128)S(1)}, f32[128,256]{1,0:T(8,128)S(1)}, u32[]{:S(2)}, u32[]{:S(2)}) collective-permute-start(f32[128,256]{1,0:T(8,128)S(1)} %get-tuple-element.52.refs_6_), channel_id=1, source_target_pairs={{0,160},{32,128},{64,224},{96,192},{128,32},{160,0},{192,96},{224,... | collective-permute-start | bytes 393224 | tf_op jit(solution)/shard_map/ppermute | solution.py:385
  27.2 7.4 %collective-permute-done.7.refs_4_ = f32[128,256]{1,0:T(8,128)S(1)} collective-permute-done((f32[128,256]{1,0:T(8,128)S(1)}, f32[128,256]{1,0:T(8,128)S(1)}, u32[]{:S(2)}, u32[]{:S(2)}) %collective-permute-start.7) | collective-permute-done | bytes 131104 | tf_op jit(solution)/shard_map/ppermute | solution.py:385
  34.6 2.1 %shard_map.151 = f32[256,1,768]{2,1,0:T(1,128)S(1)} custom-call(f32[128,256]{1,0:T(8,128)S(1)} %get-tuple-element.54.refs_0_, f32[128,256]{1,0:T(8,128)S(1)} %collective-permute-done.4.refs_1_, f32[128,256]{1,0:T(8,128)S(1)} %collective-permute-done.5.refs_2_, f32[128,256]{1,0:T(8,128)S(1)} %collective-permute-done.6.refs_3_, ...), custom_call_target="tpu_custom_call" | custom-call | flops 805306368 | bytes 3686400 | tf_op jit(solution)/shard_map/pallas_call | solution.py:112
  36.8 31.9 %all_to_all.10.got_ref = f32[256,1,768]{2,1,0:T(1,128)S(1)} all-to-all(f32[256,1,768]{2,1,0:T(1,128)S(1)} %shard_map.151), channel_id=1, replica_groups=mesh['gx'=8,'gy'=32] {'gx','gy'}, dimensions={0} | all-to-all | bytes 1572864 | tf_op jit(solution)/shard_map/all_to_all | solution.py:78
  68.7 2.0 %shard_map.152 = f32[256,1,512]{2,1,0:T(1,128)} custom-call(f32[256,1,768]{2,1,0:T(1,128)S(1)} %all_to_all.10.got_ref, f32[2,4,4,32,128]{4,3,2,1,0:T(8,128)S(1)} %copy-done.2, f32[2,8,32,128]{3,2,1,0:T(8,128)S(1)} %bitcast.9, f32[8,128]{1,0:T(8,128)S(1)} %copy-done.3, f32[8,128]{1,0:T(8,128)S(1)} %bitcast.10), custom_call_target="tpu_custom_call" | custom-call | flops 12582912 | bytes 2105344 | tf_op jit(solution)/shard_map/pallas_call | solution.py:112
  70.8 6.4 %all-to-all-start.1 = ((f32[256,1,512]{2,1,0:T(1,128)}), f32[256,1,512]{2,1,0:T(1,128)S(1)}, u32[]{:S(2)}, u32[]{:S(2)}) async-start(f32[256,1,512]{2,1,0:T(1,128)} %shard_map.152), calls=%async_computation.1 | async-start | bytes 1048576 | tf_op jit(solution)/shard_map/all_to_all | solution.py:78
  77.2 13.8 %shard_map.153 = (f32[128,256]{1,0:T(8,128)S(1)}, f32[128,256]{1,0:T(8,128)S(1)}) custom-call(s32[256,128]{1,0:T(8,128)S(1)} %bitcast.13, s32[256,128]{1,0:T(8,128)S(1)} %bitcast.15, f32[256,128]{1,0:T(8,128)S(1)} %fusion.live_ref, f32[256,1,768]{2,1,0:T(1,128)S(1)} %all_to_all.10.got_ref), custom_call_target="tpu_custom_call" | custom-call | flops 11274289152 | bytes 458752 | tf_op jit(solution)/shard_map/pallas_call | solution.py:442
  91.0 6.2 %all-to-all-done.1.got_ref = f32[256,1,512]{2,1,0:T(1,128)S(1)} async-done(((f32[256,1,512]{2,1,0:T(1,128)}), f32[256,1,512]{2,1,0:T(1,128)S(1)}, u32[]{:S(2)}, u32[]{:S(2)}) %all-to-all-start.1) | async-done | bytes 524320 | tf_op jit(solution)/shard_map/all_to_all | solution.py:78
  97.2 1.2 %copy-done.9 = bf16[2048,256]{1,0:T(8,128)(2,1)S(1)} copy-done((bf16[2048,256]{1,0:T(8,128)(2,1)S(1)}, bf16[2048,256]{1,0:T(8,128)(2,1)}, u32[]{:S(2)}) %copy-start.9) | copy-done | bytes 1048600
  98.4 2.8 %shard_map.154 = (f32[128,256]{1,0:T(8,128)S(1)}, f32[128,256]{1,0:T(8,128)S(1)}, f32[128,256]{1,0:T(8,128)S(1)}, f32[128,256]{1,0:T(8,128)S(1)}, f32[128,256]{1...) custom-call(f32[256,1,512]{2,1,0:T(1,128)S(1)} %all-to-all-done.1.got_ref, ...), custom_call_target="tpu_custom_call" | custom-call | flops 1207959552 | bytes 3670016 | tf_op jit(solution)/shard_map/pallas_call | solution.py:112
  102.3 1.5 %collective-permute-start.12 = (f32[128,256]{1,0:T(8,128)S(1)}, f32[128,256]{1,0:T(8,128)S(1)}, u32[]{:S(2)}, u32[]{:S(2)}) collective-permute-start(f32[128,256]{1,0:T(8,128)S(1)} %get-tuple-element.70), channel_id=1, source_target_pairs={{0,192},{32,224},{64,128},{96,160},{128,64},{160,96},{192,0},{224,... | collective-permute-start | bytes 393224 | tf_op jit(solution)/shard_map/ppermute | solution.py:385
  104.6 1.2 %collective-permute-start.14 = (f32[128,256]{1,0:T(8,128)S(1)}, f32[128,256]{1,0:T(8,128)S(1)}, u32[]{:S(2)}, u32[]{:S(2)}) collective-permute-start(f32[128,256]{1,0:T(8,128)S(1)} %get-tuple-element.72), channel_id=1, source_target_pairs={{0,224},{32,192},{64,160},{96,128},{128,96},{160,64},{192,32},{224... | collective-permute-start | bytes 393224 | tf_op jit(solution)/shard_map/ppermute | solution.py:385
  105.8 1.5 %collective-permute-start.15 = (f32[128,256]{1,0:T(8,128)S(1)}, f32[128,256]{1,0:T(8,128)S(1)}, u32[]{:S(2)}, u32[]{:S(2)}) collective-permute-start(f32[128,256]{1,0:T(8,128)S(1)} %get-tuple-element.73), channel_id=1, source_target_pairs={{0,128},{32,160},{64,192},{96,224},{128,0},{160,32},{192,64},{224,... | collective-permute-start | bytes 393224 | tf_op jit(solution)/shard_map/ppermute | solution.py:385
  107.3 2.9 %collective-permute-start.16 = (f32[128,256]{1,0:T(8,128)S(1)}, f32[128,256]{1,0:T(8,128)S(1)}, u32[]{:S(2)}, u32[]{:S(2)}) collective-permute-start(f32[128,256]{1,0:T(8,128)S(1)} %get-tuple-element.74), channel_id=1, source_target_pairs={{0,160},{32,128},{64,224},{96,192},{128,32},{160,0},{192,96},{224,... | collective-permute-start | bytes 393224 | tf_op jit(solution)/shard_map/ppermute | solution.py:385
  110.2 2.1 %shard_map.155 = (f32[128,256]{1,0:T(8,128)S(1)}, f32[128,256]{1,0:T(8,128)S(1)}) custom-call(s32[256,128]{1,0:T(8,128)S(1)} %bitcast.14, s32[256,128]{1,0:T(8,128)S(1)} %bitcast.16, f32[256,128]{1,0:T(8,128)S(1)} %fusion.live_ref, f32[256,1,768]{2,1,0:T(1,128)S(1)} %all_to_all.10.got_ref), custom_call_target="tpu_custom_call" | custom-call | flops 1610612736 | bytes 65536 | tf_op jit(solution)/shard_map/pallas_call | solution.py:442
  112.4 4.8 %collective-permute-done.14.refs_12_ = f32[128,256]{1,0:T(8,128)S(1)} collective-permute-done((f32[128,256]{1,0:T(8,128)S(1)}, f32[128,256]{1,0:T(8,128)S(1)}, u32[]{:S(2)}, u32[]{:S(2)}) %collective-permute-start.14) | collective-permute-done | bytes 131104 | tf_op jit(solution)/shard_map/ppermute | solution.py:385
  (53 shorter events, 5.7 us)
Async XLA Ops:
  0.6 15.6 %copy-start.1 = (f32[2,128,256]{2,1,0:T(8,128)S(1)}, f32[2,128,256]{2,1,0:T(8,128)}, u32[]{:S(2)}) copy-start(f32[2,128,256]{2,1,0:T(8,128)} %velocity_ref.1) | copy-start | bytes 786436
  3.3 12.9 %collective-permute-start = (f32[48,128]{1,0:T(8,128)}, f32[48,128]{1,0:T(8,128)S(1)}, u32[]{:S(2)}, u32[]{:S(2)}) collective-permute-start(f32[48,128]{1,0:T(8,128)} %get-tuple-element.42), channel_id=1, source_target_pairs={{0,31},{1,2},{2,1},{3,4},{4,3},{5,6},{6,5},{7,8},{8,7},{9,10},{10,... | collective-permute-start | bytes 73736 | tf_op jit(solution)/shard_map/ppermute | solution.py:490
  12.3 3.9 %collective-permute-start.1 = (f32[48,128]{1,0:T(8,128)}, f32[48,128]{1,0:T(8,128)S(1)}, u32[]{:S(2)}, u32[]{:S(2)}) collective-permute-start(f32[48,128]{1,0:T(8,128)} %get-tuple-element.43), channel_id=1, source_target_pairs={{0,1},{1,0},{2,3},{3,2},{4,5},{5,4},{6,7},{7,6},{8,9},{9,8},{10,11... | collective-permute-start | bytes 73736 | tf_op jit(solution)/shard_map/ppermute | solution.py:491
  12.3 3.7 %collective-permute-start.2 = (f32[16,256]{1,0:T(8,128)}, f32[16,256]{1,0:T(8,128)S(1)}, u32[]{:S(2)}, u32[]{:S(2)}) collective-permute-start(f32[16,256]{1,0:T(8,128)} %get-tuple-element.44), channel_id=1, source_target_pairs={{0,224},{32,64},{64,32},{96,128},{128,96},{160,192},{192,160},{224... | collective-permute-start | bytes 49160 | tf_op jit(solution)/shard_map/ppermute | solution.py:492
  14.3 20.2 %copy-start.10 = (bf16[1536,256]{1,0:T(8,128)(2,1)S(1)}, bf16[1536,256]{1,0:T(8,128)(2,1)}, u32[]{:S(2)}) copy-start(bf16[1536,256]{1,0:T(8,128)(2,1)} %constant.8.clone.refs_8_) | copy-start | bytes 2359300
  14.3 1.9 %collective-permute-start.3 = (f32[16,256]{1,0:T(8,128)}, f32[16,256]{1,0:T(8,128)S(1)}, u32[]{:S(2)}, u32[]{:S(2)}) collective-permute-start(f32[16,256]{1,0:T(8,128)} %get-tuple-element.45), channel_id=1, source_target_pairs={{0,32},{32,0},{64,96},{96,64},{128,160},{160,128},{192,224},{224,1... | collective-permute-start | bytes 49160 | tf_op jit(solution)/shard_map/ppermute | solution.py:493
  17.6 7.1 %collective-permute-start.4 = (f32[128,256]{1,0:T(8,128)S(1)}, f32[128,256]{1,0:T(8,128)S(1)}, u32[]{:S(2)}, u32[]{:S(2)}) collective-permute-start(f32[128,256]{1,0:T(8,128)S(1)} %get-tuple-element.47.refs_1_), channel_id=1, source_target_pairs={{0,64},{32,96},{64,0},{96,32},{128,192},{160,224},{192,128},{224,1... | collective-permute-start | bytes 393224 | tf_op jit(solution)/shard_map/ppermute | solution.py:385
  18.9 8.1 %collective-permute-start.5 = (f32[128,256]{1,0:T(8,128)S(1)}, f32[128,256]{1,0:T(8,128)S(1)}, u32[]{:S(2)}, u32[]{:S(2)}) collective-permute-start(f32[128,256]{1,0:T(8,128)S(1)} %get-tuple-element.48.refs_2_), channel_id=1, source_target_pairs={{0,192},{32,224},{64,128},{96,160},{128,64},{160,96},{192,0},{224,... | collective-permute-start | bytes 393224 | tf_op jit(solution)/shard_map/ppermute | solution.py:385
  21.0 6.1 %collective-permute-start.6 = (f32[128,256]{1,0:T(8,128)S(1)}, f32[128,256]{1,0:T(8,128)S(1)}, u32[]{:S(2)}, u32[]{:S(2)}) collective-permute-start(f32[128,256]{1,0:T(8,128)S(1)} %get-tuple-element.49.refs_3_), channel_id=1, source_target_pairs={{0,96},{32,64},{64,32},{96,0},{128,224},{160,192},{192,160},{224,1... | collective-permute-start | bytes 393224 | tf_op jit(solution)/shard_map/ppermute | solution.py:385
  22.7 11.8 %collective-permute-start.7 = (f32[128,256]{1,0:T(8,128)S(1)}, f32[128,256]{1,0:T(8,128)S(1)}, u32[]{:S(2)}, u32[]{:S(2)}) collective-permute-start(f32[128,256]{1,0:T(8,128)S(1)} %get-tuple-element.50.refs_4_), channel_id=1, source_target_pairs={{0,224},{32,192},{64,160},{96,128},{128,96},{160,64},{192,32},{224... | collective-permute-start | bytes 393224 | tf_op jit(solution)/shard_map/ppermute | solution.py:385
  23.3 11.2 %collective-permute-start.8 = (f32[128,256]{1,0:T(8,128)S(1)}, f32[128,256]{1,0:T(8,128)S(1)}, u32[]{:S(2)}, u32[]{:S(2)}) collective-permute-start(f32[128,256]{1,0:T(8,128)S(1)} %get-tuple-element.51.refs_5_), channel_id=1, source_target_pairs={{0,128},{32,160},{64,192},{96,224},{128,0},{160,32},{192,64},{224,... | collective-permute-start | bytes 393224 | tf_op jit(solution)/shard_map/ppermute | solution.py:385
  24.7 9.9 %collective-permute-start.9 = (f32[128,256]{1,0:T(8,128)S(1)}, f32[128,256]{1,0:T(8,128)S(1)}, u32[]{:S(2)}, u32[]{:S(2)}) collective-permute-start(f32[128,256]{1,0:T(8,128)S(1)} %get-tuple-element.52.refs_6_), channel_id=1, source_target_pairs={{0,160},{32,128},{64,224},{96,192},{128,32},{160,0},{192,96},{224,... | collective-permute-start | bytes 393224 | tf_op jit(solution)/shard_map/ppermute | solution.py:385
  27.0 7.5 %collective-permute-start.10 = (f32[128,256]{1,0:T(8,128)S(1)}, f32[128,256]{1,0:T(8,128)S(1)}, u32[]{:S(2)}, u32[]{:S(2)}) collective-permute-start(f32[128,256]{1,0:T(8,128)S(1)} %get-tuple-element.53.refs_7_), channel_id=1, source_target_pairs={{0,32},{32,0},{64,96},{96,64},{128,160},{160,128},{192,224},{224,1... | collective-permute-start | bytes 393224 | tf_op jit(solution)/shard_map/ppermute | solution.py:385
  36.7 32.0 %copy-start.2 = (f32[2,4,4,32,128]{4,3,2,1,0:T(8,128)S(1)}, f32[2,4,4,32,128]{4,3,2,1,0:T(8,128)}, u32[]{:S(2)}) copy-start(f32[2,4,4,32,128]{4,3,2,1,0:T(8,128)} %constant.10.clone.turn_ref) | copy-start | bytes 1572868
  36.8 32.0 %copy-start.3 = (f32[8,128]{1,0:T(8,128)S(1)}, f32[8,128]{1,0:T(8,128)}, u32[]{:S(2)}) copy-start(f32[8,128]{1,0:T(8,128)} %lift_ref.1) | copy-start | bytes 12292
  36.8 32.0 %copy-start.4 = (f32[128,8]{0,1:T(8,128)S(1)}, f32[128,8]{0,1:T(8,128)}, u32[]{:S(2)}) copy-start(f32[128,8]{0,1:T(8,128)} %param.18) | copy-start | bytes 12292
  70.8 26.4 %all-to-all-start.1 = ((f32[256,1,512]{2,1,0:T(1,128)}), f32[256,1,512]{2,1,0:T(1,128)S(1)}, u32[]{:S(2)}, u32[]{:S(2)}) async-start(f32[256,1,512]{2,1,0:T(1,128)} %shard_map.152), calls=%async_computation.1 | async-start | bytes 1048576 | tf_op jit(solution)/shard_map/all_to_all | solution.py:78
  101.3 6.1 %collective-permute-start.11 = (f32[128,256]{1,0:T(8,128)S(1)}, f32[128,256]{1,0:T(8,128)S(1)}, u32[]{:S(2)}, u32[]{:S(2)}) collective-permute-start(f32[128,256]{1,0:T(8,128)S(1)} %get-tuple-element.69), channel_id=1, source_target_pairs={{0,64},{32,96},{64,0},{96,32},{128,192},{160,224},{192,128},{224,1... | collective-permute-start | bytes 393224 | tf_op jit(solution)/shard_map/ppermute | solution.py:385
  102.3 7.9 %collective-permute-start.12 = (f32[128,256]{1,0:T(8,128)S(1)}, f32[128,256]{1,0:T(8,128)S(1)}, u32[]{:S(2)}, u32[]{:S(2)}) collective-permute-start(f32[128,256]{1,0:T(8,128)S(1)} %get-tuple-element.70), channel_id=1, source_target_pairs={{0,192},{32,224},{64,128},{96,160},{128,64},{160,96},{192,0},{224,... | collective-permute-start | bytes 393224 | tf_op jit(solution)/shard_map/ppermute | solution.py:385
  103.8 8.6 %collective-permute-start.13 = (f32[128,256]{1,0:T(8,128)S(1)}, f32[128,256]{1,0:T(8,128)S(1)}, u32[]{:S(2)}, u32[]{:S(2)}) collective-permute-start(f32[128,256]{1,0:T(8,128)S(1)} %get-tuple-element.71), channel_id=1, source_target_pairs={{0,96},{32,64},{64,32},{96,0},{128,224},{160,192},{192,160},{224,1... | collective-permute-start | bytes 393224 | tf_op jit(solution)/shard_map/ppermute | solution.py:385
  104.6 12.6 %collective-permute-start.14 = (f32[128,256]{1,0:T(8,128)S(1)}, f32[128,256]{1,0:T(8,128)S(1)}, u32[]{:S(2)}, u32[]{:S(2)}) collective-permute-start(f32[128,256]{1,0:T(8,128)S(1)} %get-tuple-element.72), channel_id=1, source_target_pairs={{0,224},{32,192},{64,160},{96,128},{128,96},{160,64},{192,32},{224... | collective-permute-start | bytes 393224 | tf_op jit(solution)/shard_map/ppermute | solution.py:385
  105.8 11.3 %collective-permute-start.15 = (f32[128,256]{1,0:T(8,128)S(1)}, f32[128,256]{1,0:T(8,128)S(1)}, u32[]{:S(2)}, u32[]{:S(2)}) collective-permute-start(f32[128,256]{1,0:T(8,128)S(1)} %get-tuple-element.73), channel_id=1, source_target_pairs={{0,128},{32,160},{64,192},{96,224},{128,0},{160,32},{192,64},{224,... | collective-permute-start | bytes 393224 | tf_op jit(solution)/shard_map/ppermute | solution.py:385
  107.3 9.8 %collective-permute-start.16 = (f32[128,256]{1,0:T(8,128)S(1)}, f32[128,256]{1,0:T(8,128)S(1)}, u32[]{:S(2)}, u32[]{:S(2)}) collective-permute-start(f32[128,256]{1,0:T(8,128)S(1)} %get-tuple-element.74), channel_id=1, source_target_pairs={{0,160},{32,128},{64,224},{96,192},{128,32},{160,0},{192,96},{224,... | collective-permute-start | bytes 393224 | tf_op jit(solution)/shard_map/ppermute | solution.py:385
  110.2 6.9 %collective-permute-start.17 = (f32[128,256]{1,0:T(8,128)S(1)}, f32[128,256]{1,0:T(8,128)S(1)}, u32[]{:S(2)}, u32[]{:S(2)}) collective-permute-start(f32[128,256]{1,0:T(8,128)S(1)} %get-tuple-element.75), channel_id=1, source_target_pairs={{0,32},{32,0},{64,96},{96,64},{128,160},{160,128},{192,224},{224,1... | collective-permute-start | bytes 393224 | tf_op jit(solution)/shard_map/ppermute | solution.py:385
  (9 other events, 77.0 us)

commit v8 on v7

--- a/solution.py
+++ b/solution.py
@@ -37,10 +37,8 @@
     q = np.arange(MX // 2)
     ang = 2.0 * np.pi * (q[:, None] * x[None, :]) / NX
     fore_x = np.concatenate((np.cos(ang), -np.sin(ang)))
-    m = np.arange(MX)
-    q = np.where(m < MX // 2, m, m - MX)
-    ang = 2.0 * np.pi * (x[:, None] * q[None, :]) / NX
-    back_x = np.concatenate((np.cos(ang), -np.sin(ang)))
+    back_x = np.concatenate((np.cos(ang.T), -np.sin(ang.T)), axis=1)
+    back_x[:, MX // 2] = np.cos(2.0 * np.pi * x / 8.0)
     ang = 2.0 * np.pi * np.arange(8) / 8.0
     period = np.stack([np.tile(row[:, None], (1, CY)) for row in (np.cos(ang), -np.sin(ang))])
     ang = 2.0 * np.pi * (ORDER[:, None] * np.arange(CY)[None, :]) / NY
@@ -356,16 +354,40 @@
     mixed = split_dot((table_ref[0:512], table_ref[512:1024]), modes_ref[...])
     real = mixed[:CY, :MX] - mixed[CY:, MX:]
     imag = mixed[:CY, MX:] + mixed[CY:, :MX]
-    index = lax.broadcasted_iota(jnp.int32, (CY, MX), 1)
+    row = lax.broadcasted_iota(jnp.int32, (HALF, HALF), 0)
+    col = lax.broadcasted_iota(jnp.int32, (HALF, HALF), 1)
+    mirror = jnp.where(row + col == HALF, 1.0, 0.0).astype(jnp.bfloat16)
+
+    def reflect(block):
+        high, low = pieces(block)
+        return jnp.dot(high, mirror, preferred_element_type=jnp.float32) + jnp.dot(
+            low, mirror, preferred_element_type=jnp.float32
+        )
+
+    index = lax.broadcasted_iota(jnp.int32, (CY, HALF), 1)
+    even = real[:, :HALF] + reflect(real[:, HALF:])
+    odd = imag[:, :HALF] - reflect(imag[:, HALF:])
+    odd = jnp.where(index == 0, real[:, HALF:], odd)
+    pick = jnp.where(
+        lax.broadcasted_iota(jnp.int32, (16, HALF), 1) == 0, 1.0, 0.0
+    ).astype(jnp.bfloat16)
+    last = split_dot((pick, jnp.zeros_like(pick)), imag[:, HALF:], ((1,), (1,)))[:8]
+    place = lax.broadcasted_iota(jnp.int32, (8, CY), 0)
+    sine = jnp.where(place % 4 == 0, 0.0, jnp.where(place % 2 == 0, 1.0, math.sqrt(0.5)))
+    last = last * jnp.where(place < 4, sine, -sine)
     for t in range(4):
-        turned_r, turned_i = real, imag
+        turned = (even, odd)
         if t:
             cosine, sine = quarter_turn(index, t)
-            turned_r = real * cosine - imag * sine
-            turned_i = imag * cosine + real * sine
-        field_ref[t * MX : (t + 1) * MX] = split_dot(
-            (table_ref[1024:1280], table_ref[1536:1792]), turned_r, ((1,), (1,))
-        ) + split_dot((table_ref[1280:1536], table_ref[1792:]), turned_i, ((1,), (1,)))
+            turned = (even * cosine - odd * sine, odd * cosine + even * sine)
+        block = split_dot(
+            (table_ref[1024:1280], table_ref[1280:]),
+            jnp.concatenate(turned, axis=1),
+            ((1,), (1,)),
+        )
+        field_ref[t * MX : (t + 1) * MX] = (
+            block.reshape(MX // 8, 8, CY) + last[None]
+        ).reshape(MX, CY)
     for k, ref in zip(PARTNERS, out_refs):
         owner = lax.bitwise_xor(lax.axis_index("gx"), k)
         ref[...] = field_ref[pl.ds(pl.multiple_of(owner * CX, CX), CX), :]

time: 118 us -> 118 us (level)
  no operation moved by 1% of the time
where the time goes in v8:
time: 118 us
  starting transfers between devices  36.4 us (31%)
  blocking collectives  31.9 us (27%)
  Pallas kernels  27.9 us (24%)
  waiting for transfers between devices  19.4 us (16%)
  local copies, waits for them, and re-layouts  1.28 us (1%)
    all_to_all x1, blocking collectives, all_to_all(): return lax.all_to_all(array, axis, split_axis=0, concat_axis=0, tiled=True)  31.9 us
    ppermute x14, starting transfers between devices, exchange(): lax.ppermute(block, 'gx', [(i, i ^ k) for i in range(GX)])  18.3 us
    pallas_call x2, Pallas kernels, scatter(): pl.pallas_call(scatter_kernel, grid=(steps,), in_specs=[block] * 3 + [pl....  16 us
    ppermute x14, waiting for transfers between devices, exchange(): lax.ppermute(block, 'gx', [(i, i ^ k) for i in range(GX)])  12.2 us
    pallas_call x6, Pallas kernels, local_kernel(): pl.pallas_call(kernel, in_specs=[place] * len(operands), out_specs=[vmem]...  11.9 us
    ppermute x1, starting transfers between devices, body(): odd = lax.ppermute(odd, 'gy', odd_pairs)  8.94 us
    all_to_all x1, starting transfers between devices, all_to_all(): return lax.all_to_all(array, axis, split_axis=0, concat_axis=0, tiled=True)  6.35 us
    all_to_all x1, waiting for transfers between devices, all_to_all(): return lax.all_to_all(array, axis, split_axis=0, concat_axis=0, tiled=True)  6.17 us
  transfers between devices with their start and end apart: 19, of which 5 were waited for; matrix products, arithmetic and copies ran while one was open for 0% of the time, Pallas kernels for 14%

profile of v8, /device:TPU:1, one launch (start us, length us, event | category | flops | bytes accessed | tf_op | source)
XLA Modules:
  0.0 117.9 jit_solution(17606820254250161301)
XLA Ops:
  0.6 2.7 %shard_map.149 = (f32[16,256]{1,0:T(8,128)}, f32[16,256]{1,0:T(8,128)}, f32[48,128]{1,0:T(8,128)}, f32[48,128]{1,0:T(8,128)}) custom-call(f32[8,128,256]{2,1,0:T(8,128)} %fields_ref.1, f32[2,128,256]{2,1,0:T(8,128)} %velocity_ref.1), custom_call_target="tpu_custom_call" | custom-call | bytes 1392640 | tf_op jit(solution)/shard_map/pallas_call | solution.py:110
  3.3 8.9 %collective-permute-start = (f32[48,128]{1,0:T(8,128)}, f32[48,128]{1,0:T(8,128)S(1)}, u32[]{:S(2)}, u32[]{:S(2)}) collective-permute-start(f32[48,128]{1,0:T(8,128)} %get-tuple-element.42), channel_id=1, source_target_pairs={{0,31},{1,2},{2,1},{3,4},{4,3},{5,6},{6,5},{7,8},{8,7},{9,10},{10,... | collective-permute-start | bytes 73736 | tf_op jit(solution)/shard_map/ppermute | solution.py:512
  12.3 2.1 %collective-permute-start.2 = (f32[16,256]{1,0:T(8,128)}, f32[16,256]{1,0:T(8,128)S(1)}, u32[]{:S(2)}, u32[]{:S(2)}) collective-permute-start(f32[16,256]{1,0:T(8,128)} %get-tuple-element.44), channel_id=1, source_target_pairs={{0,224},{32,64},{64,32},{96,128},{128,96},{160,192},{192,160},{224... | collective-permute-start | bytes 49160 | tf_op jit(solution)/shard_map/ppermute | solution.py:514
  16.2 1.4 %shard_map.150 = (f32[128,256]{1,0:T(8,128)S(1)}, f32[128,256]{1,0:T(8,128)S(1)}, f32[128,256]{1,0:T(8,128)S(1)}, f32[128,256]{1,0:T(8,128)S(1)}, f32[128,256]{1...) custom-call(f32[8,128,256]{2,1,0:T(8,128)S(1)} %copy-done, ...), custom_call_target="tpu_custom_call" | custom-call | bytes 2441216 | tf_op jit(solution)/shard_map/pallas_call | solution.py:110
  17.6 1.3 %collective-permute-start.4 = (f32[128,256]{1,0:T(8,128)S(1)}, f32[128,256]{1,0:T(8,128)S(1)}, u32[]{:S(2)}, u32[]{:S(2)}) collective-permute-start(f32[128,256]{1,0:T(8,128)S(1)} %get-tuple-element.47.refs_1_), channel_id=1, source_target_pairs={{0,64},{32,96},{64,0},{96,32},{128,192},{160,224},{192,128},{224,1... | collective-permute-start | bytes 393224 | tf_op jit(solution)/shard_map/ppermute | solution.py:407
  18.9 2.0 %collective-permute-start.5 = (f32[128,256]{1,0:T(8,128)S(1)}, f32[128,256]{1,0:T(8,128)S(1)}, u32[]{:S(2)}, u32[]{:S(2)}) collective-permute-start(f32[128,256]{1,0:T(8,128)S(1)} %get-tuple-element.48.refs_2_), channel_id=1, source_target_pairs={{0,192},{32,224},{64,128},{96,160},{128,64},{160,96},{192,0},{224,... | collective-permute-start | bytes 393224 | tf_op jit(solution)/shard_map/ppermute | solution.py:407
  21.0 1.7 %collective-permute-start.6 = (f32[128,256]{1,0:T(8,128)S(1)}, f32[128,256]{1,0:T(8,128)S(1)}, u32[]{:S(2)}, u32[]{:S(2)}) collective-permute-start(f32[128,256]{1,0:T(8,128)S(1)} %get-tuple-element.49.refs_3_), channel_id=1, source_target_pairs={{0,96},{32,64},{64,32},{96,0},{128,224},{160,192},{192,160},{224,1... | collective-permute-start | bytes 393224 | tf_op jit(solution)/shard_map/ppermute | solution.py:407
  23.3 1.3 %collective-permute-start.8 = (f32[128,256]{1,0:T(8,128)S(1)}, f32[128,256]{1,0:T(8,128)S(1)}, u32[]{:S(2)}, u32[]{:S(2)}) collective-permute-start(f32[128,256]{1,0:T(8,128)S(1)} %get-tuple-element.51.refs_5_), channel_id=1, source_target_pairs={{0,128},{32,160},{64,192},{96,224},{128,0},{160,32},{192,64},{224,... | collective-permute-start | bytes 393224 | tf_op jit(solution)/shard_map/ppermute | solution.py:407
  24.7 2.4 %collective-permute-start.9 = (f32[128,256]{1,0:T(8,128)S(1)}, f32[128,256]{1,0:T(8,128)S(1)}, u32[]{:S(2)}, u32[]{:S(2)}) collective-permute-start(f32[128,256]{1,0:T(8,128)S(1)} %get-tuple-element.52.refs_6_), channel_id=1, source_target_pairs={{0,160},{32,128},{64,224},{96,192},{128,32},{160,0},{192,96},{224,... | collective-permute-start | bytes 393224 | tf_op jit(solution)/shard_map/ppermute | solution.py:407
  27.2 7.4 %collective-permute-done.7.refs_4_ = f32[128,256]{1,0:T(8,128)S(1)} collective-permute-done((f32[128,256]{1,0:T(8,128)S(1)}, f32[128,256]{1,0:T(8,128)S(1)}, u32[]{:S(2)}, u32[]{:S(2)}) %collective-permute-start.7) | collective-permute-done | bytes 131104 | tf_op jit(solution)/shard_map/ppermute | solution.py:407
  34.6 2.1 %shard_map.151 = f32[256,1,768]{2,1,0:T(1,128)S(1)} custom-call(f32[128,256]{1,0:T(8,128)S(1)} %get-tuple-element.54.refs_0_, f32[128,256]{1,0:T(8,128)S(1)} %collective-permute-done.4.refs_1_, f32[128,256]{1,0:T(8,128)S(1)} %collective-permute-done.5.refs_2_, f32[128,256]{1,0:T(8,128)S(1)} %collective-permute-done.6.refs_3_, ...), custom_call_target="tpu_custom_call" | custom-call | flops 805306368 | bytes 3686400 | tf_op jit(solution)/shard_map/pallas_call | solution.py:110
  36.8 31.9 %all_to_all.10.got_ref = f32[256,1,768]{2,1,0:T(1,128)S(1)} all-to-all(f32[256,1,768]{2,1,0:T(1,128)S(1)} %shard_map.151), channel_id=1, replica_groups=mesh['gx'=8,'gy'=32] {'gx','gy'}, dimensions={0} | all-to-all | bytes 1572864 | tf_op jit(solution)/shard_map/all_to_all | solution.py:76
  68.7 2.0 %shard_map.152 = f32[256,1,512]{2,1,0:T(1,128)} custom-call(f32[256,1,768]{2,1,0:T(1,128)S(1)} %all_to_all.10.got_ref, f32[2,4,4,32,128]{4,3,2,1,0:T(8,128)S(1)} %copy-done.2, f32[2,8,32,128]{3,2,1,0:T(8,128)S(1)} %bitcast.9, f32[8,128]{1,0:T(8,128)S(1)} %copy-done.3, f32[8,128]{1,0:T(8,128)S(1)} %bitcast.10), custom_call_target="tpu_custom_call" | custom-call | flops 12582912 | bytes 2105344 | tf_op jit(solution)/shard_map/pallas_call | solution.py:110
  70.8 6.4 %all-to-all-start.1 = ((f32[256,1,512]{2,1,0:T(1,128)}), f32[256,1,512]{2,1,0:T(1,128)S(1)}, u32[]{:S(2)}, u32[]{:S(2)}) async-start(f32[256,1,512]{2,1,0:T(1,128)} %shard_map.152), calls=%async_computation.1 | async-start | bytes 1048576 | tf_op jit(solution)/shard_map/all_to_all | solution.py:76
  77.2 13.8 %shard_map.153 = (f32[128,256]{1,0:T(8,128)S(1)}, f32[128,256]{1,0:T(8,128)S(1)}) custom-call(s32[256,128]{1,0:T(8,128)S(1)} %bitcast.13, s32[256,128]{1,0:T(8,128)S(1)} %bitcast.15, f32[256,128]{1,0:T(8,128)S(1)} %fusion.live_ref, f32[256,1,768]{2,1,0:T(1,128)S(1)} %all_to_all.10.got_ref), custom_call_target="tpu_custom_call" | custom-call | flops 11274289152 | bytes 458752 | tf_op jit(solution)/shard_map/pallas_call | solution.py:464
  91.0 6.2 %all-to-all-done.1.got_ref = f32[256,1,512]{2,1,0:T(1,128)S(1)} async-done(((f32[256,1,512]{2,1,0:T(1,128)}), f32[256,1,512]{2,1,0:T(1,128)S(1)}, u32[]{:S(2)}, u32[]{:S(2)}) %all-to-all-start.1) | async-done | bytes 524320 | tf_op jit(solution)/shard_map/all_to_all | solution.py:76
  97.2 1.1 copy-done.9
  98.3 2.5 %shard_map.154 = (f32[128,256]{1,0:T(8,128)S(1)}, f32[128,256]{1,0:T(8,128)S(1)}, f32[128,256]{1,0:T(8,128)S(1)}, f32[128,256]{1,0:T(8,128)S(1)}, f32[128,256]{1...) custom-call(f32[256,1,512]{2,1,0:T(1,128)S(1)} %all-to-all-done.1.got_ref, ...), custom_call_target="tpu_custom_call" | custom-call | flops 1207959552 | bytes 3145728 | tf_op jit(solution)/shard_map/pallas_call | solution.py:110
  101.9 1.5 %collective-permute-start.12 = (f32[128,256]{1,0:T(8,128)S(1)}, f32[128,256]{1,0:T(8,128)S(1)}, u32[]{:S(2)}, u32[]{:S(2)}) collective-permute-start(f32[128,256]{1,0:T(8,128)S(1)} %get-tuple-element.70), channel_id=1, source_target_pairs={{0,192},{32,224},{64,128},{96,160},{128,64},{160,96},{192,0},{224,... | collective-permute-start | bytes 393224 | tf_op jit(solution)/shard_map/ppermute | solution.py:407
  104.2 1.2 %collective-permute-start.14 = (f32[128,256]{1,0:T(8,128)S(1)}, f32[128,256]{1,0:T(8,128)S(1)}, u32[]{:S(2)}, u32[]{:S(2)}) collective-permute-start(f32[128,256]{1,0:T(8,128)S(1)} %get-tuple-element.72), channel_id=1, source_target_pairs={{0,224},{32,192},{64,160},{96,128},{128,96},{160,64},{192,32},{224... | collective-permute-start | bytes 393224 | tf_op jit(solution)/shard_map/ppermute | solution.py:407
  105.4 1.5 %collective-permute-start.15 = (f32[128,256]{1,0:T(8,128)S(1)}, f32[128,256]{1,0:T(8,128)S(1)}, u32[]{:S(2)}, u32[]{:S(2)}) collective-permute-start(f32[128,256]{1,0:T(8,128)S(1)} %get-tuple-element.73), channel_id=1, source_target_pairs={{0,128},{32,160},{64,192},{96,224},{128,0},{160,32},{192,64},{224,... | collective-permute-start | bytes 393224 | tf_op jit(solution)/shard_map/ppermute | solution.py:407
  106.9 2.9 %collective-permute-start.16 = (f32[128,256]{1,0:T(8,128)S(1)}, f32[128,256]{1,0:T(8,128)S(1)}, u32[]{:S(2)}, u32[]{:S(2)}) collective-permute-start(f32[128,256]{1,0:T(8,128)S(1)} %get-tuple-element.74), channel_id=1, source_target_pairs={{0,160},{32,128},{64,224},{96,192},{128,32},{160,0},{192,96},{224,... | collective-permute-start | bytes 393224 | tf_op jit(solution)/shard_map/ppermute | solution.py:407
  109.8 2.2 %shard_map.155 = (f32[128,256]{1,0:T(8,128)S(1)}, f32[128,256]{1,0:T(8,128)S(1)}) custom-call(s32[256,128]{1,0:T(8,128)S(1)} %bitcast.14, s32[256,128]{1,0:T(8,128)S(1)} %bitcast.16, f32[256,128]{1,0:T(8,128)S(1)} %fusion.live_ref, f32[256,1,768]{2,1,0:T(1,128)S(1)} %all_to_all.10.got_ref), custom_call_target="tpu_custom_call" | custom-call | flops 1610612736 | bytes 65536 | tf_op jit(solution)/shard_map/pallas_call | solution.py:464
  112.0 4.8 %collective-permute-done.14.refs_12_ = f32[128,256]{1,0:T(8,128)S(1)} collective-permute-done((f32[128,256]{1,0:T(8,128)S(1)}, f32[128,256]{1,0:T(8,128)S(1)}, u32[]{:S(2)}, u32[]{:S(2)}) %collective-permute-start.14) | collective-permute-done | bytes 131104 | tf_op jit(solution)/shard_map/ppermute | solution.py:407
  (53 shorter events, 5.7 us)
Async XLA Ops:
  0.6 15.6 %copy-start.1 = (f32[2,128,256]{2,1,0:T(8,128)S(1)}, f32[2,128,256]{2,1,0:T(8,128)}, u32[]{:S(2)}) copy-start(f32[2,128,256]{2,1,0:T(8,128)} %velocity_ref.1) | copy-start | bytes 786436
  3.3 12.9 %collective-permute-start = (f32[48,128]{1,0:T(8,128)}, f32[48,128]{1,0:T(8,128)S(1)}, u32[]{:S(2)}, u32[]{:S(2)}) collective-permute-start(f32[48,128]{1,0:T(8,128)} %get-tuple-element.42), channel_id=1, source_target_pairs={{0,31},{1,2},{2,1},{3,4},{4,3},{5,6},{6,5},{7,8},{8,7},{9,10},{10,... | collective-permute-start | bytes 73736 | tf_op jit(solution)/shard_map/ppermute | solution.py:512
  12.3 3.9 %collective-permute-start.1 = (f32[48,128]{1,0:T(8,128)}, f32[48,128]{1,0:T(8,128)S(1)}, u32[]{:S(2)}, u32[]{:S(2)}) collective-permute-start(f32[48,128]{1,0:T(8,128)} %get-tuple-element.43), channel_id=1, source_target_pairs={{0,1},{1,0},{2,3},{3,2},{4,5},{5,4},{6,7},{7,6},{8,9},{9,8},{10,11... | collective-permute-start | bytes 73736 | tf_op jit(solution)/shard_map/ppermute | solution.py:513
  12.3 3.7 %collective-permute-start.2 = (f32[16,256]{1,0:T(8,128)}, f32[16,256]{1,0:T(8,128)S(1)}, u32[]{:S(2)}, u32[]{:S(2)}) collective-permute-start(f32[16,256]{1,0:T(8,128)} %get-tuple-element.44), channel_id=1, source_target_pairs={{0,224},{32,64},{64,32},{96,128},{128,96},{160,192},{192,160},{224... | collective-permute-start | bytes 49160 | tf_op jit(solution)/shard_map/ppermute | solution.py:514
  14.3 20.2 %copy-start.10 = (bf16[1536,256]{1,0:T(8,128)(2,1)S(1)}, bf16[1536,256]{1,0:T(8,128)(2,1)}, u32[]{:S(2)}) copy-start(bf16[1536,256]{1,0:T(8,128)(2,1)} %constant.8.clone.refs_8_) | copy-start | bytes 2359300
  14.3 1.9 %collective-permute-start.3 = (f32[16,256]{1,0:T(8,128)}, f32[16,256]{1,0:T(8,128)S(1)}, u32[]{:S(2)}, u32[]{:S(2)}) collective-permute-start(f32[16,256]{1,0:T(8,128)} %get-tuple-element.45), channel_id=1, source_target_pairs={{0,32},{32,0},{64,96},{96,64},{128,160},{160,128},{192,224},{224,1... | collective-permute-start | bytes 49160 | tf_op jit(solution)/shard_map/ppermute | solution.py:515
  17.6 7.1 %collective-permute-start.4 = (f32[128,256]{1,0:T(8,128)S(1)}, f32[128,256]{1,0:T(8,128)S(1)}, u32[]{:S(2)}, u32[]{:S(2)}) collective-permute-start(f32[128,256]{1,0:T(8,128)S(1)} %get-tuple-element.47.refs_1_), channel_id=1, source_target_pairs={{0,64},{32,96},{64,0},{96,32},{128,192},{160,224},{192,128},{224,1... | collective-permute-start | bytes 393224 | tf_op jit(solution)/shard_map/ppermute | solution.py:407
  18.9 8.1 %collective-permute-start.5 = (f32[128,256]{1,0:T(8,128)S(1)}, f32[128,256]{1,0:T(8,128)S(1)}, u32[]{:S(2)}, u32[]{:S(2)}) collective-permute-start(f32[128,256]{1,0:T(8,128)S(1)} %get-tuple-element.48.refs_2_), channel_id=1, source_target_pairs={{0,192},{32,224},{64,128},{96,160},{128,64},{160,96},{192,0},{224,... | collective-permute-start | bytes 393224 | tf_op jit(solution)/shard_map/ppermute | solution.py:407
  21.0 6.1 %collective-permute-start.6 = (f32[128,256]{1,0:T(8,128)S(1)}, f32[128,256]{1,0:T(8,128)S(1)}, u32[]{:S(2)}, u32[]{:S(2)}) collective-permute-start(f32[128,256]{1,0:T(8,128)S(1)} %get-tuple-element.49.refs_3_), channel_id=1, source_target_pairs={{0,96},{32,64},{64,32},{96,0},{128,224},{160,192},{192,160},{224,1... | collective-permute-start | bytes 393224 | tf_op jit(solution)/shard_map/ppermute | solution.py:407
  22.7 11.8 %collective-permute-start.7 = (f32[128,256]{1,0:T(8,128)S(1)}, f32[128,256]{1,0:T(8,128)S(1)}, u32[]{:S(2)}, u32[]{:S(2)}) collective-permute-start(f32[128,256]{1,0:T(8,128)S(1)} %get-tuple-element.50.refs_4_), channel_id=1, source_target_pairs={{0,224},{32,192},{64,160},{96,128},{128,96},{160,64},{192,32},{224... | collective-permute-start | bytes 393224 | tf_op jit(solution)/shard_map/ppermute | solution.py:407
  23.3 11.2 %collective-permute-start.8 = (f32[128,256]{1,0:T(8,128)S(1)}, f32[128,256]{1,0:T(8,128)S(1)}, u32[]{:S(2)}, u32[]{:S(2)}) collective-permute-start(f32[128,256]{1,0:T(8,128)S(1)} %get-tuple-element.51.refs_5_), channel_id=1, source_target_pairs={{0,128},{32,160},{64,192},{96,224},{128,0},{160,32},{192,64},{224,... | collective-permute-start | bytes 393224 | tf_op jit(solution)/shard_map/ppermute | solution.py:407
  24.7 9.9 %collective-permute-start.9 = (f32[128,256]{1,0:T(8,128)S(1)}, f32[128,256]{1,0:T(8,128)S(1)}, u32[]{:S(2)}, u32[]{:S(2)}) collective-permute-start(f32[128,256]{1,0:T(8,128)S(1)} %get-tuple-element.52.refs_6_), channel_id=1, source_target_pairs={{0,160},{32,128},{64,224},{96,192},{128,32},{160,0},{192,96},{224,... | collective-permute-start | bytes 393224 | tf_op jit(solution)/shard_map/ppermute | solution.py:407
  27.0 7.5 %collective-permute-start.10 = (f32[128,256]{1,0:T(8,128)S(1)}, f32[128,256]{1,0:T(8,128)S(1)}, u32[]{:S(2)}, u32[]{:S(2)}) collective-permute-start(f32[128,256]{1,0:T(8,128)S(1)} %get-tuple-element.53.refs_7_), channel_id=1, source_target_pairs={{0,32},{32,0},{64,96},{96,64},{128,160},{160,128},{192,224},{224,1... | collective-permute-start | bytes 393224 | tf_op jit(solution)/shard_map/ppermute | solution.py:407
  36.7 32.0 %copy-start.2 = (f32[2,4,4,32,128]{4,3,2,1,0:T(8,128)S(1)}, f32[2,4,4,32,128]{4,3,2,1,0:T(8,128)}, u32[]{:S(2)}) copy-start(f32[2,4,4,32,128]{4,3,2,1,0:T(8,128)} %constant.10.clone.turn_ref) | copy-start | bytes 1572868
  36.8 32.0 %copy-start.3 = (f32[8,128]{1,0:T(8,128)S(1)}, f32[8,128]{1,0:T(8,128)}, u32[]{:S(2)}) copy-start(f32[8,128]{1,0:T(8,128)} %lift_ref.1) | copy-start | bytes 12292
  36.8 32.0 %copy-start.4 = (f32[128,8]{0,1:T(8,128)S(1)}, f32[128,8]{0,1:T(8,128)}, u32[]{:S(2)}) copy-start(f32[128,8]{0,1:T(8,128)} %param.18) | copy-start | bytes 12292
  70.8 26.4 %all-to-all-start.1 = ((f32[256,1,512]{2,1,0:T(1,128)}), f32[256,1,512]{2,1,0:T(1,128)S(1)}, u32[]{:S(2)}, u32[]{:S(2)}) async-start(f32[256,1,512]{2,1,0:T(1,128)} %shard_map.152), calls=%async_computation.1 | async-start | bytes 1048576 | tf_op jit(solution)/shard_map/all_to_all | solution.py:76
  100.9 6.1 %collective-permute-start.11 = (f32[128,256]{1,0:T(8,128)S(1)}, f32[128,256]{1,0:T(8,128)S(1)}, u32[]{:S(2)}, u32[]{:S(2)}) collective-permute-start(f32[128,256]{1,0:T(8,128)S(1)} %get-tuple-element.69), channel_id=1, source_target_pairs={{0,64},{32,96},{64,0},{96,32},{128,192},{160,224},{192,128},{224,1... | collective-permute-start | bytes 393224 | tf_op jit(solution)/shard_map/ppermute | solution.py:407
  101.9 7.9 %collective-permute-start.12 = (f32[128,256]{1,0:T(8,128)S(1)}, f32[128,256]{1,0:T(8,128)S(1)}, u32[]{:S(2)}, u32[]{:S(2)}) collective-permute-start(f32[128,256]{1,0:T(8,128)S(1)} %get-tuple-element.70), channel_id=1, source_target_pairs={{0,192},{32,224},{64,128},{96,160},{128,64},{160,96},{192,0},{224,... | collective-permute-start | bytes 393224 | tf_op jit(solution)/shard_map/ppermute | solution.py:407
  103.4 8.6 %collective-permute-start.13 = (f32[128,256]{1,0:T(8,128)S(1)}, f32[128,256]{1,0:T(8,128)S(1)}, u32[]{:S(2)}, u32[]{:S(2)}) collective-permute-start(f32[128,256]{1,0:T(8,128)S(1)} %get-tuple-element.71), channel_id=1, source_target_pairs={{0,96},{32,64},{64,32},{96,0},{128,224},{160,192},{192,160},{224,1... | collective-permute-start | bytes 393224 | tf_op jit(solution)/shard_map/ppermute | solution.py:407
  104.2 12.6 %collective-permute-start.14 = (f32[128,256]{1,0:T(8,128)S(1)}, f32[128,256]{1,0:T(8,128)S(1)}, u32[]{:S(2)}, u32[]{:S(2)}) collective-permute-start(f32[128,256]{1,0:T(8,128)S(1)} %get-tuple-element.72), channel_id=1, source_target_pairs={{0,224},{32,192},{64,160},{96,128},{128,96},{160,64},{192,32},{224... | collective-permute-start | bytes 393224 | tf_op jit(solution)/shard_map/ppermute | solution.py:407
  105.4 11.3 %collective-permute-start.15 = (f32[128,256]{1,0:T(8,128)S(1)}, f32[128,256]{1,0:T(8,128)S(1)}, u32[]{:S(2)}, u32[]{:S(2)}) collective-permute-start(f32[128,256]{1,0:T(8,128)S(1)} %get-tuple-element.73), channel_id=1, source_target_pairs={{0,128},{32,160},{64,192},{96,224},{128,0},{160,32},{192,64},{224,... | collective-permute-start | bytes 393224 | tf_op jit(solution)/shard_map/ppermute | solution.py:407
  106.9 9.8 %collective-permute-start.16 = (f32[128,256]{1,0:T(8,128)S(1)}, f32[128,256]{1,0:T(8,128)S(1)}, u32[]{:S(2)}, u32[]{:S(2)}) collective-permute-start(f32[128,256]{1,0:T(8,128)S(1)} %get-tuple-element.74), channel_id=1, source_target_pairs={{0,160},{32,128},{64,224},{96,192},{128,32},{160,0},{192,96},{224,... | collective-permute-start | bytes 393224 | tf_op jit(solution)/shard_map/ppermute | solution.py:407
  109.8 6.9 %collective-permute-start.17 = (f32[128,256]{1,0:T(8,128)S(1)}, f32[128,256]{1,0:T(8,128)S(1)}, u32[]{:S(2)}, u32[]{:S(2)}) collective-permute-start(f32[128,256]{1,0:T(8,128)S(1)} %get-tuple-element.75), channel_id=1, source_target_pairs={{0,32},{32,0},{64,96},{96,64},{128,160},{160,128},{192,224},{224,1... | collective-permute-start | bytes 393224 | tf_op jit(solution)/shard_map/ppermute | solution.py:407
  (9 other events, 76.9 us)

commit v9 on v8

--- a/solution.py
+++ b/solution.py
@@ -209,6 +209,10 @@
         ref[...] = held_ref[lax.bitwise_xor(gx, k)]
 
 
+def fetch_kernel(table_ref, out_ref):
+    out_ref[...] = table_ref[...]
+
+
 def quarter_turn(index, t):
     place = lax.rem(index * t, 4)
     cosine = jnp.where(place == 0, 1.0, jnp.where(place == 2, -1.0, 0.0))
@@ -555,20 +559,24 @@
         flops=6 * 2 * 512 * 128 * 16,
     )[0]
 
+    sent, table = lax.optimization_barrier((sent, jnp.asarray(BACK)))
+    table = local_kernel(
+        fetch_kernel, [jax.ShapeDtypeStruct(BACK.shape, jnp.bfloat16)], (table,)
+    )[0]
     points = (cell_rows[0], cell_cols[0], live)
-    w_0, wh_0 = scatter(*points, got, 0, 224, 56)
+    w_0, wh_0 = scatter(*points, got, 0, 192, 48)
 
     back = all_to_all(sent, ("gx", "gy"))
-    back, w_0, wh_0 = lax.optimization_barrier((back, w_0, wh_0))
+    back, w_0, wh_0, table = lax.optimization_barrier((back, w_0, wh_0, table))
     blocks = local_kernel(
         backward_kernel,
         [shape(CX, CY)] * GX,
-        (back, jnp.asarray(BACK)),
+        (back, table),
         flops=3 * 2 * (512 * NX * CY + 512 * 256 * 512),
         scratch=[pltpu.VMEM((MY, 2 * MX), jnp.float32), pltpu.VMEM((NX, CY), jnp.float32)],
     )
     got, w_0 = lax.optimization_barrier((got, w_0))
-    w_1, wh_1 = scatter(*points, got, 224, 256, 32)
+    w_1, wh_1 = scatter(*points, got, 192, 256, 32)
     return tuple(
         local_kernel(
             finish_kernel,

time: 118 us -> 118 us (level)
  waiting for transfers between devices: 19.4 us -> 16.8 us
    ppermute x14, waiting for transfers between devices: 12.2 us -> 8.87 us  [exchange(): lax.ppermute(block, 'gx', [(i, i ^ k) for i in range(GX)])]
    pallas_call x6 -> x7, Pallas kernels: 11.9 us -> 11.9 us  [local_kernel(): pl.pallas_call(kernel, in_specs=[place] * len(operands), out_specs=[vmem]...]
  transfers between devices with their start and end apart: 19 -> 19, of which waited for: 5 -> 5; matrix products, arithmetic and copies ran while one was open for 0% -> 1% of each run, Pallas kernels for 14% -> 14%
where the time goes in v9:
time: 118 us
  starting transfers between devices  37.2 us (32%)
  blocking collectives  32.3 us (27%)
  Pallas kernels  28.4 us (24%)
  waiting for transfers between devices  16.8 us (14%)
    all_to_all x1, blocking collectives, all_to_all(): return lax.all_to_all(array, axis, split_axis=0, concat_axis=0, tiled=True)  32.3 us
    ppermute x14, starting transfers between devices, exchange(): lax.ppermute(block, 'gx', [(i, i ^ k) for i in range(GX)])  19.1 us
    pallas_call x2, Pallas kernels, scatter(): pl.pallas_call(scatter_kernel, grid=(steps,), in_specs=[block] * 3 + [pl....  16.5 us
    pallas_call x7, Pallas kernels, local_kernel(): pl.pallas_call(kernel, in_specs=[place] * len(operands), out_specs=[vmem]...  11.9 us
    ppermute x1, starting transfers between devices, body(): odd = lax.ppermute(odd, 'gy', odd_pairs)  8.94 us
    ppermute x14, waiting for transfers between devices, exchange(): lax.ppermute(block, 'gx', [(i, i ^ k) for i in range(GX)])  8.87 us
    all_to_all x1, waiting for transfers between devices, all_to_all(): return lax.all_to_all(array, axis, split_axis=0, concat_axis=0, tiled=True)  6.91 us
    all_to_all x1, starting transfers between devices, all_to_all(): return lax.all_to_all(array, axis, split_axis=0, concat_axis=0, tiled=True)  6.35 us
  transfers between devices with their start and end apart: 19, of which 5 were waited for; matrix products, arithmetic and copies ran while one was open for 1% of the time, Pallas kernels for 14%

profile of v9, /device:TPU:1, one launch (start us, length us, event | category | flops | bytes accessed | tf_op | source)
XLA Modules:
  0.0 117.7 jit_solution(7028620130703732270)
XLA Ops:
  0.6 2.7 %shard_map.149 = (f32[16,256]{1,0:T(8,128)}, f32[16,256]{1,0:T(8,128)}, f32[48,128]{1,0:T(8,128)}, f32[48,128]{1,0:T(8,128)}) custom-call(f32[8,128,256]{2,1,0:T(8,128)} %fields_ref.1, f32[2,128,256]{2,1,0:T(8,128)} %velocity_ref.1), custom_call_target="tpu_custom_call" | custom-call | bytes 1392640 | tf_op jit(solution)/shard_map/pallas_call | solution.py:110
  3.3 8.9 %collective-permute-start = (f32[48,128]{1,0:T(8,128)}, f32[48,128]{1,0:T(8,128)S(1)}, u32[]{:S(2)}, u32[]{:S(2)}) collective-permute-start(f32[48,128]{1,0:T(8,128)} %get-tuple-element.45), channel_id=1, source_target_pairs={{0,31},{1,2},{2,1},{3,4},{4,3},{5,6},{6,5},{7,8},{8,7},{9,10},{10,... | collective-permute-start | bytes 73736 | tf_op jit(solution)/shard_map/ppermute | solution.py:516
  12.3 2.1 %collective-permute-start.2 = (f32[16,256]{1,0:T(8,128)}, f32[16,256]{1,0:T(8,128)S(1)}, u32[]{:S(2)}, u32[]{:S(2)}) collective-permute-start(f32[16,256]{1,0:T(8,128)} %get-tuple-element.47), channel_id=1, source_target_pairs={{0,224},{32,64},{64,32},{96,128},{128,96},{160,192},{192,160},{224... | collective-permute-start | bytes 49160 | tf_op jit(solution)/shard_map/ppermute | solution.py:518
  16.2 1.4 %shard_map.150 = (f32[128,256]{1,0:T(8,128)S(1)}, f32[128,256]{1,0:T(8,128)S(1)}, f32[128,256]{1,0:T(8,128)S(1)}, f32[128,256]{1,0:T(8,128)S(1)}, f32[128,256]{1...) custom-call(f32[8,128,256]{2,1,0:T(8,128)S(1)} %copy-done, ...), custom_call_target="tpu_custom_call" | custom-call | bytes 2441216 | tf_op jit(solution)/shard_map/pallas_call | solution.py:110
  17.6 1.7 %collective-permute-start.10 = (f32[128,256]{1,0:T(8,128)S(1)}, f32[128,256]{1,0:T(8,128)S(1)}, u32[]{:S(2)}, u32[]{:S(2)}) collective-permute-start(f32[128,256]{1,0:T(8,128)S(1)} %get-tuple-element.56.refs_7_), channel_id=1, source_target_pairs={{0,32},{32,0},{64,96},{96,64},{128,160},{160,128},{192,224},{224,1... | collective-permute-start | bytes 393224 | tf_op jit(solution)/shard_map/ppermute | solution.py:411
  20.1 1.9 %collective-permute-start.5 = (f32[128,256]{1,0:T(8,128)S(1)}, f32[128,256]{1,0:T(8,128)S(1)}, u32[]{:S(2)}, u32[]{:S(2)}) collective-permute-start(f32[128,256]{1,0:T(8,128)S(1)} %get-tuple-element.51.refs_2_), channel_id=1, source_target_pairs={{0,192},{32,224},{64,128},{96,160},{128,64},{160,96},{192,0},{224,... | collective-permute-start | bytes 393224 | tf_op jit(solution)/shard_map/ppermute | solution.py:411
  23.4 2.1 %collective-permute-start.8 = (f32[128,256]{1,0:T(8,128)S(1)}, f32[128,256]{1,0:T(8,128)S(1)}, u32[]{:S(2)}, u32[]{:S(2)}) collective-permute-start(f32[128,256]{1,0:T(8,128)S(1)} %get-tuple-element.54.refs_5_), channel_id=1, source_target_pairs={{0,128},{32,160},{64,192},{96,224},{128,0},{160,32},{192,64},{224,... | collective-permute-start | bytes 393224 | tf_op jit(solution)/shard_map/ppermute | solution.py:411
  25.6 2.2 %collective-permute-start.9 = (f32[128,256]{1,0:T(8,128)S(1)}, f32[128,256]{1,0:T(8,128)S(1)}, u32[]{:S(2)}, u32[]{:S(2)}) collective-permute-start(f32[128,256]{1,0:T(8,128)S(1)} %get-tuple-element.55.refs_6_), channel_id=1, source_target_pairs={{0,160},{32,128},{64,224},{96,192},{128,32},{160,0},{192,96},{224,... | collective-permute-start | bytes 393224 | tf_op jit(solution)/shard_map/ppermute | solution.py:411
  28.6 6.5 %collective-permute-done.7.refs_4_ = f32[128,256]{1,0:T(8,128)S(1)} collective-permute-done((f32[128,256]{1,0:T(8,128)S(1)}, f32[128,256]{1,0:T(8,128)S(1)}, u32[]{:S(2)}, u32[]{:S(2)}) %collective-permute-start.7) | collective-permute-done | bytes 131104 | tf_op jit(solution)/shard_map/ppermute | solution.py:411
  35.1 2.1 %shard_map.151 = f32[256,1,768]{2,1,0:T(1,128)S(1)} custom-call(f32[128,256]{1,0:T(8,128)S(1)} %get-tuple-element.57.refs_0_, f32[128,256]{1,0:T(8,128)S(1)} %collective-permute-done.4.refs_1_, f32[128,256]{1,0:T(8,128)S(1)} %collective-permute-done.5.refs_2_, f32[128,256]{1,0:T(8,128)S(1)} %collective-permute-done.6.refs_3_, ...), custom_call_target="tpu_custom_call" | custom-call | flops 805306368 | bytes 3686400 | tf_op jit(solution)/shard_map/pallas_call | solution.py:110
  37.3 32.3 %all_to_all.10.got_ref = f32[256,1,768]{2,1,0:T(1,128)S(1)} all-to-all(f32[256,1,768]{2,1,0:T(1,128)S(1)} %shard_map.151), channel_id=1, replica_groups=mesh['gx'=8,'gy'=32] {'gx','gy'}, dimensions={0} | all-to-all | bytes 1572864 | tf_op jit(solution)/shard_map/all_to_all | solution.py:76
  69.6 2.0 %shard_map.152 = f32[256,1,512]{2,1,0:T(1,128)} custom-call(f32[256,1,768]{2,1,0:T(1,128)S(1)} %all_to_all.10.got_ref, f32[2,4,4,32,128]{4,3,2,1,0:T(8,128)S(1)} %copy-done.3, f32[2,8,32,128]{3,2,1,0:T(8,128)S(1)} %bitcast.9, f32[8,128]{1,0:T(8,128)S(1)} %copy-done.12, f32[8,128]{1,0:T(8,128)S(1)} %bitcast.10), custom_call_target="tpu_custom_call" | custom-call | flops 12582912 | bytes 2105344 | tf_op jit(solution)/shard_map/pallas_call | solution.py:110
  71.7 6.4 %all-to-all-start.1 = ((f32[256,1,512]{2,1,0:T(1,128)}), f32[256,1,512]{2,1,0:T(1,128)S(1)}, u32[]{:S(2)}, u32[]{:S(2)}) async-start(f32[256,1,512]{2,1,0:T(1,128)} %shard_map.152), calls=%async_computation.1 | async-start | bytes 1048576 | tf_op jit(solution)/shard_map/all_to_all | solution.py:76
  79.1 12.1 %shard_map.153 = (f32[128,256]{1,0:T(8,128)S(1)}, f32[128,256]{1,0:T(8,128)S(1)}) custom-call(s32[256,128]{1,0:T(8,128)S(1)} %bitcast.13, s32[256,128]{1,0:T(8,128)S(1)} %bitcast.15, f32[256,128]{1,0:T(8,128)S(1)} %copy-done.10, f32[256,1,768]{2,1,0:T(1,128)S(1)} %all_to_all.10.got_ref), custom_call_target="tpu_custom_call" | custom-call | flops 9663676416 | bytes 393216 | tf_op jit(solution)/shard_map/pallas_call | solution.py:468
  91.2 6.9 %all-to-all-done.1.got_ref = f32[256,1,512]{2,1,0:T(1,128)S(1)} async-done(((f32[256,1,512]{2,1,0:T(1,128)}), f32[256,1,512]{2,1,0:T(1,128)S(1)}, u32[]{:S(2)}, u32[]{:S(2)}) %all-to-all-start.1) | async-done | bytes 524320 | tf_op jit(solution)/shard_map/all_to_all | solution.py:76
  98.1 2.5 %shard_map.155 = (f32[128,256]{1,0:T(8,128)S(1)}, f32[128,256]{1,0:T(8,128)S(1)}, f32[128,256]{1,0:T(8,128)S(1)}, f32[128,256]{1,0:T(8,128)S(1)}, f32[128,256]{1...) custom-call(f32[256,1,512]{2,1,0:T(1,128)S(1)} %all-to-all-done.1.got_ref, ...), custom_call_target="tpu_custom_call" | custom-call | flops 1207959552 | bytes 3145728 | tf_op jit(solution)/shard_map/pallas_call | solution.py:110
  100.6 1.0 collective-permute-start.11
  101.6 1.5 %collective-permute-start.12 = (f32[128,256]{1,0:T(8,128)S(1)}, f32[128,256]{1,0:T(8,128)S(1)}, u32[]{:S(2)}, u32[]{:S(2)}) collective-permute-start(f32[128,256]{1,0:T(8,128)S(1)} %get-tuple-element.76), channel_id=1, source_target_pairs={{0,192},{32,224},{64,128},{96,160},{128,64},{160,96},{192,0},{224,... | collective-permute-start | bytes 393224 | tf_op jit(solution)/shard_map/ppermute | solution.py:411
  103.9 1.2 %collective-permute-start.14 = (f32[128,256]{1,0:T(8,128)S(1)}, f32[128,256]{1,0:T(8,128)S(1)}, u32[]{:S(2)}, u32[]{:S(2)}) collective-permute-start(f32[128,256]{1,0:T(8,128)S(1)} %get-tuple-element.78), channel_id=1, source_target_pairs={{0,224},{32,192},{64,160},{96,128},{128,96},{160,64},{192,32},{224... | collective-permute-start | bytes 393224 | tf_op jit(solution)/shard_map/ppermute | solution.py:411
  105.2 1.5 %collective-permute-start.15 = (f32[128,256]{1,0:T(8,128)S(1)}, f32[128,256]{1,0:T(8,128)S(1)}, u32[]{:S(2)}, u32[]{:S(2)}) collective-permute-start(f32[128,256]{1,0:T(8,128)S(1)} %get-tuple-element.79), channel_id=1, source_target_pairs={{0,128},{32,160},{64,192},{96,224},{128,0},{160,32},{192,64},{224,... | collective-permute-start | bytes 393224 | tf_op jit(solution)/shard_map/ppermute | solution.py:411
  106.7 2.9 %collective-permute-start.16 = (f32[128,256]{1,0:T(8,128)S(1)}, f32[128,256]{1,0:T(8,128)S(1)}, u32[]{:S(2)}, u32[]{:S(2)}) collective-permute-start(f32[128,256]{1,0:T(8,128)S(1)} %get-tuple-element.80), channel_id=1, source_target_pairs={{0,160},{32,128},{64,224},{96,192},{128,32},{160,0},{192,96},{224,... | collective-permute-start | bytes 393224 | tf_op jit(solution)/shard_map/ppermute | solution.py:411
  109.7 4.4 %shard_map.156 = (f32[128,256]{1,0:T(8,128)S(1)}, f32[128,256]{1,0:T(8,128)S(1)}) custom-call(s32[256,128]{1,0:T(8,128)S(1)} %bitcast.14, s32[256,128]{1,0:T(8,128)S(1)} %bitcast.16, f32[256,128]{1,0:T(8,128)S(1)} %copy-done.11, f32[256,1,768]{2,1,0:T(1,128)S(1)} %all_to_all.10.got_ref), custom_call_target="tpu_custom_call" | custom-call | flops 3221225472 | bytes 131072 | tf_op jit(solution)/shard_map/pallas_call | solution.py:468
  114.2 2.3 %collective-permute-done.14.refs_12_ = f32[128,256]{1,0:T(8,128)S(1)} collective-permute-done((f32[128,256]{1,0:T(8,128)S(1)}, f32[128,256]{1,0:T(8,128)S(1)}, u32[]{:S(2)}, u32[]{:S(2)}) %collective-permute-start.14) | collective-permute-done | bytes 131104 | tf_op jit(solution)/shard_map/ppermute | solution.py:411
  116.5 1.1 shard_map.157
  (74 shorter events, 6.7 us)
Async XLA Ops:
  0.6 15.6 %copy-start = (f32[8,128,256]{2,1,0:T(8,128)S(1)}, f32[8,128,256]{2,1,0:T(8,128)}, u32[]{:S(2)}) copy-start(f32[8,128,256]{2,1,0:T(8,128)} %fields_ref.1) | copy-start | bytes 3145732
  3.3 12.9 %collective-permute-start = (f32[48,128]{1,0:T(8,128)}, f32[48,128]{1,0:T(8,128)S(1)}, u32[]{:S(2)}, u32[]{:S(2)}) collective-permute-start(f32[48,128]{1,0:T(8,128)} %get-tuple-element.45), channel_id=1, source_target_pairs={{0,31},{1,2},{2,1},{3,4},{4,3},{5,6},{6,5},{7,8},{8,7},{9,10},{10,... | collective-permute-start | bytes 73736 | tf_op jit(solution)/shard_map/ppermute | solution.py:516
  12.3 3.9 %collective-permute-start.1 = (f32[48,128]{1,0:T(8,128)}, f32[48,128]{1,0:T(8,128)S(1)}, u32[]{:S(2)}, u32[]{:S(2)}) collective-permute-start(f32[48,128]{1,0:T(8,128)} %get-tuple-element.46), channel_id=1, source_target_pairs={{0,1},{1,0},{2,3},{3,2},{4,5},{5,4},{6,7},{7,6},{8,9},{9,8},{10,11... | collective-permute-start | bytes 73736 | tf_op jit(solution)/shard_map/ppermute | solution.py:517
  12.3 3.7 %collective-permute-start.2 = (f32[16,256]{1,0:T(8,128)}, f32[16,256]{1,0:T(8,128)S(1)}, u32[]{:S(2)}, u32[]{:S(2)}) collective-permute-start(f32[16,256]{1,0:T(8,128)} %get-tuple-element.47), channel_id=1, source_target_pairs={{0,224},{32,64},{64,32},{96,128},{128,96},{160,192},{192,160},{224... | collective-permute-start | bytes 49160 | tf_op jit(solution)/shard_map/ppermute | solution.py:518
  14.3 20.7 %copy-start.20 = (bf16[1536,256]{1,0:T(8,128)(2,1)S(1)}, bf16[1536,256]{1,0:T(8,128)(2,1)}, u32[]{:S(2)}) copy-start(bf16[1536,256]{1,0:T(8,128)(2,1)} %constant.8.clone.refs_8_) | copy-start | bytes 2359300
  14.3 1.9 %collective-permute-start.3 = (f32[16,256]{1,0:T(8,128)}, f32[16,256]{1,0:T(8,128)S(1)}, u32[]{:S(2)}, u32[]{:S(2)}) collective-permute-start(f32[16,256]{1,0:T(8,128)} %get-tuple-element.48), channel_id=1, source_target_pairs={{0,32},{32,0},{64,96},{96,64},{128,160},{160,128},{192,224},{224,1... | collective-permute-start | bytes 49160 | tf_op jit(solution)/shard_map/ppermute | solution.py:519
  17.6 5.8 %collective-permute-start.10 = (f32[128,256]{1,0:T(8,128)S(1)}, f32[128,256]{1,0:T(8,128)S(1)}, u32[]{:S(2)}, u32[]{:S(2)}) collective-permute-start(f32[128,256]{1,0:T(8,128)S(1)} %get-tuple-element.56.refs_7_), channel_id=1, source_target_pairs={{0,32},{32,0},{64,96},{96,64},{128,160},{160,128},{192,224},{224,1... | collective-permute-start | bytes 393224 | tf_op jit(solution)/shard_map/ppermute | solution.py:411
  19.3 6.2 %collective-permute-start.4 = (f32[128,256]{1,0:T(8,128)S(1)}, f32[128,256]{1,0:T(8,128)S(1)}, u32[]{:S(2)}, u32[]{:S(2)}) collective-permute-start(f32[128,256]{1,0:T(8,128)S(1)} %get-tuple-element.50.refs_1_), channel_id=1, source_target_pairs={{0,64},{32,96},{64,0},{96,32},{128,192},{160,224},{192,128},{224,1... | collective-permute-start | bytes 393224 | tf_op jit(solution)/shard_map/ppermute | solution.py:411
  20.1 8.4 %collective-permute-start.5 = (f32[128,256]{1,0:T(8,128)S(1)}, f32[128,256]{1,0:T(8,128)S(1)}, u32[]{:S(2)}, u32[]{:S(2)}) collective-permute-start(f32[128,256]{1,0:T(8,128)S(1)} %get-tuple-element.51.refs_2_), channel_id=1, source_target_pairs={{0,192},{32,224},{64,128},{96,160},{128,64},{160,96},{192,0},{224,... | collective-permute-start | bytes 393224 | tf_op jit(solution)/shard_map/ppermute | solution.py:411
  22.0 6.5 %collective-permute-start.6 = (f32[128,256]{1,0:T(8,128)S(1)}, f32[128,256]{1,0:T(8,128)S(1)}, u32[]{:S(2)}, u32[]{:S(2)}) collective-permute-start(f32[128,256]{1,0:T(8,128)S(1)} %get-tuple-element.52.refs_3_), channel_id=1, source_target_pairs={{0,96},{32,64},{64,32},{96,0},{128,224},{160,192},{192,160},{224,1... | collective-permute-start | bytes 393224 | tf_op jit(solution)/shard_map/ppermute | solution.py:411
  22.9 12.2 %collective-permute-start.7 = (f32[128,256]{1,0:T(8,128)S(1)}, f32[128,256]{1,0:T(8,128)S(1)}, u32[]{:S(2)}, u32[]{:S(2)}) collective-permute-start(f32[128,256]{1,0:T(8,128)S(1)} %get-tuple-element.53.refs_4_), channel_id=1, source_target_pairs={{0,224},{32,192},{64,160},{96,128},{128,96},{160,64},{192,32},{224... | collective-permute-start | bytes 393224 | tf_op jit(solution)/shard_map/ppermute | solution.py:411
  23.4 11.7 %collective-permute-start.8 = (f32[128,256]{1,0:T(8,128)S(1)}, f32[128,256]{1,0:T(8,128)S(1)}, u32[]{:S(2)}, u32[]{:S(2)}) collective-permute-start(f32[128,256]{1,0:T(8,128)S(1)} %get-tuple-element.54.refs_5_), channel_id=1, source_target_pairs={{0,128},{32,160},{64,192},{96,224},{128,0},{160,32},{192,64},{224,... | collective-permute-start | bytes 393224 | tf_op jit(solution)/shard_map/ppermute | solution.py:411
  25.6 9.5 %collective-permute-start.9 = (f32[128,256]{1,0:T(8,128)S(1)}, f32[128,256]{1,0:T(8,128)S(1)}, u32[]{:S(2)}, u32[]{:S(2)}) collective-permute-start(f32[128,256]{1,0:T(8,128)S(1)} %get-tuple-element.55.refs_6_), channel_id=1, source_target_pairs={{0,160},{32,128},{64,224},{96,192},{128,32},{160,0},{192,96},{224,... | collective-permute-start | bytes 393224 | tf_op jit(solution)/shard_map/ppermute | solution.py:411
  37.2 32.4 %copy-start.3 = (f32[2,4,4,32,128]{4,3,2,1,0:T(8,128)S(1)}, f32[2,4,4,32,128]{4,3,2,1,0:T(8,128)}, u32[]{:S(2)}) copy-start(f32[2,4,4,32,128]{4,3,2,1,0:T(8,128)} %constant.10.clone.turn_ref) | copy-start | bytes 1572868
  37.3 32.4 %copy-start.12 = (f32[8,128]{1,0:T(8,128)S(1)}, f32[8,128]{1,0:T(8,128)}, u32[]{:S(2)}) copy-start(f32[8,128]{1,0:T(8,128)} %lift_ref.1) | copy-start | bytes 12292
  37.3 32.3 %copy-start.13 = (f32[128,8]{0,1:T(8,128)S(1)}, f32[128,8]{0,1:T(8,128)}, u32[]{:S(2)}) copy-start(f32[128,8]{0,1:T(8,128)} %param.18) | copy-start | bytes 12292
  71.7 26.4 %all-to-all-start.1 = ((f32[256,1,512]{2,1,0:T(1,128)}), f32[256,1,512]{2,1,0:T(1,128)S(1)}, u32[]{:S(2)}, u32[]{:S(2)}) async-start(f32[256,1,512]{2,1,0:T(1,128)} %shard_map.152), calls=%async_computation.1 | async-start | bytes 1048576 | tf_op jit(solution)/shard_map/all_to_all | solution.py:76
  100.6 6.1 %collective-permute-start.11 = (f32[128,256]{1,0:T(8,128)S(1)}, f32[128,256]{1,0:T(8,128)S(1)}, u32[]{:S(2)}, u32[]{:S(2)}) collective-permute-start(f32[128,256]{1,0:T(8,128)S(1)} %get-tuple-element.75), channel_id=1, source_target_pairs={{0,64},{32,96},{64,0},{96,32},{128,192},{160,224},{192,128},{224,1... | collective-permute-start | bytes 393224 | tf_op jit(solution)/shard_map/ppermute | solution.py:411
  101.6 7.9 %collective-permute-start.12 = (f32[128,256]{1,0:T(8,128)S(1)}, f32[128,256]{1,0:T(8,128)S(1)}, u32[]{:S(2)}, u32[]{:S(2)}) collective-permute-start(f32[128,256]{1,0:T(8,128)S(1)} %get-tuple-element.76), channel_id=1, source_target_pairs={{0,192},{32,224},{64,128},{96,160},{128,64},{160,96},{192,0},{224,... | collective-permute-start | bytes 393224 | tf_op jit(solution)/shard_map/ppermute | solution.py:411
  103.2 11.0 %collective-permute-start.13 = (f32[128,256]{1,0:T(8,128)S(1)}, f32[128,256]{1,0:T(8,128)S(1)}, u32[]{:S(2)}, u32[]{:S(2)}) collective-permute-start(f32[128,256]{1,0:T(8,128)S(1)} %get-tuple-element.77), channel_id=1, source_target_pairs={{0,96},{32,64},{64,32},{96,0},{128,224},{160,192},{192,160},{224,1... | collective-permute-start | bytes 393224 | tf_op jit(solution)/shard_map/ppermute | solution.py:411
  103.9 12.6 %collective-permute-start.14 = (f32[128,256]{1,0:T(8,128)S(1)}, f32[128,256]{1,0:T(8,128)S(1)}, u32[]{:S(2)}, u32[]{:S(2)}) collective-permute-start(f32[128,256]{1,0:T(8,128)S(1)} %get-tuple-element.78), channel_id=1, source_target_pairs={{0,224},{32,192},{64,160},{96,128},{128,96},{160,64},{192,32},{224... | collective-permute-start | bytes 393224 | tf_op jit(solution)/shard_map/ppermute | solution.py:411
  105.2 11.3 %collective-permute-start.15 = (f32[128,256]{1,0:T(8,128)S(1)}, f32[128,256]{1,0:T(8,128)S(1)}, u32[]{:S(2)}, u32[]{:S(2)}) collective-permute-start(f32[128,256]{1,0:T(8,128)S(1)} %get-tuple-element.79), channel_id=1, source_target_pairs={{0,128},{32,160},{64,192},{96,224},{128,0},{160,32},{192,64},{224,... | collective-permute-start | bytes 393224 | tf_op jit(solution)/shard_map/ppermute | solution.py:411
  106.7 9.8 %collective-permute-start.16 = (f32[128,256]{1,0:T(8,128)S(1)}, f32[128,256]{1,0:T(8,128)S(1)}, u32[]{:S(2)}, u32[]{:S(2)}) collective-permute-start(f32[128,256]{1,0:T(8,128)S(1)} %get-tuple-element.80), channel_id=1, source_target_pairs={{0,160},{32,128},{64,224},{96,192},{128,32},{160,0},{192,96},{224,... | collective-permute-start | bytes 393224 | tf_op jit(solution)/shard_map/ppermute | solution.py:411
  109.6 6.9 %collective-permute-start.17 = (f32[128,256]{1,0:T(8,128)S(1)}, f32[128,256]{1,0:T(8,128)S(1)}, u32[]{:S(2)}, u32[]{:S(2)}) collective-permute-start(f32[128,256]{1,0:T(8,128)S(1)} %get-tuple-element.81), channel_id=1, source_target_pairs={{0,32},{32,0},{64,96},{96,64},{128,160},{160,128},{192,224},{224,1... | collective-permute-start | bytes 393224 | tf_op jit(solution)/shard_map/ppermute | solution.py:411
  (19 other events, 147.6 us)
